TPU v7x, 32 devices: a whole 2x2x4 slice. The times are simulated.
32 devices in a mesh: slab: 16 (over z, y, x), blk: 2 (over core).
Axes of the slice: x: 2, y: 2, z: 4, core: 2. Of those that a mesh axis runs over, the one named last changes fastest.
Arguments:
- interior: float32 [32, 128, 512], P('slab', 'blk'), may hold values from -6 to 6
- sources: float32 [32, 128, 512], P('slab', 'blk'), may hold values from -12 to 12
- absorption: float32 [32, 128, 512], P('slab', 'blk'), may hold values from 0.1 to 4
- bem_panel: bfloat16 [8192, 16384], P('blk', 'slab'), may hold values from -0.0625 to 0.0625
- incident: bfloat16 [16384, 512], P('slab'), may hold values from -160 to 160
- node_cell: int32 [16384], P('slab'), may hold values from 0 to 255
- offset: int32 [1], replicated, may hold values from 0 to 8192, as said below
Outputs:
- relaxed: float32 [32, 128, 512], P('slab', 'blk')
- boundary_flux: float32 [8192, 512], P(('blk', 'slab'))
Inputs may be any that keep to these rules, and one draw needn't show every extreme that they name: offset is a multiple of 8192; rows offset to offset + 8191 lie among the 16384 boundary nodes.
All inputs are finite; a program needn't handle non-finite values.
Results may differ from a plain program's by a relative error of at most 0.0034.
Values sent between devices are 32-bit elements; how exact they have to be, the bound alone decides.
No kernel may reach another device: no remote copies, remote signals or barrier semaphores. Data moves between devices by JAX's collectives and lax.ppermute only.
A program may use at most 64 MiB of HBM per device.

v0:
```python
import jax
import jax.numpy as jnp
from jax import lax
from jax.sharding import PartitionSpec as P

SWEEPS = 2


omega = 0.6
center_weight = 8.0 / 3.0


def padded_2(cells, sides, width):
    for axis, dim in sides:
        count = lax.axis_size(axis)
        ends = count - 1
        head = lax.slice_in_dim(cells, 0, width, axis=dim)
        tail = lax.slice_in_dim(cells, cells.shape[dim] - width, cells.shape[dim], axis=dim)
        cells = jnp.concatenate(
            [
                lax.ppermute(tail, axis, [(i, (i + 1) % count) for i in range(ends)]),
                cells,
                lax.ppermute(head, axis, [((i + 1) % count, i) for i in range(ends)]),
            ],
            axis=dim,
        )
    return cells


def stiffness(padded):
    along_x = padded[:, :, :-2] + padded[:, :, 2:]
    middle = padded[:, :, 1:-1]
    plus_mid = along_x + middle
    plane_sum = plus_mid[:, :-2] + plus_mid[:, 1:-1] + plus_mid[:, 2:]
    total_sum = plane_sum[:-2] + plane_sum[1:-1] + plane_sum[2:]
    cross_xy = along_x[:, :-2] + along_x[:, 2:]
    corner_sum = cross_xy[:-2] + cross_xy[2:]
    face_sum = (
        along_x[1:-1, 1:-1]
        + middle[1:-1, :-2]
        + middle[1:-1, 2:]
        + middle[:-2, 1:-1]
        + middle[2:, 1:-1]
    )
    center = middle[1:-1, 1:-1]
    edge_sum = total_sum - center - face_sum - corner_sum
    return center_weight * center - edge_sum / 6.0 - corner_sum / 12.0


def sweep_once(padded, sources, absorption):
    center = padded[1:-1, 1:-1, 1:-1]
    applied = stiffness(padded) + absorption * center
    return center + omega * (sources - applied) / (center_weight + absorption)


def pad_x(values):
    return jnp.pad(values, ((0, 0), (0, 0), (1, 1)))


def per_device(interior, sources, absorption, bem_panel, incident, node_cell, offset):
    depth_z, depth_y, width_x = interior.shape
    current = interior
    for sweep_idx in range(SWEEPS):
        padded = padded_2(current, (("slab", 0), ("blk", 1)), 1)
        current = sweep_once(pad_x(padded), sources, absorption)
    slab_cols = incident.shape[0]
    own_count = slab_cols // lax.axis_size("blk")
    x_faces = jnp.stack([interior[:, :, 0], interior[:, :, width_x - 1]], axis=-1).reshape(-1)
    own_cells = lax.dynamic_slice_in_dim(node_cell, lax.axis_index("blk") * own_count, own_count, 0)
    own_trace = jnp.take(x_faces, own_cells, axis=0)
    trace = lax.all_gather(own_trace, "blk", axis=0, tiled=True)
    fields = (incident.astype(jnp.float32) + trace[:, None]).astype(jnp.bfloat16)
    wide = fields.astype(jnp.float32)
    node_total = slab_cols * lax.axis_size("slab")
    squares = lax.psum(jnp.sum(wide * wide, axis=0), "slab")
    norms = jnp.sqrt(squares / node_total + 1e-06)
    panel_rows = bem_panel.shape[0]
    first_col = lax.axis_index("slab") * slab_cols
    shift_rows = offset[0] + lax.axis_index("blk") * panel_rows - first_col
    share = panel_rows // lax.axis_size("slab")
    product = jnp.dot(bem_panel, fields, preferred_element_type=jnp.float32)
    node_pos = shift_rows + jnp.arange(share * lax.axis_size("slab"), dtype=jnp.int32)
    valid = (node_pos >= 0) & (node_pos < slab_cols)
    picked = jnp.take(wide, jnp.clip(node_pos, 0, slab_cols - 1), axis=0)
    summed = product + 0.5 * jnp.where(valid[:, None], picked, 0.0)
    summed = summed / norms[None, :]
    owned = lax.psum_scatter(summed, "slab", scatter_dimension=0, tiled=True)
    return (current, owned)


def solution(mesh):
    in_specs = (
        P("slab", "blk", None),
        P("slab", "blk", None),
        P("slab", "blk", None),
        P("blk", "slab"),
        P("slab", None),
        P("slab"),
        P(),
    )
    out_specs = (P("slab", "blk", None), P(("blk", "slab"), None))
    return jax.shard_map(
        per_device, mesh=mesh, in_specs=in_specs, out_specs=out_specs, check_vma=False
    )
```

profile of v0, /device:TPU:0, one launch (start us, length us, event | category | flops | bytes accessed | tf_op | source)
XLA Modules:
  0.0 292.9 jit_solution(4510916669527935515)
XLA Ops:
  7.9 0.8 compare_select_fusion.2
  8.7 1.0 fusion.45
  9.9 0.1 copy.15
  10.0 0.1 reshape.43
  10.1 3.5 %gather_fusion = f32[512]{0:T(512)S(1)} fusion(f32[256]{0:T(256)S(1)} %reshape.43, s32[1024]{0:T(1024)S(1)} %pad_clamp_fusion), kind=kCustom, calls=%fused_computation | custom fusion | bytes 6144 | tf_op jit(solution)/shard_map/jit(_take)/gather | solution.py:70
  13.6 0.8 and_select_fusion
  14.4 1.9 all-gather
  16.3 1.6 multiply_reduce_fusion
  17.9 16.9 %gather_fusion.1 = f32[4096,512]{1,0:T(8,128)} fusion(f32[1024,512]{1,0:T(8,128)S(1)} %get-tuple-element.13, s32[4096]{0:T(1024)S(1)} %broadcast_clamp_fusion), kind=kCustom, calls=%fused_computation.1 | custom fusion | bytes 16793600 | tf_op jit(solution)/shard_map/jit(_take)/gather | solution.py:84
  34.8 9.1 %copy.16 = f32[4096,512]{0,1:T(8,128)} copy(f32[4096,512]{1,0:T(8,128)} %gather_fusion.1) | data formatting | bytes 16777216 | tf_op jit(solution)/shard_map/jit(_take)/gather | solution.py:84
  43.8 43.3 %psum.7 = f32[512]{0:T(512)S(1)} all-reduce(f32[512]{0:T(512)S(1)} %get-tuple-element.12), channel_id=1, replica_groups=mesh['slab'=16,'blk'=2] {'slab'}, use_global_device_ids=true, to_apply=%region_1.2 | all-reduce | flops 512 | bytes 4096 | tf_op jit(solution)/shard_map/psum | solution.py:75
  87.2 13.4 %fusion = f32[4096,512]{0,1:T(8,128)} fusion(f32[4096,512]{0,1:T(8,128)} %copy.16, bf16[4096,1024]{1,0:T(8,128)(2,1)} %param.10, f32[512]{0:T(512)S(1)} %add_sqrt_fusion, pred[4096]{0:T(1024)(128)(4,1)S(1)} %get-tuple-element.26, pred[4096]{0:T(1024)(128)(4,1)S(1)} %get-tuple-element.27, bf16[1024,512]{1,0:T(8,128)(2,1)S(1)} %copy-done.1, f32[1024]{0:T(1024)S(1)} %bitcast.12), kind=kOutput, calls=%fused_computation.3 | convolution fusion | flops 4307025920 | bytes 26228736 | tf_op jit(solution)/shard_map/dot_general | solution.py:81
  100.5 0.9 copy-done
  101.5 1.3 collective-permute-start
  102.8 1.3 collective-permute-start.1
  104.1 14.8 %collective-permute-done = f32[1,64,512]{2,1,0:T(8,128)S(1)} collective-permute-done((f32[1,64,512]{2,1,0:T(8,128)S(1)}, f32[1,64,512]{2,1,0:T(8,128)S(1)}, u32[]{:S(2)}, u32[]{:S(2)}) %collective-permute-start) | collective-permute-done | bytes 131104 | tf_op jit(solution)/shard_map/ppermute | solution.py:21
  119.0 1.3 collective-permute-start.2
  120.3 1.3 collective-permute-start.3
  121.6 1.8 collective-permute-done.3
  123.5 0.4 fusion.39
  123.9 0.2 slice_add_fusion.3
  124.1 0.3 fusion.28
  124.4 4.4 %collective-permute-start.4 = (f32[1,64,512]{2,1,0:T(8,128)S(1)}, f32[1,64,512]{2,1,0:T(8,128)S(1)}, u32[]{:S(2)}, u32[]{:S(2)}) collective-permute-start(f32[1,64,512]{2,1,0:T(8,128)S(1)} %get-tuple-element.20), channel_id=1, source_target_pairs={{0,2},{2,4},{4,6},{6,8},{8,10},{10,12},{12,14},{14,16},{16,18},{18... | collective-permute-start | bytes 393224 | tf_op jit(solution)/shard_map/ppermute | solution.py:21
  128.8 1.3 collective-permute-start.5
  130.2 17.8 %collective-permute-done.4 = f32[1,64,512]{2,1,0:T(8,128)S(1)} collective-permute-done((f32[1,64,512]{2,1,0:T(8,128)S(1)}, f32[1,64,512]{2,1,0:T(8,128)S(1)}, u32[]{:S(2)}, u32[]{:S(2)}) %collective-permute-start.4) | collective-permute-done | bytes 131104 | tf_op jit(solution)/shard_map/ppermute | solution.py:21
  148.0 1.5 collective-permute-start.6
  149.5 1.3 collective-permute-start.7
  150.8 1.8 collective-permute-done.7
  152.7 0.4 fusion.41
  153.2 1.0 fusion.13
  154.2 129.8 %reduce-scatter.2.cloned.1.call-done = f32[256,512]{0,1:T(8,128)} async-done(((f32[4096,512]{0,1:T(8,128)}), f32[256,512]{0,1:T(8,128)}) %reduce-scatter.2.cloned.1.call-update) | async-done | bytes 524304 | tf_op jit(solution)/shard_map/reduce_scatter | solution.py:87
  284.0 2.0 copy.17
  (32 shorter events, 0.8 us)
Async XLA Ops:
  7.2 276.9 %reduce-scatter.2.cloned.1.call-start = ((), (), s32[]{:S(2)}) async-start(), calls=%async_computation.1 | async-start | bytes 8912896 | tf_op jit(solution)/shard_map/reduce_scatter | solution.py:87
  34.8 52.4 %copy-start.1 = (bf16[1024,512]{1,0:T(8,128)(2,1)S(1)}, bf16[1024,512]{1,0:T(8,128)(2,1)}, u32[]{:S(2)}) copy-start(bf16[1024,512]{1,0:T(8,128)(2,1)} %param.11) | copy-start | bytes 3145732
  100.5 0.9 copy-start
  100.5 23.5 %copy-start.2 = (f32[2,64,512]{2,1,0:T(8,128)S(1)}, f32[2,64,512]{2,1,0:T(8,128)}, u32[]{:S(2)}) copy-start(f32[2,64,512]{2,1,0:T(8,128)} %param.8) | copy-start | bytes 786436
  100.5 23.6 %copy-start.3 = (f32[2,64,512]{2,1,0:T(8,128)S(1)}, f32[2,64,512]{2,1,0:T(8,128)}, u32[]{:S(2)}) copy-start(f32[2,64,512]{2,1,0:T(8,128)} %param.9) | copy-start | bytes 786436
  101.5 17.5 %collective-permute-start = (f32[1,64,512]{2,1,0:T(8,128)S(1)}, f32[1,64,512]{2,1,0:T(8,128)S(1)}, u32[]{:S(2)}, u32[]{:S(2)}) collective-permute-start(f32[1,64,512]{2,1,0:T(8,128)S(1)} %get-tuple-element.22), channel_id=1, source_target_pairs={{0,2},{2,4},{4,6},{6,8},{8,10},{10,12},{12,14},{14,16},{16,18},{18... | collective-permute-start | bytes 393224 | tf_op jit(solution)/shard_map/ppermute | solution.py:21
  102.8 16.2 %collective-permute-start.1 = (f32[1,64,512]{2,1,0:T(8,128)S(1)}, f32[1,64,512]{2,1,0:T(8,128)S(1)}, u32[]{:S(2)}, u32[]{:S(2)}) collective-permute-start(f32[1,64,512]{2,1,0:T(8,128)S(1)} %get-tuple-element.23), channel_id=1, source_target_pairs={{2,0},{4,2},{6,4},{8,6},{10,8},{12,10},{14,12},{16,14},{18,16},{20... | collective-permute-start | bytes 393224 | tf_op jit(solution)/shard_map/ppermute | solution.py:23
  119.0 2.6 collective-permute-start.2
  120.3 3.1 %collective-permute-start.3 = (f32[4,1,512]{2,1,0:T(1,128)S(1)}, f32[4,1,512]{2,1,0:T(1,128)S(1)}, u32[]{:S(2)}, u32[]{:S(2)}) collective-permute-start(f32[4,1,512]{2,1,0:T(1,128)S(1)} %get-tuple-element.17), channel_id=1, source_target_pairs={{1,0},{3,2},{5,4},{7,6},{9,8},{11,10},{13,12},{15,14},{17,16},{19,... | collective-permute-start | bytes 24584 | tf_op jit(solution)/shard_map/ppermute | solution.py:23
  124.4 23.5 %collective-permute-start.4 = (f32[1,64,512]{2,1,0:T(8,128)S(1)}, f32[1,64,512]{2,1,0:T(8,128)S(1)}, u32[]{:S(2)}, u32[]{:S(2)}) collective-permute-start(f32[1,64,512]{2,1,0:T(8,128)S(1)} %get-tuple-element.20), channel_id=1, source_target_pairs={{0,2},{2,4},{4,6},{6,8},{8,10},{10,12},{12,14},{14,16},{16,18},{18... | collective-permute-start | bytes 393224 | tf_op jit(solution)/shard_map/ppermute | solution.py:21
  128.8 19.1 %collective-permute-start.5 = (f32[1,64,512]{2,1,0:T(8,128)S(1)}, f32[1,64,512]{2,1,0:T(8,128)S(1)}, u32[]{:S(2)}, u32[]{:S(2)}) collective-permute-start(f32[1,64,512]{2,1,0:T(8,128)S(1)} %get-tuple-element.21), channel_id=1, source_target_pairs={{2,0},{4,2},{6,4},{8,6},{10,8},{12,10},{14,12},{16,14},{18,16},{20... | collective-permute-start | bytes 393224 | tf_op jit(solution)/shard_map/ppermute | solution.py:23
  148.0 2.8 collective-permute-start.6
  149.5 3.1 %collective-permute-start.7 = (f32[4,1,512]{2,1,0:T(1,128)S(1)}, f32[4,1,512]{2,1,0:T(1,128)S(1)}, u32[]{:S(2)}, u32[]{:S(2)}) collective-permute-start(f32[4,1,512]{2,1,0:T(1,128)S(1)} %get-tuple-element.15), channel_id=1, source_target_pairs={{1,0},{3,2},{5,4},{7,6},{9,8},{11,10},{13,12},{15,14},{17,16},{19,... | collective-permute-start | bytes 24584 | tf_op jit(solution)/shard_map/ppermute | solution.py:23
Sparse Core Ops, SparseCore 0:
  100.7 183.3 reduce-scatter.1
where the time goes:
time: 295 us; the launch traced here: 293 us
  waiting for transfers between devices  166 us (56%)
  blocking collectives  45.2 us (15%)
  local copies, waits for them, and re-layouts  33.9 us (11%)
  between operations  14.9 us (5%)
  starting transfers between devices  13.7 us (5%)
  matrix products  13.4 us (5%)
  other arithmetic  5.85 us (2%)
    reduce_scatter x1, waiting for transfers between devices, per_device(): owned = lax.psum_scatter(summed, 'slab', scatter_dimension=0, tiled=True)  130 us
    psum x1, blocking collectives, per_device(): squares = lax.psum(jnp.sum(wide * wide, axis=0), 'slab')  43.3 us
    ppermute x4, waiting for transfers between devices, padded_2(): lax.ppermute(tail, axis, [(i, (i + 1) % count) for i in range(ends)])  32.6 us
    gather x2, local copies, waits for them, and re-layouts, per_device(): picked = jnp.take(wide, jnp.clip(node_pos, 0, slab_cols - 1), axis=0)  25.9 us
    dot_general x1, matrix products, per_device(): product = jnp.dot(bem_panel, fields, preferred_element_type=jnp.float32)  13.4 us
    ppermute x4, starting transfers between devices, padded_2(): lax.ppermute(tail, axis, [(i, (i + 1) % count) for i in range(ends)])  8.5 us
  transfers between devices with their start and end apart: 9, of which 5 were waited for; matrix products, arithmetic and copies ran while one was open for 1% of the time, Pallas kernels for 0%

commit v1 on v0

v1 whole, which is shorter than its diff:
```python
import jax
import jax.numpy as jnp
from jax import lax
from jax.sharding import PartitionSpec as P

SWEEPS = 2

omega = 0.6
center_weight = 8.0 / 3.0

PIECES = ((8, (0, 2, 1)), (10, (2, 1, 0)), (10, (1, 2, 0)), (4, (0, 1, 2)))


def slab_dims(count):
    bits = count.bit_length() - 1
    if count != 1 << bits or bits > 6:
        return None
    dims = [1, 1, 1]
    for bit in range(bits):
        dims[bit % 3] *= 2
    return tuple(dims)


def strides_of(dims):
    return (dims[1] * dims[2], dims[2], 1)


def pairs_along(dims, axis, hops):
    stride = strides_of(dims)[axis]
    count = dims[0] * dims[1] * dims[2]
    found = []
    for source in range(count):
        here = source // stride % dims[axis]
        for begin, end in hops:
            if begin == here:
                found.append((source, source + (end - begin) * stride))
    return found


def pick(array, index, axis):
    return lax.dynamic_index_in_dim(array, index, axis, keepdims=False)


def reduce_line(data, dims, axis, dim_pos, place):
    size = dims[axis]
    if size == 1:
        return jnp.squeeze(data, dim_pos)
    swap = [(0, 1), (1, 0)]
    if size == 2:
        send = pick(data, 1 - place, dim_pos)
        got = lax.ppermute(send, "slab", pairs_along(dims, axis, swap))
        return pick(data, place, dim_pos) + got
    shape = data.shape
    data = data.reshape(shape[:dim_pos] + (2, 2) + shape[dim_pos + 1 :])
    side = place // 2
    near = pick(data, side, dim_pos)
    far = pick(data, 1 - side, dim_pos)
    got = lax.ppermute(far, "slab", pairs_along(dims, axis, [(0, 1), (3, 2)]))
    got = lax.ppermute(far + got, "slab", pairs_along(dims, axis, [(1, 2), (2, 1)]))
    near = near + got
    send = pick(near, 1 - place % 2, dim_pos)
    got = lax.ppermute(send, "slab", pairs_along(dims, axis, swap + [(2, 3), (3, 2)]))
    return pick(near, place % 2, dim_pos) + got


def reduce_scatter(product, dims):
    index = lax.axis_index("slab")
    strides = strides_of(dims)
    places = [index // strides[axis] % dims[axis] for axis in range(3)]
    rows = product.shape[0] // (dims[0] * dims[1] * dims[2])
    chunks = product.reshape(dims + (rows, product.shape[1]))
    parts = []
    first = 0
    done = 0
    for share, order in PIECES:
        done += share
        last = rows * done // 32
        data = chunks[:, :, :, first:last]
        left = [0, 1, 2]
        for axis in order:
            data = reduce_line(data, dims, axis, left.index(axis), places[axis])
            left.remove(axis)
        parts.append(data)
        first = last
    return jnp.concatenate(parts, axis=0)


def sum_slabs(values, count):
    step = 1
    while step < count:
        values = values + lax.ppermute(values, "slab", [(i, i ^ step) for i in range(count)])
        step *= 2
    return values


def padded_2(cells, sides, width):
    for axis, dim in sides:
        count = lax.axis_size(axis)
        head = lax.slice_in_dim(cells, 0, width, axis=dim)
        tail = lax.slice_in_dim(cells, cells.shape[dim] - width, cells.shape[dim], axis=dim)
        if count == 2:
            first = lax.axis_index(axis) == 0
            got = lax.ppermute(jnp.where(first, tail, head), axis, [(0, 1), (1, 0)])
            before, after = jnp.where(first, 0.0, got), jnp.where(first, got, 0.0)
        else:
            ends = count - 1
            before = lax.ppermute(tail, axis, [(i, i + 1) for i in range(ends)])
            after = lax.ppermute(head, axis, [(i + 1, i) for i in range(ends)])
        cells = jnp.concatenate([before, cells, after], axis=dim)
    return cells


def stiffness(padded):
    along_x = padded[:, :, :-2] + padded[:, :, 2:]
    middle = padded[:, :, 1:-1]
    plus_mid = along_x + middle
    plane_sum = plus_mid[:, :-2] + plus_mid[:, 1:-1] + plus_mid[:, 2:]
    total_sum = plane_sum[:-2] + plane_sum[1:-1] + plane_sum[2:]
    cross_xy = along_x[:, :-2] + along_x[:, 2:]
    corner_sum = cross_xy[:-2] + cross_xy[2:]
    face_sum = (
        along_x[1:-1, 1:-1]
        + middle[1:-1, :-2]
        + middle[1:-1, 2:]
        + middle[:-2, 1:-1]
        + middle[2:, 1:-1]
    )
    center = middle[1:-1, 1:-1]
    edge_sum = total_sum - center - face_sum - corner_sum
    return center_weight * center - edge_sum / 6.0 - corner_sum / 12.0


def sweep_once(padded, sources, absorption):
    center = padded[1:-1, 1:-1, 1:-1]
    applied = stiffness(padded) + absorption * center
    return center + omega * (sources - applied) / (center_weight + absorption)


def pad_x(values):
    return jnp.pad(values, ((0, 0), (0, 0), (1, 1)))


def per_device(interior, sources, absorption, bem_panel, incident, node_cell, offset):
    depth_z, depth_y, width_x = interior.shape
    slab_count = lax.axis_size("slab")
    blk_count = lax.axis_size("blk")
    slab_cols = incident.shape[0]
    panel_rows = bem_panel.shape[0]
    own_count = slab_cols // blk_count

    x_faces = jnp.stack([interior[:, :, 0], interior[:, :, width_x - 1]], axis=-1).reshape(-1)
    own_cells = lax.dynamic_slice_in_dim(node_cell, lax.axis_index("blk") * own_count, own_count, 0)
    own_trace = jnp.take(x_faces, own_cells, axis=0)
    trace = lax.all_gather(own_trace, "blk", axis=0, tiled=True)
    fields = (incident.astype(jnp.float32) + trace[:, None]).astype(jnp.bfloat16)
    wide = fields.astype(jnp.float32)
    node_total = slab_cols * slab_count

    common = min(panel_rows, slab_cols)
    shift = offset[0] + lax.axis_index("blk") * panel_rows - lax.axis_index("slab") * slab_cols
    row_at = jnp.clip(-shift, 0, panel_rows - common)
    node_at = jnp.clip(shift, 0, slab_cols - common)
    meets = (shift + panel_rows > 0) & (shift < slab_cols)
    jump = jnp.where(meets, 0.5, 0.0) * lax.dynamic_slice_in_dim(wide, node_at, common, 0)
    product = jnp.dot(bem_panel, fields, preferred_element_type=jnp.float32)
    old = lax.dynamic_slice_in_dim(product, row_at, common, 0)
    product = lax.dynamic_update_slice_in_dim(product, old + jump, row_at, 0)

    owned = reduce_scatter(product, slab_dims(slab_count))
    squares = sum_slabs(jnp.sum(wide * wide, axis=0, keepdims=True), slab_count)
    norms = jnp.sqrt(squares / node_total + 1e-06)

    current = interior
    for sweep_idx in range(SWEEPS):
        padded = padded_2(current, (("slab", 0), ("blk", 1)), 1)
        current = sweep_once(pad_x(padded), sources, absorption)
    return (current, owned / norms)


def solution(mesh):
    in_specs = (
        P("slab", "blk", None),
        P("slab", "blk", None),
        P("slab", "blk", None),
        P("blk", "slab"),
        P("slab", None),
        P("slab"),
        P(),
    )
    out_specs = (P("slab", "blk", None), P(("blk", "slab"), None))
    return jax.shard_map(
        per_device, mesh=mesh, in_specs=in_specs, out_specs=out_specs, check_vma=False
    )
```

time: 295 us -> 242 us (0.82)
  waiting for transfers between devices: 166 us -> 45.2 us
  local copies, waits for them, and re-layouts: 33.9 us -> 109 us
  starting transfers between devices: 13.7 us -> 62.4 us
  blocking collectives: 45.2 us -> 1.77 us
  between operations: 14.9 us -> 1.97 us
  other arithmetic: 5.85 us -> 13.4 us
  matrix products: 13.4 us -> 6.98 us
    reduce_scatter x1 -> x0, waiting for transfers between devices: 130 us -> none  [per_device(): owned = lax.psum_scatter(summed, 'slab', scatter_dimension=0, tiled=True)]
    ppermute x8 -> x30, starting transfers between devices: 13.7 us -> 62.4 us  [the longest x4 17.7 us: reduce_line(): lax.ppermute(send, 'slab', pairs_along(dims, axis, swap + [(2, 3), (3, 2)]))]
    psum x1 -> x0, blocking collectives: 43.3 us -> none  [per_device(): squares = lax.psum(jnp.sum(wide * wide, axis=0), 'slab')]
    dynamic_slice x0 -> x8, local copies, waits for them, and re-layouts: none -> 38.1 us  [pick(): return lax.dynamic_index_in_dim(array, index, axis, keepdims=False)]
    gather x2 -> x0, local copies, waits for them, and re-layouts: 25.9 us -> none  [per_device(): picked = jnp.take(wide, jnp.clip(node_pos, 0, slab_cols - 1), axis=0)]
    slice x0 -> x4, local copies, waits for them, and re-layouts: none -> 23.5 us  [reduce_scatter(): data = chunks[:, :, :, first:last]]
    unnamed x13 -> x37, local copies, waits for them, and re-layouts: 3.16 us -> 17.8 us
    reshape x0 -> x1, local copies, waits for them, and re-layouts: none -> 11.8 us  [reduce_scatter(): chunks = product.reshape(dims + (rows, product.shape[1]))]
  transfers between devices with their start and end apart: 9 -> 30, of which waited for: 5 -> 11; matrix products, arithmetic and copies ran while one was open for 1% -> 50% of each run, Pallas kernels for 0% -> 0%
where the time goes in v1:
time: 242 us; the launch traced here: 241 us
  local copies, waits for them, and re-layouts  109 us (45%)
  starting transfers between devices  62.4 us (26%)
  waiting for transfers between devices  45.2 us (19%)
  other arithmetic  13.4 us (6%)
  matrix products  6.98 us (3%)
    dynamic_slice x8, local copies, waits for them, and re-layouts, pick(): return lax.dynamic_index_in_dim(array, index, axis, keepdims=False)  38.1 us
    slice x4, local copies, waits for them, and re-layouts, reduce_scatter(): data = chunks[:, :, :, first:last]  23.5 us
    unnamed x37, local copies, waits for them, and re-layouts  17.8 us
    ppermute x4, starting transfers between devices, reduce_line(): lax.ppermute(send, 'slab', pairs_along(dims, axis, swap + [(2, 3), (3, 2)]))  17.7 us
    ppermute x8, waiting for transfers between devices, reduce_line(): got = lax.ppermute(send, 'slab', pairs_along(dims, axis, swap))  16.1 us
    ppermute x4, waiting for transfers between devices, reduce_line(): lax.ppermute(send, 'slab', pairs_along(dims, axis, swap + [(2, 3), (3, 2)]))  14.5 us
    ppermute x4, waiting for transfers between devices, reduce_line(): got = lax.ppermute(far, 'slab', pairs_along(dims, axis, [(0, 1), (3, 2)]))  12.5 us
    ppermute x8, starting transfers between devices, reduce_line(): got = lax.ppermute(send, 'slab', pairs_along(dims, axis, swap))  12.1 us
  transfers between devices with their start and end apart: 30, of which 11 were waited for; matrix products, arithmetic and copies ran while one was open for 50% of the time, Pallas kernels for 0%

profile of v1, /device:TPU:0, one launch (start us, length us, event | category | flops | bytes accessed | tf_op | source)
XLA Modules:
  0.0 240.7 jit_solution(10135135305663363980)
XLA Ops:
  2.4 4.8 %collective-permute-start = (f32[1,64,512]{2,1,0:T(8,128)}, f32[1,64,512]{2,1,0:T(8,128)S(1)}, u32[]{:S(2)}, u32[]{:S(2)}) collective-permute-start(f32[1,64,512]{2,1,0:T(8,128)} %get-tuple-element.22), channel_id=1, source_target_pairs={{0,2},{2,4},{4,6},{6,8},{8,10},{10,12},{12,14},{14,16},{16,18},{18... | collective-permute-start | bytes 393224 | tf_op jit(solution)/shard_map/ppermute | solution.py:107
  11.4 3.5 %gather_fusion = f32[512]{0:T(512)S(1)} fusion(f32[256]{0:T(256)S(1)} %reshape.28, s32[1024]{0:T(1024)S(1)} %pad_clamp_fusion), kind=kCustom, calls=%fused_computation | custom fusion | bytes 6144 | tf_op jit(solution)/shard_map/jit(_take)/gather | solution.py:153
  17.3 7.0 %fusion.2 = f32[512,4096]{1,0:T(8,128)S(1)} fusion(bf16[4096,1024]{1,0:T(8,128)(2,1)} %param.10, bf16[1024,512]{0,1:T(8,128)(2,1)S(1)} %copy.23, f32[1024]{0:T(1024)S(1)} %bitcast.93), kind=kOutput, calls=%fused_computation.9 | convolution fusion | flops 4296540160 | bytes 17829888 | tf_op jit(solution)/shard_map/dot_general | solution.py:165
  24.3 3.3 %copy-done.1 = f32[512,4096]{1,0:T(8,128)} copy-done((f32[512,4096]{1,0:T(8,128)}, f32[512,4096]{1,0:T(8,128)S(1)}, u32[]{:S(2)}) %copy-start.1) | copy-done | bytes 8388632
  28.5 2.7 %collective-permute-start.26 = (f32[1,512]{1,0:T(1,128)S(1)}, f32[1,512]{1,0:T(1,128)S(1)}, u32[]{:S(2)}, u32[]{:S(2)}) collective-permute-start(f32[1,512]{1,0:T(1,128)S(1)} %bitcast.96), channel_id=1, source_target_pairs={{0,2},{2,0},{4,6},{6,4},{8,10},{10,8},{12,14},{14,12},{16,18},{18,... | collective-permute-start | bytes 6152 | tf_op jit(solution)/shard_map/ppermute | solution.py:91
  31.2 10.3 %dynamic_update_slice.3 = f32[4096,512]{0,1:T(8,128)} dynamic-update-slice(f32[4096,512]{0,1:T(8,128)} %bitcast.84, f32[1024,512]{0,1:T(8,128)S(1)} %get-tuple-element.17, s32[]{:T(128)S(6)} %min.5, s32[]{:T(128)} %constant.215.clone.1) | dynamic-update-slice | bytes 4194308 | tf_op jit(solution)/shard_map/dynamic_update_slice | solution.py:167
  41.5 11.8 %reshape.29 = f32[4,2,2,256,512]{3,2,1,0,4:T(2,128)} reshape(f32[4096,512]{0,1:T(8,128)} %dynamic_update_slice.3) | data formatting | bytes 16777216 | tf_op jit(solution)/shard_map/reshape | solution.py:71
  53.3 8.6 %slice.247 = f32[4,2,2,32,512]{3,2,1,0,4:T(2,128)} slice(f32[4,2,2,256,512]{3,2,1,0,4:T(2,128)} %reshape.29), slice={[0:4], [0:2], [0:2], [224:256], [0:512]} | slice | bytes 2097152 | tf_op jit(solution)/shard_map/slice | solution.py:78
  61.9 5.0 %constant_dynamic-slice_fusion.1 = (f32[1,2,2,2,32,512]{4,3,2,1,0,5:T(2,128)S(1)}, f32[1,2,2,2,32,512]{4,3,2,1,0,5:T(2,128)}) fusion(f32[2,2,2,2,32,512]{4,3,2,1,0,5:T(2,128)} %bitcast.83, s32[]{:T(128)S(6)} %select_n.173, s32[]{:T(128)S(6)} %select_n.174), kind=kLoop, calls=%fused_computation.105 | loop fusion | bytes 2097160 | tf_op jit(solution)/shard_map/jit(dynamic_index_in_dim)/dynamic_slice | solution.py:41
  66.9 3.8 %copy.40 = f32[1,2,2,2,32,512]{5,4,3,2,1,0:T(8,128)} copy(f32[1,2,2,2,32,512]{4,3,2,1,0,5:T(2,128)} %get-tuple-element.15) | data formatting | bytes 1048576
  70.6 4.7 %collective-permute-start.21 = (f32[2,2,2,32,512]{4,3,2,1,0:T(8,128)}, f32[2,2,2,32,512]{4,3,2,1,0:T(8,128)}, u32[]{:S(2)}, u32[]{:S(2)}) collective-permute-start(f32[2,2,2,32,512]{4,3,2,1,0:T(8,128)} %bitcast.34), channel_id=1, source_target_pairs={{0,8},{2,10},{4,12},{6,14},{24,16},{26,18},{28,20},{30,22},{1,9},{... | collective-permute-start | bytes 1572872 | tf_op jit(solution)/shard_map/ppermute | solution.py:58
  77.6 3.4 %constant_dynamic-slice_fusion.7 = (f32[1,2,2,2,64,512]{4,3,2,1,0,5:T(2,128)}, f32[1,2,2,2,64,512]{4,3,2,1,0,5:T(2,128)}) fusion(f32[2,2,2,2,64,512]{4,3,2,1,0,5:T(2,128)S(1)} %bitcast.82, s32[]{:T(128)S(6)} %select_n.173, s32[]{:T(128)S(6)} %select_n.174), kind=kLoop, calls=%fused_computation.111 | loop fusion | bytes 4194312 | tf_op jit(solution)/shard_map/jit(dynamic_index_in_dim)/dynamic_slice | solution.py:41
  80.9 3.9 %copy.38 = f32[1,2,2,2,64,512]{5,4,3,2,1,0:T(8,128)} copy(f32[1,2,2,2,64,512]{4,3,2,1,0,5:T(2,128)} %get-tuple-element.9) | data formatting | bytes 2097152
  87.2 12.7 %fusion.39 = (f32[4,2,2,80,512]{3,2,1,0,4:T(2,128)}, f32[4,2,2,80,512]{3,2,1,0,4:T(2,128)}) fusion(f32[4,2,2,256,512]{3,2,1,0,4:T(2,128)} %reshape.29), kind=kLoop, calls=%fused_computation.126 | loop fusion | bytes 10485760 | tf_op jit(solution)/shard_map/slice | solution.py:78
  101.3 9.8 %constant_dynamic-slice_fusion.5 = (f32[4,2,1,80,512]{3,2,1,0,4:T(1,128)}, f32[4,2,1,80,512]{3,2,1,0,4:T(1,128)}) fusion(f32[4,2,2,80,512]{3,2,1,0,4:T(2,128)} %get-tuple-element.6, s32[]{:T(128)S(6)} %select_n.179, s32[]{:T(128)S(6)} %select_n.180), kind=kLoop, calls=%fused_computation.109 | loop fusion | bytes 5242888 | tf_op jit(solution)/shard_map/jit(dynamic_index_in_dim)/dynamic_slice | solution.py:41
  113.8 3.3 %collective-permute-start.3 = (f32[1,64,512]{2,1,0:T(8,128)}, f32[1,64,512]{2,1,0:T(8,128)S(1)}, u32[]{:S(2)}, u32[]{:S(2)}) collective-permute-start(f32[1,64,512]{2,1,0:T(8,128)} %get-tuple-element.20), channel_id=1, source_target_pairs={{0,2},{2,4},{4,6},{6,8},{8,10},{10,12},{12,14},{14,16},{16,18},{18... | collective-permute-start | bytes 393224 | tf_op jit(solution)/shard_map/ppermute | solution.py:107
  118.7 3.5 %constant_dynamic-slice_fusion.3 = (f32[4,1,2,80,512]{3,2,1,0,4:T(2,128)}, f32[4,1,2,80,512]{3,2,1,0,4:T(2,128)}) fusion(f32[4,2,2,80,512]{3,2,1,0,4:T(2,128)S(1)} %copy-done, s32[]{:T(128)S(6)} %select_n.183, s32[]{:T(128)S(6)} %select_n.184), kind=kLoop, calls=%fused_computation.107 | loop fusion | bytes 5242888 | tf_op jit(solution)/shard_map/jit(dynamic_index_in_dim)/dynamic_slice | solution.py:41
  124.6 2.9 %copy.37 = f32[1,2,2,2,64,512]{5,4,3,2,1,0:T(8,128)S(1)} copy(f32[1,2,2,2,64,512]{4,3,2,1,0,5:T(2,128)} %get-tuple-element.8) | data formatting | bytes 2097152
  127.4 4.2 %copy.29 = f32[4,2,1,80,512]{4,3,0,1,2:T(8,128)} copy(f32[4,2,1,80,512]{3,2,1,0,4:T(1,128)S(1)} %copy-done.3) | data formatting | bytes 2621440 | tf_op jit(solution)/shard_map/jit(dynamic_index_in_dim)/dynamic_slice | solution.py:41
  131.6 4.0 %copy.31 = f32[4,1,2,80,512]{4,3,0,2,1:T(8,128)} copy(f32[4,1,2,80,512]{3,2,1,0,4:T(2,128)} %get-tuple-element.12) | data formatting | bytes 2621440 | tf_op jit(solution)/shard_map/jit(dynamic_index_in_dim)/dynamic_slice | solution.py:41
  135.6 4.1 %copy.32 = f32[4,1,2,80,512]{4,3,0,2,1:T(8,128)} copy(f32[4,1,2,80,512]{3,2,1,0,4:T(2,128)} %get-tuple-element.13) | data formatting | bytes 2621440 | tf_op jit(solution)/shard_map/jit(dynamic_index_in_dim)/dynamic_slice | solution.py:41
  139.7 4.2 %copy.30 = f32[4,2,1,80,512]{4,3,0,1,2:T(8,128)} copy(f32[4,2,1,80,512]{3,2,1,0,4:T(1,128)S(1)} %copy-done.2) | data formatting | bytes 2621440 | tf_op jit(solution)/shard_map/jit(dynamic_index_in_dim)/dynamic_slice | solution.py:41
  148.1 2.9 %collective-permute-start.29 = (f32[1,512]{1,0:T(1,128)S(1)}, f32[1,512]{1,0:T(1,128)S(1)}, u32[]{:S(2)}, u32[]{:S(2)}) collective-permute-start(f32[1,512]{1,0:T(1,128)S(1)} %add.361), channel_id=1, source_target_pairs={{0,16},{2,18},{4,20},{6,22},{8,24},{10,26},{12,28},{14,30},{16,0},... | collective-permute-start | bytes 6152 | tf_op jit(solution)/shard_map/ppermute | solution.py:91
  160.5 15.0 %collective-permute-start.23 = (f32[2,2,32,512]{3,2,1,0:T(8,128)S(1)}, f32[2,2,32,512]{3,2,1,0:T(8,128)S(1)}, u32[]{:S(2)}, u32[]{:S(2)}) collective-permute-start(f32[2,2,32,512]{3,2,1,0:T(8,128)S(1)} %dynamic-slice_bitcast_fusion.5), channel_id=1, source_target_pairs={{0,8},{2,10},{4,12},{6,14},{8,0},{10,2},{12,4},{14,6},{16,24},{18,... | collective-permute-start | bytes 786440 | tf_op jit(solution)/shard_map/ppermute | solution.py:62
  178.0 3.3 %collective-permute-done.23 = f32[2,2,32,512]{3,2,1,0:T(8,128)S(1)} collective-permute-done((f32[2,2,32,512]{3,2,1,0:T(8,128)S(1)}, f32[2,2,32,512]{3,2,1,0:T(8,128)S(1)}, u32[]{:S(2)}, u32[]{:S(2)}) %collective-permute-start.23) | collective-permute-done | bytes 262176 | tf_op jit(solution)/shard_map/ppermute | solution.py:62
  189.0 10.6 %collective-permute-done.12 = f32[4,80,512]{2,1,0:T(8,128)S(1)} collective-permute-done((f32[4,80,512]{2,1,0:T(8,128)S(1)}, f32[4,80,512]{2,1,0:T(8,128)S(1)}, u32[]{:S(2)}, u32[]{:S(2)}) %collective-permute-start.12) | collective-permute-done | bytes 655392 | tf_op jit(solution)/shard_map/ppermute | solution.py:51
  199.8 3.4 %collective-permute-start.13 = (f32[2,80,512]{2,1,0:T(8,128)S(1)}, f32[2,80,512]{2,1,0:T(8,128)S(1)}, u32[]{:S(2)}, u32[]{:S(2)}) collective-permute-start(f32[2,80,512]{2,1,0:T(8,128)S(1)} %dynamic-slice_bitcast_fusion.4), channel_id=1, source_target_pairs={{0,8},{2,10},{4,12},{6,14},{24,16},{26,18},{28,20},{30,22},{1,9},{... | collective-permute-start | bytes 983048 | tf_op jit(solution)/shard_map/ppermute | solution.py:58
  205.1 6.2 %collective-permute-done.13 = f32[2,80,512]{2,1,0:T(8,128)S(1)} collective-permute-done((f32[2,80,512]{2,1,0:T(8,128)S(1)}, f32[2,80,512]{2,1,0:T(8,128)S(1)}, u32[]{:S(2)}, u32[]{:S(2)}) %collective-permute-start.13) | collective-permute-done | bytes 327712 | tf_op jit(solution)/shard_map/ppermute | solution.py:58
  212.0 6.3 %collective-permute-done.18 = f32[2,80,512]{2,1,0:T(8,128)S(1)} collective-permute-done((f32[2,80,512]{2,1,0:T(8,128)S(1)}, f32[2,80,512]{2,1,0:T(8,128)S(1)}, u32[]{:S(2)}, u32[]{:S(2)}) %collective-permute-start.18) | collective-permute-done | bytes 327712 | tf_op jit(solution)/shard_map/ppermute | solution.py:58
  219.1 7.0 %collective-permute-done.8 = f32[2,2,64,512]{3,2,1,0:T(8,128)S(1)} collective-permute-done((f32[2,2,64,512]{3,2,1,0:T(8,128)S(1)}, f32[2,2,64,512]{3,2,1,0:T(8,128)S(1)}, u32[]{:S(2)}, u32[]{:S(2)}) %collective-permute-start.8) | collective-permute-done | bytes 524320 | tf_op jit(solution)/shard_map/ppermute | solution.py:62
  231.6 3.1 %collective-permute-done.15 = f32[80,512]{1,0:T(8,128)S(1)} collective-permute-done((f32[80,512]{1,0:T(8,128)S(1)}, f32[80,512]{1,0:T(8,128)S(1)}, u32[]{:S(2)}, u32[]{:S(2)}) %collective-permute-start.15) | collective-permute-done | bytes 163872 | tf_op jit(solution)/shard_map/ppermute | solution.py:62
  236.9 2.9 %collective-permute-done.10 = f32[64,512]{1,0:T(8,128)S(1)} collective-permute-done((f32[64,512]{1,0:T(8,128)S(1)}, f32[64,512]{1,0:T(8,128)S(1)}, u32[]{:S(2)}, u32[]{:S(2)}) %collective-permute-start.10) | collective-permute-done | bytes 131104 | tf_op jit(solution)/shard_map/ppermute | solution.py:51
  (143 shorter events, 56.6 us)
Async XLA Ops:
  2.4 98.7 %collective-permute-start = (f32[1,64,512]{2,1,0:T(8,128)}, f32[1,64,512]{2,1,0:T(8,128)S(1)}, u32[]{:S(2)}, u32[]{:S(2)}) collective-permute-start(f32[1,64,512]{2,1,0:T(8,128)} %get-tuple-element.22), channel_id=1, source_target_pairs={{0,2},{2,4},{4,6},{6,8},{8,10},{10,12},{12,14},{14,16},{16,18},{18... | collective-permute-start | bytes 393224 | tf_op jit(solution)/shard_map/ppermute | solution.py:107
  7.2 93.9 %collective-permute-start.1 = (f32[1,64,512]{2,1,0:T(8,128)S(1)}, f32[1,64,512]{2,1,0:T(8,128)S(1)}, u32[]{:S(2)}, u32[]{:S(2)}) collective-permute-start(f32[1,64,512]{2,1,0:T(8,128)S(1)} %get-tuple-element.23), channel_id=1, source_target_pairs={{2,0},{4,2},{6,4},{8,6},{10,8},{12,10},{14,12},{16,14},{18,16},{20... | collective-permute-start | bytes 393224 | tf_op jit(solution)/shard_map/ppermute | solution.py:108
  28.5 71.4 %collective-permute-start.26 = (f32[1,512]{1,0:T(1,128)S(1)}, f32[1,512]{1,0:T(1,128)S(1)}, u32[]{:S(2)}, u32[]{:S(2)}) collective-permute-start(f32[1,512]{1,0:T(1,128)S(1)} %bitcast.96), channel_id=1, source_target_pairs={{0,2},{2,0},{4,6},{6,4},{8,10},{10,8},{12,14},{14,12},{16,18},{18,... | collective-permute-start | bytes 6152 | tf_op jit(solution)/shard_map/ppermute | solution.py:91
  70.6 85.4 %collective-permute-start.21 = (f32[2,2,2,32,512]{4,3,2,1,0:T(8,128)}, f32[2,2,2,32,512]{4,3,2,1,0:T(8,128)}, u32[]{:S(2)}, u32[]{:S(2)}) collective-permute-start(f32[2,2,2,32,512]{4,3,2,1,0:T(8,128)} %bitcast.34), channel_id=1, source_target_pairs={{0,8},{2,10},{4,12},{6,14},{24,16},{26,18},{28,20},{30,22},{1,9},{... | collective-permute-start | bytes 1572872 | tf_op jit(solution)/shard_map/ppermute | solution.py:58
  84.8 16.3 %copy-start.6 = (f32[2,64,512]{2,1,0:T(8,128)S(1)}, f32[2,64,512]{2,1,0:T(8,128)}, u32[]{:S(2)}) copy-start(f32[2,64,512]{2,1,0:T(8,128)} %param.7) | copy-start | bytes 786436
  84.8 90.7 %collective-permute-start.6 = (f32[2,2,2,64,512]{4,3,2,1,0:T(8,128)}, f32[2,2,2,64,512]{4,3,2,1,0:T(8,128)}, u32[]{:S(2)}, u32[]{:S(2)}) collective-permute-start(f32[2,2,2,64,512]{4,3,2,1,0:T(8,128)} %bitcast.7), channel_id=1, source_target_pairs={{0,8},{2,10},{4,12},{6,14},{24,16},{26,18},{28,20},{30,22},{1,9},{... | collective-permute-start | bytes 3145736 | tf_op jit(solution)/shard_map/ppermute | solution.py:58
  99.9 11.2 %collective-permute-start.27 = (f32[1,512]{1,0:T(1,128)S(1)}, f32[1,512]{1,0:T(1,128)S(1)}, u32[]{:S(2)}, u32[]{:S(2)}) collective-permute-start(f32[1,512]{1,0:T(1,128)S(1)} %add.359), channel_id=1, source_target_pairs={{0,4},{2,6},{4,0},{6,2},{8,12},{10,14},{12,8},{14,10},{16,20},{18,... | collective-permute-start | bytes 6152 | tf_op jit(solution)/shard_map/ppermute | solution.py:91
  101.2 10.0 %collective-permute-start.2 = (f32[4,1,512]{2,1,0:T(1,128)S(1)}, f32[4,1,512]{2,1,0:T(1,128)S(1)}, u32[]{:S(2)}, u32[]{:S(2)}) collective-permute-start(f32[4,1,512]{2,1,0:T(1,128)S(1)} %broadcast_select_fusion.5), channel_id=1, source_target_pairs={{0,1},{1,0},{2,3},{3,2},{4,5},{5,4},{6,7},{7,6},{8,9},{9,8},{10,11... | collective-permute-start | bytes 24584 | tf_op jit(solution)/shard_map/ppermute | solution.py:103
  111.1 32.8 %collective-permute-start.28 = (f32[1,512]{1,0:T(1,128)S(1)}, f32[1,512]{1,0:T(1,128)S(1)}, u32[]{:S(2)}, u32[]{:S(2)}) collective-permute-start(f32[1,512]{1,0:T(1,128)S(1)} %add.360), channel_id=1, source_target_pairs={{0,8},{2,10},{4,12},{6,14},{8,0},{10,2},{12,4},{14,6},{16,24},{18,... | collective-permute-start | bytes 6152 | tf_op jit(solution)/shard_map/ppermute | solution.py:91
  113.8 32.8 %collective-permute-start.3 = (f32[1,64,512]{2,1,0:T(8,128)}, f32[1,64,512]{2,1,0:T(8,128)S(1)}, u32[]{:S(2)}, u32[]{:S(2)}) collective-permute-start(f32[1,64,512]{2,1,0:T(8,128)} %get-tuple-element.20), channel_id=1, source_target_pairs={{0,2},{2,4},{4,6},{6,8},{8,10},{10,12},{12,14},{14,16},{16,18},{18... | collective-permute-start | bytes 393224 | tf_op jit(solution)/shard_map/ppermute | solution.py:107
  117.1 31.0 %collective-permute-start.4 = (f32[1,64,512]{2,1,0:T(8,128)}, f32[1,64,512]{2,1,0:T(8,128)}, u32[]{:S(2)}, u32[]{:S(2)}) collective-permute-start(f32[1,64,512]{2,1,0:T(8,128)} %get-tuple-element.21), channel_id=1, source_target_pairs={{2,0},{4,2},{6,4},{8,6},{10,8},{12,10},{14,12},{16,14},{18,16},{20... | collective-permute-start | bytes 393224 | tf_op jit(solution)/shard_map/ppermute | solution.py:108
  143.9 38.6 %collective-permute-start.11 = (f32[4,2,80,512]{3,2,0,1:T(8,128)}, f32[4,2,80,512]{3,2,0,1:T(8,128)S(1)}, u32[]{:S(2)}, u32[]{:S(2)}) collective-permute-start(f32[4,2,80,512]{3,2,0,1:T(8,128)} %bitcast.92), channel_id=1, source_target_pairs={{0,2},{2,0},{4,6},{6,4},{8,10},{10,8},{12,14},{14,12},{16,18},{18,... | collective-permute-start | bytes 3932168 | tf_op jit(solution)/shard_map/ppermute | solution.py:51
  146.6 37.4 %collective-permute-start.16 = (f32[4,2,80,512]{3,2,0,1:T(8,128)}, f32[4,2,80,512]{3,2,0,1:T(8,128)S(1)}, u32[]{:S(2)}, u32[]{:S(2)}) collective-permute-start(f32[4,2,80,512]{3,2,0,1:T(8,128)} %bitcast.91), channel_id=1, source_target_pairs={{0,4},{2,6},{4,0},{6,2},{8,12},{10,14},{12,8},{14,10},{16,20},{18,... | collective-permute-start | bytes 3932168 | tf_op jit(solution)/shard_map/ppermute | solution.py:51
  148.1 4.5 %collective-permute-start.29 = (f32[1,512]{1,0:T(1,128)S(1)}, f32[1,512]{1,0:T(1,128)S(1)}, u32[]{:S(2)}, u32[]{:S(2)}) collective-permute-start(f32[1,512]{1,0:T(1,128)S(1)} %add.361), channel_id=1, source_target_pairs={{0,16},{2,18},{4,20},{6,22},{8,24},{10,26},{12,28},{14,30},{16,0},... | collective-permute-start | bytes 6152 | tf_op jit(solution)/shard_map/ppermute | solution.py:91
  152.6 1.2 collective-permute-start.5
  157.4 3.0 %collective-permute-start.22 = (f32[2,2,2,32,512]{4,3,2,1,0:T(8,128)S(1)}, f32[2,2,2,32,512]{4,3,2,1,0:T(8,128)S(1)}, u32[]{:S(2)}, u32[]{:S(2)}) collective-permute-start(f32[2,2,2,32,512]{4,3,2,1,0:T(8,128)S(1)} %bitcast_add_fusion.16), channel_id=1, source_target_pairs={{8,16},{10,18},{12,20},{14,22},{16,8},{18,10},{20,12},{22,14},{9,1... | collective-permute-start | bytes 1572872 | tf_op jit(solution)/shard_map/ppermute | solution.py:59
  160.5 21.9 %copy-start.5 = (f32[4,2,1,80,512]{4,3,0,1,2:T(8,128)S(1)}, f32[4,2,1,80,512]{4,3,0,1,2:T(8,128)}, u32[]{:S(2)}) copy-start(f32[4,2,1,80,512]{4,3,0,1,2:T(8,128)} %copy.29) | copy-start | bytes 3932164
  160.5 20.8 %collective-permute-start.23 = (f32[2,2,32,512]{3,2,1,0:T(8,128)S(1)}, f32[2,2,32,512]{3,2,1,0:T(8,128)S(1)}, u32[]{:S(2)}, u32[]{:S(2)}) collective-permute-start(f32[2,2,32,512]{3,2,1,0:T(8,128)S(1)} %dynamic-slice_bitcast_fusion.5), channel_id=1, source_target_pairs={{0,8},{2,10},{4,12},{6,14},{8,0},{10,2},{12,4},{14,6},{16,24},{18,... | collective-permute-start | bytes 786440 | tf_op jit(solution)/shard_map/ppermute | solution.py:62
  177.3 27.4 %collective-permute-start.7 = (f32[2,2,2,64,512]{4,3,2,1,0:T(8,128)S(1)}, f32[2,2,2,64,512]{4,3,2,1,0:T(8,128)S(1)}, u32[]{:S(2)}, u32[]{:S(2)}) collective-permute-start(f32[2,2,2,64,512]{4,3,2,1,0:T(8,128)S(1)} %bitcast_add_fusion.17), channel_id=1, source_target_pairs={{8,16},{10,18},{12,20},{14,22},{16,8},{18,10},{20,12},{22,14},{9,1... | collective-permute-start | bytes 3145736 | tf_op jit(solution)/shard_map/ppermute | solution.py:59
  181.4 6.5 %collective-permute-start.24 = (f32[2,32,512]{2,1,0:T(8,128)S(1)}, f32[2,32,512]{2,1,0:T(8,128)S(1)}, u32[]{:S(2)}, u32[]{:S(2)}) collective-permute-start(f32[2,32,512]{2,1,0:T(8,128)S(1)} %dynamic-slice_bitcast_fusion.9), channel_id=1, source_target_pairs={{0,4},{2,6},{4,0},{6,2},{8,12},{10,14},{12,8},{14,10},{16,20},{18,... | collective-permute-start | bytes 393224 | tf_op jit(solution)/shard_map/ppermute | solution.py:51
  182.8 16.8 %collective-permute-start.12 = (f32[4,80,512]{2,1,0:T(8,128)S(1)}, f32[4,80,512]{2,1,0:T(8,128)S(1)}, u32[]{:S(2)}, u32[]{:S(2)}) collective-permute-start(f32[4,80,512]{2,1,0:T(8,128)S(1)} %dynamic-slice_bitcast_fusion.1), channel_id=1, source_target_pairs={{0,4},{2,6},{4,0},{6,2},{8,12},{10,14},{12,8},{14,10},{16,20},{18,... | collective-permute-start | bytes 1966088 | tf_op jit(solution)/shard_map/ppermute | solution.py:51
  184.3 18.9 %collective-permute-start.17 = (f32[4,80,512]{2,1,0:T(8,128)S(1)}, f32[4,80,512]{2,1,0:T(8,128)S(1)}, u32[]{:S(2)}, u32[]{:S(2)}) collective-permute-start(f32[4,80,512]{2,1,0:T(8,128)S(1)} %dynamic-slice_bitcast_fusion), channel_id=1, source_target_pairs={{0,2},{2,0},{4,6},{6,4},{8,10},{10,8},{12,14},{14,12},{16,18},{18,... | collective-permute-start | bytes 1966088 | tf_op jit(solution)/shard_map/ppermute | solution.py:51
  188.0 17.1 %collective-permute-start.25 = (f32[32,512]{1,0:T(8,128)S(1)}, f32[32,512]{1,0:T(8,128)S(1)}, u32[]{:S(2)}, u32[]{:S(2)}) collective-permute-start(f32[32,512]{1,0:T(8,128)S(1)} %dynamic-slice_bitcast_fusion.11), channel_id=1, source_target_pairs={{0,2},{2,0},{4,6},{6,4},{8,10},{10,8},{12,14},{14,12},{16,18},{18,... | collective-permute-start | bytes 196616 | tf_op jit(solution)/shard_map/ppermute | solution.py:51
  199.8 11.5 %collective-permute-start.13 = (f32[2,80,512]{2,1,0:T(8,128)S(1)}, f32[2,80,512]{2,1,0:T(8,128)S(1)}, u32[]{:S(2)}, u32[]{:S(2)}) collective-permute-start(f32[2,80,512]{2,1,0:T(8,128)S(1)} %dynamic-slice_bitcast_fusion.4), channel_id=1, source_target_pairs={{0,8},{2,10},{4,12},{6,14},{24,16},{26,18},{28,20},{30,22},{1,9},{... | collective-permute-start | bytes 983048 | tf_op jit(solution)/shard_map/ppermute | solution.py:58
  203.3 15.0 %collective-permute-start.18 = (f32[2,80,512]{2,1,0:T(8,128)S(1)}, f32[2,80,512]{2,1,0:T(8,128)S(1)}, u32[]{:S(2)}, u32[]{:S(2)}) collective-permute-start(f32[2,80,512]{2,1,0:T(8,128)S(1)} %dynamic-slice_bitcast_fusion.3), channel_id=1, source_target_pairs={{0,8},{2,10},{4,12},{6,14},{24,16},{26,18},{28,20},{30,22},{1,9},{... | collective-permute-start | bytes 983048 | tf_op jit(solution)/shard_map/ppermute | solution.py:58
  204.9 21.1 %collective-permute-start.8 = (f32[2,2,64,512]{3,2,1,0:T(8,128)S(1)}, f32[2,2,64,512]{3,2,1,0:T(8,128)S(1)}, u32[]{:S(2)}, u32[]{:S(2)}) collective-permute-start(f32[2,2,64,512]{3,2,1,0:T(8,128)S(1)} %dynamic-slice_bitcast_fusion.2), channel_id=1, source_target_pairs={{0,8},{2,10},{4,12},{6,14},{8,0},{10,2},{12,4},{14,6},{16,24},{18,... | collective-permute-start | bytes 1572872 | tf_op jit(solution)/shard_map/ppermute | solution.py:62
  211.3 17.4 %collective-permute-start.14 = (f32[2,80,512]{2,1,0:T(8,128)S(1)}, f32[2,80,512]{2,1,0:T(8,128)S(1)}, u32[]{:S(2)}, u32[]{:S(2)}) collective-permute-start(f32[2,80,512]{2,1,0:T(8,128)S(1)} %fusion.44), channel_id=1, source_target_pairs={{8,16},{10,18},{12,20},{14,22},{16,8},{18,10},{20,12},{22,14},{9,1... | collective-permute-start | bytes 983048 | tf_op jit(solution)/shard_map/ppermute | solution.py:59
  218.4 13.0 %collective-permute-start.19 = (f32[2,80,512]{2,1,0:T(8,128)S(1)}, f32[2,80,512]{2,1,0:T(8,128)S(1)}, u32[]{:S(2)}, u32[]{:S(2)}) collective-permute-start(f32[2,80,512]{2,1,0:T(8,128)S(1)} %fusion.45), channel_id=1, source_target_pairs={{8,16},{10,18},{12,20},{14,22},{16,8},{18,10},{20,12},{22,14},{9,1... | collective-permute-start | bytes 983048 | tf_op jit(solution)/shard_map/ppermute | solution.py:59
  226.2 8.6 %collective-permute-start.9 = (f32[2,64,512]{2,1,0:T(8,128)S(1)}, f32[2,64,512]{2,1,0:T(8,128)S(1)}, u32[]{:S(2)}, u32[]{:S(2)}) collective-permute-start(f32[2,64,512]{2,1,0:T(8,128)S(1)} %dynamic-slice_bitcast_fusion.6), channel_id=1, source_target_pairs={{0,2},{2,0},{4,6},{6,4},{8,10},{10,8},{12,14},{14,12},{16,18},{18,... | collective-permute-start | bytes 786440 | tf_op jit(solution)/shard_map/ppermute | solution.py:51
  228.9 5.8 %collective-permute-start.15 = (f32[80,512]{1,0:T(8,128)S(1)}, f32[80,512]{1,0:T(8,128)S(1)}, u32[]{:S(2)}, u32[]{:S(2)}) collective-permute-start(f32[80,512]{1,0:T(8,128)S(1)} %dynamic-slice_bitcast_fusion.8), channel_id=1, source_target_pairs={{0,8},{2,10},{4,12},{6,14},{8,0},{10,2},{12,4},{14,6},{16,24},{18,... | collective-permute-start | bytes 491528 | tf_op jit(solution)/shard_map/ppermute | solution.py:62
  231.5 5.4 %collective-permute-start.20 = (f32[80,512]{1,0:T(8,128)S(1)}, f32[80,512]{1,0:T(8,128)S(1)}, u32[]{:S(2)}, u32[]{:S(2)}) collective-permute-start(f32[80,512]{1,0:T(8,128)S(1)} %dynamic-slice_bitcast_fusion.7), channel_id=1, source_target_pairs={{0,8},{2,10},{4,12},{6,14},{8,0},{10,2},{12,4},{14,6},{16,24},{18,... | collective-permute-start | bytes 491528 | tf_op jit(solution)/shard_map/ppermute | solution.py:62
  234.8 5.0 %collective-permute-start.10 = (f32[64,512]{1,0:T(8,128)S(1)}, f32[64,512]{1,0:T(8,128)S(1)}, u32[]{:S(2)}, u32[]{:S(2)}) collective-permute-start(f32[64,512]{1,0:T(8,128)S(1)} %dynamic-slice_bitcast_fusion.10), channel_id=1, source_target_pairs={{0,4},{2,6},{4,0},{6,2},{8,12},{10,14},{12,8},{14,10},{16,20},{18,... | collective-permute-start | bytes 393224 | tf_op jit(solution)/shard_map/ppermute | solution.py:51
  (13 other events, 58.5 us)

commit v2 on v0

v2 whole, which is shorter than its diff:
```python
import functools

import jax
import jax.numpy as jnp
from jax import lax
from jax.experimental import pallas as pl
from jax.experimental.pallas import tpu as pltpu
from jax.sharding import PartitionSpec as P

SWEEPS = 2

omega = 0.6
center_weight = 8.0 / 3.0
LANES = 128
ROW_UNIT = 16
TILE = 8
LIMIT = 24 * 2**20

PIECES = ((2, (0, 2, 1)), (4, (1, 2, 0)), (4, (2, 0, 1)), (3, (0, 1, 2)), (3, (1, 2, 0)))
ARRIVALS = (0, 0, 1, 3, 2, 0, 1, 0, 4, 2, 0, 3, 1, 4, 2, 3, 4, 1, 3, 2, 4, 3, 1, 2, 4)
EARLY = 3
CARRIER = 0


def slab_dims(count):
    bits = count.bit_length() - 1
    if count != 1 << bits or bits > 6:
        return None
    dims = [1, 1, 1]
    for bit in range(bits):
        dims[bit % 3] *= 2
    return tuple(dims)


def strides_of(dims):
    return (dims[1] * dims[2], dims[2], 1)


def pairs_along(dims, axis, hops):
    stride = strides_of(dims)[axis]
    count = dims[0] * dims[1] * dims[2]
    found = []
    for source in range(count):
        here = source // stride % dims[axis]
        for begin, end in hops:
            if begin == here:
                found.append((source, source + (end - begin) * stride))
    return found


def others_of(axis):
    return [other for other in range(3) if other != axis]


class Piece:
    def __init__(self, first, rows, order, dims, extra):
        self.first, self.rows, self.order, self.dims, self.extra = first, rows, order, dims, extra
        self.steps = []
        left = [0, 1, 2]
        for axis in order:
            count = 1
            for other in left:
                count *= dims[other] if other != axis else 1
            if dims[axis] == 2:
                self.steps.append(("swap", axis, tuple(left), count))
            elif dims[axis] == 4:
                for kind in ("outer", "inner", "swap4"):
                    self.steps.append((kind, axis, tuple(left), count))
            left.remove(axis)

    def height(self):
        return self.rows + self.extra

    def halves(self, number, places):
        _, axis, left, _ = self.steps[number]
        spans = [self.dims[other] for other in left]
        at = left.index(axis)
        inner = 1
        for span in spans[at + 1 :]:
            inner *= span
        outer = 1
        for span in spans[:at]:
            outer *= span
        size, place = spans[at], places[axis]
        if size == 2:
            sent, kept = [1 - place], [place]
        else:
            side = place // 2
            sent, kept = [2 - 2 * side, 3 - 2 * side], [2 * side, 2 * side + 1]
        return [
            [i * (size * inner) + block * inner + j for i in range(outer) for block in half for j in range(inner)]
            for half in (sent, kept)
        ]

    def halves_of_two(self, number, places):
        _, axis, left, _ = self.steps[number]
        inner = 1
        for other in left[left.index(axis) + 1 :]:
            inner *= self.dims[other]
        outer = self.steps[number][3] // inner
        own = lax.rem(jnp.asarray(places[axis], jnp.int32), 2)
        return [
            [i * (2 * inner) + at * inner + j for i in range(outer) for j in range(inner)]
            for at in (1 - own, own)
        ]

    def window(self, which, places):
        axis = self.order[0]
        place, index = places[axis], [slice(None)] * 3
        if self.dims[axis] == 2:
            index[axis] = 1 - place if which == 0 else place
        else:
            side = place // 2
            index[axis] = pl.ds(2 - 2 * side if which == 0 else 2 * side, 2)
        return tuple(index) + (pl.ds(self.first, self.rows), slice(None))

    def window_shape(self):
        axis = self.order[0]
        spans = [self.dims[other] // 2 if other == axis else self.dims[other] for other in range(3)]
        if self.dims[axis] == 2:
            del spans[axis]
        return tuple(spans) + (self.rows,)

    def pairs(self, number):
        kind, axis, _, _ = self.steps[number]
        hops = {
            "swap": [(0, 1), (1, 0)],
            "outer": [(0, 1), (3, 2)],
            "inner": [(1, 2), (2, 1)],
            "swap4": [(0, 1), (1, 0), (2, 3), (3, 2)],
        }[kind]
        return pairs_along(self.dims, axis, hops)


def places_of(slab, dims):
    strides = strides_of(dims)
    return [lax.rem(lax.div(slab, strides[axis]), dims[axis]) for axis in range(3)]


def panel_copies(pieces, which, panel, panel_bufs, sems):
    places = places_of(lax.axis_index("slab"), pieces[0].dims)
    jobs = []
    for number, piece in enumerate(pieces):
        copy = pltpu.make_async_copy(
            panel.at[piece.window(which, places)], panel_bufs[number], sems.at[number]
        )
        copy.start()
        jobs.append((piece, piece.halves(0, places)[which], copy, panel_bufs[number]))
    return jobs


def multiply(jobs, shift, chunk_rows, fields, squares, outs):
    node_count, width = fields.shape
    for (piece, chunks, copy, panel_buf), out in zip(jobs, outs):
        copy.wait()
        rows = piece.rows
        lhs = panel_buf[...].reshape(len(chunks) * rows, node_count)
        product = jnp.dot(lhs, fields[...], preferred_element_type=jnp.float32)
        for block, chunk in enumerate(chunks):
            out[block, 0:rows, :] = product[block * rows : (block + 1) * rows]
            node = shift + chunk * chunk_rows

            @pl.when((node >= 0) & (node < node_count))
            def _(block=block, node=node):
                at = pl.multiple_of(node + piece.first, ROW_UNIT)
                jump = fields[pl.ds(at, rows), :].astype(jnp.float32)
                out[block, 0:rows, :] += 0.5 * jump

            if piece.extra:
                row = lax.broadcasted_iota(jnp.int32, (TILE, width), 0)
                out[block, rows : rows + TILE, :] = jnp.where(row == 0, squares[...], 0.0)


def make_fields(blk, interiors, cells, incident, fields, squares):
    tables = []
    for block in interiors:
        depth_z, depth_y, width = block.shape
        flat_left = block[:, :, :LANES].reshape(depth_z * depth_y, LANES)
        flat_right = block[:, :, width - LANES :].reshape(depth_z * depth_y, LANES)
        tables.append((flat_left.T[0:1, :], flat_right.T[LANES - 1 : LANES, :]))
    node_count = incident.shape[0]
    per_block = node_count // (2 if len(interiors) == 2 else len(interiors))
    across = cells[...].T
    lane = lax.broadcasted_iota(jnp.int32, (LANES, tables[0][0].shape[1]), 1)
    total = jnp.zeros((8, incident.shape[1]), jnp.float32)
    for part in range(node_count // LANES):
        owner = part * LANES // per_block
        if len(interiors) == 2:
            mine = blk == owner
            left = jnp.where(mine, tables[0][0], tables[1][0])
            right = jnp.where(mine, tables[0][1], tables[1][1])
        else:
            left, right = tables[owner]
        cell = across[:, part : part + 1]
        column = cell >> 1
        value = jnp.where((cell & 1) == 1, right, left)
        trace = jnp.sum(jnp.where(lane == column, value, 0.0), axis=1, keepdims=True)
        rows = pl.ds(part * LANES, LANES)
        field = (incident[rows, :].astype(jnp.float32) + trace).astype(jnp.bfloat16)
        fields[rows, :] = field
        wide = field.astype(jnp.float32)
        total = total + jnp.sum((wide * wide).reshape(LANES // 8, 8, wide.shape[1]), axis=0)
    squares[...] = jnp.sum(total, axis=0, keepdims=True)


def shift_of(offset, panel_rows, node_count):
    return (
        offset[0] + lax.axis_index("blk") * panel_rows - lax.axis_index("slab") * node_count
    )


def first_kernel(pieces, blocks, offset, *refs):
    interiors, refs = refs[:blocks], refs[blocks:]
    cells, incident, panel, fields, squares = refs[:5]
    count = len(pieces)
    outs, refs = refs[5 : 5 + count], refs[5 + count :]
    panel_bufs, refs = refs[:count], refs[count:]
    interior_bufs, refs = refs[:blocks], refs[blocks:]
    cells_buf, incident_buf, sems, in_sems = refs
    copies = []
    sources = list(interiors) + [cells, incident]
    targets = list(interior_bufs) + [cells_buf, incident_buf]
    for number, (source, target) in enumerate(zip(sources, targets)):
        copy = pltpu.make_async_copy(source, target, in_sems.at[number])
        copy.start()
        copies.append(copy)
    jobs = panel_copies(pieces, 0, panel, panel_bufs, sems)
    for copy in copies:
        copy.wait()
    make_fields(lax.axis_index("blk"), interior_bufs, cells_buf, incident_buf, fields, squares)
    chunk_rows = panel.shape[3]
    shift = shift_of(offset, chunk_rows * lax.axis_size("slab"), incident.shape[0])
    multiply(jobs, shift, chunk_rows, fields, squares, outs)


def later_kernel(pieces, which, offset, fields, squares, panel, token, *refs):
    count = len(pieces)
    outs, panel_bufs = refs[:count], refs[count : 2 * count]
    sems = refs[2 * count]
    jobs = panel_copies(pieces, which, panel, panel_bufs, sems)
    chunk_rows = panel.shape[3]
    shift = shift_of(offset, chunk_rows * lax.axis_size("slab"), fields.shape[0])
    multiply(jobs, shift, chunk_rows, fields, squares, outs)


def piece_scratch(pieces, depth):
    return [
        pltpu.VMEM(piece.window_shape() + (depth,), jnp.bfloat16) for piece in pieces
    ], pltpu.SemaphoreType.DMA((len(pieces),))


def piece_shapes(pieces, width):
    return [
        pltpu.VMEM((len(piece.halves(0, [0, 0, 0])[0]), piece.height(), width), jnp.float32)
        for piece in pieces
    ]


def piece_cost(pieces, depth, width):
    rows = sum(piece.rows * len(piece.halves(0, [0, 0, 0])[0]) for piece in pieces)
    return pl.CostEstimate(
        flops=2 * rows * depth * width, bytes_accessed=2 * rows * depth, transcendentals=0
    )


IN_HBM = pl.BlockSpec(memory_space=pltpu.HBM)
ANYWHERE = pl.BlockSpec(memory_space=pl.ANY)
IN_VMEM = pl.BlockSpec(memory_space=pltpu.VMEM)
IN_SMEM = pl.BlockSpec(memory_space=pltpu.SMEM)
PARAMS = pltpu.CompilerParams(vmem_limit_bytes=LIMIT)


def in_hbm(array):
    return pltpu.with_memory_space_constraint(array, pltpu.HBM)


def first_products(pieces, offset, interiors, cells, incident, panel):
    depth, width = incident.shape
    bufs, sems = piece_scratch(pieces, depth)
    return pl.pallas_call(
        functools.partial(first_kernel, pieces, len(interiors)),
        in_specs=[IN_SMEM] + [ANYWHERE] * len(interiors) + [IN_HBM] * 3,
        out_specs=[IN_VMEM] * (2 + len(pieces)),
        out_shape=[pltpu.VMEM(incident.shape, jnp.bfloat16), pltpu.VMEM((1, width), jnp.float32)]
        + piece_shapes(pieces, width),
        scratch_shapes=bufs
        + [pltpu.VMEM(block.shape, block.dtype) for block in interiors]
        + [pltpu.VMEM(cells.shape, cells.dtype), pltpu.VMEM(incident.shape, incident.dtype)]
        + [sems, pltpu.SemaphoreType.DMA((len(interiors) + 2,))],
        compiler_params=PARAMS,
        cost_estimate=piece_cost(pieces, depth, width),
        name="fields_and_first_rows",
    )(offset, in_hbm(interiors[0]), *interiors[1:], in_hbm(cells), in_hbm(incident), in_hbm(panel))


def later_products(pieces, which, offset, fields, squares, panel, token):
    depth, width = fields.shape
    bufs, sems = piece_scratch(pieces, depth)
    return pl.pallas_call(
        functools.partial(later_kernel, pieces, which),
        in_specs=[IN_SMEM, IN_VMEM, IN_VMEM, IN_HBM, ANYWHERE],
        out_specs=[IN_VMEM] * len(pieces),
        out_shape=piece_shapes(pieces, width),
        scratch_shapes=bufs + [sems],
        compiler_params=PARAMS,
        cost_estimate=piece_cost(pieces, depth, width),
        name="kept_rows" if which else "sent_rows",
    )(offset, fields, squares, in_hbm(panel), token)


def arrival_kernel(pick_blocks, dims, got, base, token, *outs):
    picked = pick_blocks(places_of(lax.axis_index("slab"), dims))
    for blocks, out in zip(picked, outs):
        for number, block in enumerate(blocks):
            out[number] = got[block] + base[block]


def add_arrival(pick_blocks, dims, got, base, token, name):
    shapes = [
        pltpu.VMEM((len(blocks),) + base.shape[1:], jnp.float32) for blocks in pick_blocks([0, 0, 0])
    ]
    return pl.pallas_call(
        functools.partial(arrival_kernel, pick_blocks, dims),
        in_specs=[IN_VMEM, IN_VMEM, ANYWHERE],
        out_specs=[IN_VMEM] * len(shapes),
        out_shape=shapes,
        compiler_params=PARAMS,
        cost_estimate=pl.CostEstimate(flops=base.size, bytes_accessed=4 * base.size, transcendentals=0),
        name=name,
    )(got, base, token)


class Course:
    def __init__(self, piece, number, far, near):
        self.piece, self.number = piece, number
        self.step, self.near, self.sent = 0, near, far
        self.done = None
        self.start()

    def start(self):
        self.got = lax.ppermute(self.sent, "slab", self.piece.pairs(self.step))

    def arrive(self, token):
        piece, step = self.piece, self.step
        kind, axis, _, count = piece.steps[step]
        last = step + 1 == len(piece.steps)
        base = self.near
        if kind == "outer":
            base = self.sent
            pick_blocks = lambda places: [list(range(2 * count))]
        elif kind == "inner":
            pick_blocks = lambda places: piece.halves_of_two(step, places)
        elif last:
            pick_blocks = lambda places: [[0]]
        else:
            pick_blocks = lambda places: piece.halves(step + 1, places)
        outs = add_arrival(
            pick_blocks, piece.dims, self.got, base, token, f"arrival_{self.number}_{step}"
        )
        if last:
            self.done = outs[0]
        else:
            if kind != "outer":
                self.near = outs[1]
            self.sent = outs[0]
            self.step += 1
            self.start()
        return outs[0]


def finish_kernel(node_total, carrier, rows, *refs):
    parts, out = refs[:-1], refs[-1]
    squares = parts[carrier][0, rows[carrier] : rows[carrier] + 1, :]
    norms = jnp.sqrt(squares / node_total + 1e-06)
    first = 0
    for part, height in zip(parts, rows):
        out[first : first + height, :] = part[0, :height, :] / norms
        first += height


def edge_rows(cells, other):
    count = lax.axis_size("blk")
    head, tail = cells[:, :1], cells[:, -1:]
    if count == 2:
        first = lax.axis_index("blk") == 0
        if other is None:
            got = lax.ppermute(jnp.where(first, tail, head), "blk", [(0, 1), (1, 0)])
        else:
            got = jnp.where(first, other[:, :1], other[:, -1:])
        return jnp.where(first, 0.0, got), jnp.where(first, got, 0.0)
    ends = count - 1
    return (
        lax.ppermute(tail, "blk", [(i, i + 1) for i in range(ends)]),
        lax.ppermute(head, "blk", [(i + 1, i) for i in range(ends)]),
    )


def with_halo(cells, other):
    before, after = edge_rows(cells, other)
    cells = jnp.concatenate([before, cells, after], axis=1)
    ends = lax.axis_size("slab") - 1
    below = lax.ppermute(cells[-1:], "slab", [(i, i + 1) for i in range(ends)])
    above = lax.ppermute(cells[:1], "slab", [(i + 1, i) for i in range(ends)])
    return jnp.concatenate([below, cells, above], axis=0)


def stiffness(padded):
    along_x = padded[:, :, :-2] + padded[:, :, 2:]
    middle = padded[:, :, 1:-1]
    plus_mid = along_x + middle
    plane_sum = plus_mid[:, :-2] + plus_mid[:, 1:-1] + plus_mid[:, 2:]
    total_sum = plane_sum[:-2] + plane_sum[1:-1] + plane_sum[2:]
    cross_xy = along_x[:, :-2] + along_x[:, 2:]
    corner_sum = cross_xy[:-2] + cross_xy[2:]
    face_sum = (
        along_x[1:-1, 1:-1]
        + middle[1:-1, :-2]
        + middle[1:-1, 2:]
        + middle[:-2, 1:-1]
        + middle[2:, 1:-1]
    )
    center = middle[1:-1, 1:-1]
    edge_sum = total_sum - center - face_sum - corner_sum
    return center_weight * center - edge_sum / 6.0 - corner_sum / 12.0


def sweep_once(padded, sources, absorption):
    center = padded[1:-1, 1:-1, 1:-1]
    applied = stiffness(padded) + absorption * center
    return center + omega * (sources - applied) / (center_weight + absorption)


def pad_x(values):
    return jnp.pad(values, ((0, 0), (0, 0), (1, 1)))


def per_device(interior, sources, absorption, bem_panel, incident, node_cell, offset):
    slab_count = lax.axis_size("slab")
    blk_count = lax.axis_size("blk")
    slab_cols, width = incident.shape
    panel_rows = bem_panel.shape[0]
    node_total = slab_cols * slab_count
    chunk_rows = panel_rows // slab_count
    dims = slab_dims(slab_count)

    if blk_count == 2:
        other = lax.ppermute(interior, "blk", [(0, 1), (1, 0)])
        interiors = [interior, other]
    else:
        other = None
        gathered = lax.all_gather(interior, "blk", axis=0)
        interiors = [gathered[i] for i in range(blk_count)]

    units, first, done = chunk_rows // ROW_UNIT, 0, 0
    spans = []
    for share, order in PIECES:
        done += share
        last = (units * done // 16) * ROW_UNIT
        if last > first:
            spans.append((first, last - first, order))
        first = last
    carrier = min(CARRIER, len(spans) - 1)
    pieces = [
        Piece(at, rows, order, dims, TILE if number == carrier else 0)
        for number, (at, rows, order) in enumerate(spans)
    ]
    cells = node_cell.reshape(slab_cols // LANES, LANES)

    panel = bem_panel.reshape(dims + (chunk_rows, slab_cols))
    early, late = pieces[:EARLY], pieces[EARLY:]
    fields, squares, *far = first_products(early, offset, interiors, cells, incident, panel)
    token = far[0]
    if late:
        more = later_products(late, 0, offset, fields, squares, panel, token)
        far, token = list(far) + list(more), more[0]
    near = later_products(pieces, 1, offset, fields, squares, panel, token)
    token = near[0]
    courses = [
        Course(piece, number, sent, kept)
        for number, (piece, sent, kept) in enumerate(zip(pieces, far, near))
    ]
    steps = sum(len(piece.steps) for piece in pieces)
    arrivals = ARRIVALS if steps == len(ARRIVALS) else list(range(len(pieces))) * steps
    for number in arrivals:
        if courses[number].done is None:
            token = courses[number].arrive(token)
    owned = pl.pallas_call(
        functools.partial(finish_kernel, node_total, carrier, [piece.rows for piece in pieces]),
        in_specs=[IN_VMEM] * len(pieces),
        out_specs=IN_VMEM,
        out_shape=jax.ShapeDtypeStruct((chunk_rows, width), jnp.float32),
        compiler_params=PARAMS,
        name="divide_by_norms",
    )(*[course.done for course in courses])

    current = interior
    for sweep_idx in range(SWEEPS):
        padded = with_halo(current, other if sweep_idx == 0 else None)
        current = sweep_once(pad_x(padded), sources, absorption)
    return (current, owned)


def solution(mesh):
    in_specs = (
        P("slab", "blk", None),
        P("slab", "blk", None),
        P("slab", "blk", None),
        P("blk", "slab"),
        P("slab", None),
        P("slab"),
        P(),
    )
    out_specs = (P("slab", "blk", None), P(("blk", "slab"), None))
    return jax.shard_map(
        per_device, mesh=mesh, in_specs=in_specs, out_specs=out_specs, check_vma=False
    )
```

time: 295 us -> 139 us (0.47)
  waiting for transfers between devices: 166 us -> 51.6 us
  starting transfers between devices: 13.7 us -> 68.3 us
  blocking collectives: 45.2 us -> 0 us
  local copies, waits for them, and re-layouts: 33.9 us -> 0.06 us
  Pallas kernels: 0 us -> 14.1 us
  matrix products: 13.4 us -> 0 us
  between operations: 14.9 us -> 1.84 us
  other arithmetic: 5.85 us -> 2.66 us
    reduce_scatter x1 -> x0, waiting for transfers between devices: 130 us -> none  [per_device(): owned = lax.psum_scatter(summed, 'slab', scatter_dimension=0, tiled=True)]
    ppermute x8 -> x31, starting transfers between devices: 13.7 us -> 68.3 us  [the longest x25 58.3 us: start(): self.got = lax.ppermute(self.sent, 'slab', self.piece.pairs(self.step))]
    psum x1 -> x0, blocking collectives: 43.3 us -> none  [per_device(): squares = lax.psum(jnp.sum(wide * wide, axis=0), 'slab')]
    gather x3 -> x0, local copies, waits for them, and re-layouts: 29.4 us -> none  [the longest x2 25.9 us: per_device(): picked = jnp.take(wide, jnp.clip(node_pos, 0, slab_cols - 1), axis=0)]
    ppermute x8 -> x31, waiting for transfers between devices: 36.2 us -> 51.6 us  [the longest x25 33.2 us: start(): self.got = lax.ppermute(self.sent, 'slab', self.piece.pairs(self.step))]
    pallas_call x0 -> x29, Pallas kernels: none -> 14.1 us  [the longest x2 7.05 us: later_products(): pl.pallas_call(functools.partial(later_kernel, pieces, which), in_specs=[...]
    dot_general x1 -> x0, matrix products: 13.4 us -> none  [per_device(): product = jnp.dot(bem_panel, fields, preferred_element_type=jnp.float32)]
    unnamed x13 -> x6, local copies, waits for them, and re-layouts: 3.16 us -> 0.02 us
  transfers between devices with their start and end apart: 9 -> 31, of which waited for: 5 -> 12; matrix products, arithmetic and copies ran while one was open for 1% -> 2% of each run, Pallas kernels for 0% -> 6%
where the time goes in v2:
time: 139 us
  starting transfers between devices  68.3 us (49%)
  waiting for transfers between devices  51.6 us (37%)
  Pallas kernels  14.1 us (10%)
  other arithmetic  2.66 us (2%)
  between operations  1.84 us (1%)
    ppermute x25, starting transfers between devices, start(): self.got = lax.ppermute(self.sent, 'slab', self.piece.pairs(self.step))  58.3 us
    ppermute x25, waiting for transfers between devices, start(): self.got = lax.ppermute(self.sent, 'slab', self.piece.pairs(self.step))  33.2 us
    ppermute x2, waiting for transfers between devices, with_halo(): below = lax.ppermute(cells[-1:], 'slab', [(i, i + 1) for i in range(ends)])  16.6 us
    pallas_call x2, Pallas kernels, later_products(): pl.pallas_call(functools.partial(later_kernel, pieces, which), in_specs=[...  7.05 us
    ppermute x2, starting transfers between devices, with_halo(): below = lax.ppermute(cells[-1:], 'slab', [(i, i + 1) for i in range(ends)])  6.85 us
    pallas_call x1, Pallas kernels, first_products(): pl.pallas_call(functools.partial(first_kernel, pieces, len(interiors)), i...  4.76 us
  transfers between devices with their start and end apart: 31, of which 12 were waited for; matrix products, arithmetic and copies ran while one was open for 2% of the time, Pallas kernels for 6%

profile of v2, /device:TPU:0, one launch (start us, length us, event | category | flops | bytes accessed | tf_op | source)
XLA Modules:
  0.0 138.6 jit_solution(6550558829537112071)
XLA Ops:
  2.5 4.8 %fields_and_first_rows.1 = (bf16[1024,512]{1,0:T(8,128)(2,1)S(1)}, f32[1,512]{1,0:T(1,128)S(1)}, f32[8,40,512]{2,1,0:T(8,128)S(1)}, f32[8,64,512]{2,1,0:T(8,128)S(1)}, f32[8,64,512]{2,1,0:T(8,128)S(1)}) custom-call(s32[1]{0:T(128)S(6)} %copy.9.offset, f32[2,64,512]{2,1,0:T(8,128)} %refs_0_.1, f32[2,64,512]{2,1,0:T(8,128)S(1)} %collective-permute-done.refs_1_, ...), custom_call_target="tpu_custom_call" | custom-call | flops 1342177280 | bytes 2621440 | tf_op jit(solution)/shard_map/fields_and_first_rows/pallas_call | solution.py:280
  7.3 4.8 %collective-permute-start.6 = (f32[8,40,512]{2,1,0:T(8,128)S(1)}, f32[8,40,512]{2,1,0:T(8,128)S(1)}, u32[]{:S(2)}, u32[]{:S(2)}) collective-permute-start(f32[8,40,512]{2,1,0:T(8,128)S(1)} %get-tuple-element.44.token.base), channel_id=1, source_target_pairs={{0,8},{2,10},{4,12},{6,14},{24,16},{26,18},{28,20},{30,22},{1,9},{... | collective-permute-start | bytes 1966088 | tf_op jit(solution)/shard_map/ppermute | solution.py:341
  12.1 1.6 %collective-permute-start.11 = (f32[8,64,512]{2,1,0:T(8,128)S(1)}, f32[8,64,512]{2,1,0:T(8,128)S(1)}, u32[]{:S(2)}, u32[]{:S(2)}) collective-permute-start(f32[8,64,512]{2,1,0:T(8,128)S(1)} %get-tuple-element.53), channel_id=1, source_target_pairs={{0,4},{2,6},{4,0},{6,2},{8,12},{10,14},{12,8},{14,10},{16,20},{18,... | collective-permute-start | bytes 3145736 | tf_op jit(solution)/shard_map/ppermute | solution.py:341
  13.7 1.5 %collective-permute-start.9 = (f32[8,64,512]{2,1,0:T(8,128)S(1)}, f32[8,64,512]{2,1,0:T(8,128)S(1)}, u32[]{:S(2)}, u32[]{:S(2)}) collective-permute-start(f32[8,64,512]{2,1,0:T(8,128)S(1)} %get-tuple-element.51), channel_id=1, source_target_pairs={{0,2},{2,0},{4,6},{6,4},{8,10},{10,8},{12,14},{14,12},{16,18},{18,... | collective-permute-start | bytes 3145736 | tf_op jit(solution)/shard_map/ppermute | solution.py:341
  15.3 2.5 %collective-permute-start.1 = (f32[1,66,512]{2,1,0:T(8,128)S(1)}, f32[1,66,512]{2,1,0:T(8,128)S(1)}, u32[]{:S(2)}, u32[]{:S(2)}) collective-permute-start(f32[1,66,512]{2,1,0:T(8,128)S(1)} %get-tuple-element.94), channel_id=1, source_target_pairs={{0,2},{2,4},{4,6},{6,8},{8,10},{10,12},{12,14},{14,16},{16,18},{18... | collective-permute-start | bytes 405512 | tf_op jit(solution)/shard_map/ppermute | solution.py:402
  17.8 1.3 collective-permute-start.2
  19.1 2.5 %sent_rows.1 = (f32[8,48,512]{2,1,0:T(8,128)S(1)}, f32[8,48,512]{2,1,0:T(8,128)S(1)}) custom-call(s32[1]{0:T(128)S(6)} %copy.9.offset, bf16[1024,512]{1,0:T(8,128)(2,1)S(1)} %get-tuple-element.45.fields, f32[1,512]{1,0:T(1,128)S(1)} %get-tuple-element.46.squares, bf16[4,2,2,256,1024]{4,3,2,1,0:T(8,128)(2,1)} %bitcast.3, ...), custom_call_target="tpu_custom_call" | custom-call | flops 805306368 | bytes 1572864 | tf_op jit(solution)/shard_map/sent_rows/pallas_call | solution.py:299
  21.5 4.6 %kept_rows.1 = (f32[8,40,512]{2,1,0:T(8,128)S(1)}, f32[8,64,512]{2,1,0:T(8,128)S(1)}, f32[8,64,512]{2,1,0:T(8,128)S(1)}, f32[8,48,512]{2,1,0:T(8,128)S(1)}, f32[8,48,512]{2,1,0:T(8,128)S(1)}) custom-call(s32[1]{0:T(128)S(6)} %copy.9.offset, bf16[1024,512]{1,0:T(8,128)(2,1)S(1)} %get-tuple-element.45.fields, f32[1,512]{1,0:T(1,128)S(1)} %get-tuple-element.46.squares, ...), custom_call_target="tpu_custom_call" | custom-call | flops 2147483648 | bytes 4194304 | tf_op jit(solution)/shard_map/kept_rows/pallas_call | solution.py:299
  27.2 16.6 %collective-permute-done.1 = f32[1,66,512]{2,1,0:T(8,128)S(1)} collective-permute-done((f32[1,66,512]{2,1,0:T(8,128)S(1)}, f32[1,66,512]{2,1,0:T(8,128)S(1)}, u32[]{:S(2)}, u32[]{:S(2)}) %collective-permute-start.1) | collective-permute-done | bytes 135200 | tf_op jit(solution)/shard_map/ppermute | solution.py:402
  43.8 1.6 %collective-permute-start.10 = (f32[8,48,512]{2,1,0:T(8,128)S(1)}, f32[8,48,512]{2,1,0:T(8,128)S(1)}, u32[]{:S(2)}, u32[]{:S(2)}) collective-permute-start(f32[8,48,512]{2,1,0:T(8,128)S(1)} %get-tuple-element.47.token.base), channel_id=1, source_target_pairs={{0,8},{2,10},{4,12},{6,14},{24,16},{26,18},{28,20},{30,22},{1,9},{... | collective-permute-start | bytes 2359304 | tf_op jit(solution)/shard_map/ppermute | solution.py:341
  47.9 1.4 %collective-permute-start.13 = (f32[4,64,512]{2,1,0:T(8,128)S(1)}, f32[4,64,512]{2,1,0:T(8,128)S(1)}, u32[]{:S(2)}, u32[]{:S(2)}) collective-permute-start(f32[4,64,512]{2,1,0:T(8,128)S(1)} %get-tuple-element.55.token), channel_id=1, source_target_pairs={{0,2},{2,0},{4,6},{6,4},{8,10},{10,8},{12,14},{14,12},{16,18},{18,... | collective-permute-start | bytes 1572872 | tf_op jit(solution)/shard_map/ppermute | solution.py:341
  49.3 14.0 %collective-permute-done.10.got = f32[8,48,512]{2,1,0:T(8,128)S(1)} collective-permute-done((f32[8,48,512]{2,1,0:T(8,128)S(1)}, f32[8,48,512]{2,1,0:T(8,128)S(1)}, u32[]{:S(2)}, u32[]{:S(2)}) %collective-permute-start.10) | collective-permute-done | bytes 786464 | tf_op jit(solution)/shard_map/ppermute | solution.py:341
  63.5 4.4 %collective-permute-start.15 = (f32[4,64,512]{2,1,0:T(8,128)S(1)}, f32[4,64,512]{2,1,0:T(8,128)S(1)}, u32[]{:S(2)}, u32[]{:S(2)}) collective-permute-start(f32[4,64,512]{2,1,0:T(8,128)S(1)} %get-tuple-element.56.token.base), channel_id=1, source_target_pairs={{0,8},{2,10},{4,12},{6,14},{24,16},{26,18},{28,20},{30,22},{1,9},{... | collective-permute-start | bytes 1572872 | tf_op jit(solution)/shard_map/ppermute | solution.py:341
  68.0 2.3 %collective-permute-done.8.got = f32[4,40,512]{2,1,0:T(8,128)S(1)} collective-permute-done((f32[4,40,512]{2,1,0:T(8,128)S(1)}, f32[4,40,512]{2,1,0:T(8,128)S(1)}, u32[]{:S(2)}, u32[]{:S(2)}) %collective-permute-start.8) | collective-permute-done | bytes 327712 | tf_op jit(solution)/shard_map/ppermute | solution.py:341
  71.1 2.5 %collective-permute-start.12 = (f32[2,40,512]{2,1,0:T(8,128)S(1)}, f32[2,40,512]{2,1,0:T(8,128)S(1)}, u32[]{:S(2)}, u32[]{:S(2)}) collective-permute-start(f32[2,40,512]{2,1,0:T(8,128)S(1)} %get-tuple-element.57.token), channel_id=1, source_target_pairs={{0,2},{2,0},{4,6},{6,4},{8,10},{10,8},{12,14},{14,12},{16,18},{18,... | collective-permute-start | bytes 491528 | tf_op jit(solution)/shard_map/ppermute | solution.py:341
  73.8 3.2 %collective-permute-done.12.got = f32[2,40,512]{2,1,0:T(8,128)S(1)} collective-permute-done((f32[2,40,512]{2,1,0:T(8,128)S(1)}, f32[2,40,512]{2,1,0:T(8,128)S(1)}, u32[]{:S(2)}, u32[]{:S(2)}) %collective-permute-start.12) | collective-permute-done | bytes 163872 | tf_op jit(solution)/shard_map/ppermute | solution.py:341
  77.1 2.5 %collective-permute-done.15.got = f32[4,64,512]{2,1,0:T(8,128)S(1)} collective-permute-done((f32[4,64,512]{2,1,0:T(8,128)S(1)}, f32[4,64,512]{2,1,0:T(8,128)S(1)}, u32[]{:S(2)}, u32[]{:S(2)}) %collective-permute-start.15) | collective-permute-done | bytes 524320 | tf_op jit(solution)/shard_map/ppermute | solution.py:341
  80.4 4.4 %collective-permute-start.4 = (f32[1,66,512]{2,1,0:T(8,128)S(1)}, f32[1,66,512]{2,1,0:T(8,128)S(1)}, u32[]{:S(2)}, u32[]{:S(2)}) collective-permute-start(f32[1,66,512]{2,1,0:T(8,128)S(1)} %get-tuple-element.92), channel_id=1, source_target_pairs={{0,2},{2,4},{4,6},{6,8},{8,10},{10,12},{12,14},{14,16},{16,18},{18... | collective-permute-start | bytes 405512 | tf_op jit(solution)/shard_map/ppermute | solution.py:402
  84.8 1.3 collective-permute-start.5
  86.1 2.7 %collective-permute-start.20 = (f32[4,48,512]{2,1,0:T(8,128)S(1)}, f32[4,48,512]{2,1,0:T(8,128)S(1)}, u32[]{:S(2)}, u32[]{:S(2)}) collective-permute-start(f32[4,48,512]{2,1,0:T(8,128)S(1)} %get-tuple-element.65.token), channel_id=1, source_target_pairs={{0,2},{2,0},{4,6},{6,4},{8,10},{10,8},{12,14},{14,12},{16,18},{18,... | collective-permute-start | bytes 1179656 | tf_op jit(solution)/shard_map/ppermute | solution.py:341
  88.8 3.5 %collective-permute-start.14 = (f32[1,40,512]{2,1,0:T(8,128)S(1)}, f32[1,40,512]{2,1,0:T(8,128)S(1)}, u32[]{:S(2)}, u32[]{:S(2)}) collective-permute-start(f32[1,40,512]{2,1,0:T(8,128)S(1)} %get-tuple-element.61.token), channel_id=1, source_target_pairs={{0,4},{2,6},{4,0},{6,2},{8,12},{10,14},{12,8},{14,10},{16,20},{18,... | collective-permute-start | bytes 245768 | tf_op jit(solution)/shard_map/ppermute | solution.py:341
  92.3 1.1 collective-permute-done.5
  93.5 7.0 %collective-permute-start.17 = (f32[2,64,512]{2,1,0:T(8,128)S(1)}, f32[2,64,512]{2,1,0:T(8,128)S(1)}, u32[]{:S(2)}, u32[]{:S(2)}) collective-permute-start(f32[2,64,512]{2,1,0:T(8,128)S(1)} %get-tuple-element.60.token.base), channel_id=1, source_target_pairs={{0,8},{2,10},{4,12},{6,14},{24,16},{26,18},{28,20},{30,22},{1,9},{... | collective-permute-start | bytes 786440 | tf_op jit(solution)/shard_map/ppermute | solution.py:341
  101.2 5.3 %collective-permute-done.17.got = f32[2,64,512]{2,1,0:T(8,128)S(1)} collective-permute-done((f32[2,64,512]{2,1,0:T(8,128)S(1)}, f32[2,64,512]{2,1,0:T(8,128)S(1)}, u32[]{:S(2)}, u32[]{:S(2)}) %collective-permute-start.17) | collective-permute-done | bytes 262176 | tf_op jit(solution)/shard_map/ppermute | solution.py:341
  107.3 11.1 %collective-permute-start.21 = (f32[2,48,512]{2,1,0:T(8,128)S(1)}, f32[2,48,512]{2,1,0:T(8,128)S(1)}, u32[]{:S(2)}, u32[]{:S(2)}) collective-permute-start(f32[2,48,512]{2,1,0:T(8,128)S(1)} %get-tuple-element.70.token.base), channel_id=1, source_target_pairs={{0,8},{2,10},{4,12},{6,14},{24,16},{26,18},{28,20},{30,22},{1,9},{... | collective-permute-start | bytes 589832 | tf_op jit(solution)/shard_map/ppermute | solution.py:341
  118.8 2.0 %collective-permute-start.25 = (f32[2,48,512]{2,1,0:T(8,128)S(1)}, f32[2,48,512]{2,1,0:T(8,128)S(1)}, u32[]{:S(2)}, u32[]{:S(2)}) collective-permute-start(f32[2,48,512]{2,1,0:T(8,128)S(1)} %get-tuple-element.74.token), channel_id=1, source_target_pairs={{0,4},{2,6},{4,0},{6,2},{8,12},{10,14},{12,8},{14,10},{16,20},{18,... | collective-permute-start | bytes 589832 | tf_op jit(solution)/shard_map/ppermute | solution.py:341
  120.8 2.2 %collective-permute-done.21.got = f32[2,48,512]{2,1,0:T(8,128)S(1)} collective-permute-done((f32[2,48,512]{2,1,0:T(8,128)S(1)}, f32[2,48,512]{2,1,0:T(8,128)S(1)}, u32[]{:S(2)}, u32[]{:S(2)}) %collective-permute-start.21) | collective-permute-done | bytes 196640 | tf_op jit(solution)/shard_map/ppermute | solution.py:341
  123.9 4.8 %collective-permute-start.24 = (f32[1,64,512]{2,1,0:T(8,128)S(1)}, f32[1,64,512]{2,1,0:T(8,128)S(1)}, u32[]{:S(2)}, u32[]{:S(2)}) collective-permute-start(f32[1,64,512]{2,1,0:T(8,128)S(1)} %get-tuple-element.75.token), channel_id=1, source_target_pairs={{0,8},{2,10},{4,12},{6,14},{8,0},{10,2},{12,4},{14,6},{16,24},{18,... | collective-permute-start | bytes 393224 | tf_op jit(solution)/shard_map/ppermute | solution.py:341
  128.9 4.1 %collective-permute-start.29 = (f32[1,64,512]{2,1,0:T(8,128)S(1)}, f32[1,64,512]{2,1,0:T(8,128)S(1)}, u32[]{:S(2)}, u32[]{:S(2)}) collective-permute-start(f32[1,64,512]{2,1,0:T(8,128)S(1)} %get-tuple-element.82.token), channel_id=1, source_target_pairs={{0,4},{2,6},{4,0},{6,2},{8,12},{10,14},{12,8},{14,10},{16,20},{18,... | collective-permute-start | bytes 393224 | tf_op jit(solution)/shard_map/ppermute | solution.py:341
  133.2 1.0 fusion.12
  134.2 1.7 %collective-permute-done.29.got = f32[1,64,512]{2,1,0:T(8,128)S(1)} collective-permute-done((f32[1,64,512]{2,1,0:T(8,128)S(1)}, f32[1,64,512]{2,1,0:T(8,128)S(1)}, u32[]{:S(2)}, u32[]{:S(2)}) %collective-permute-start.29) | collective-permute-done | bytes 131104 | tf_op jit(solution)/shard_map/ppermute | solution.py:341
  135.9 1.7 %collective-permute-done.30.got = f32[1,48,512]{2,1,0:T(8,128)S(1)} collective-permute-done((f32[1,48,512]{2,1,0:T(8,128)S(1)}, f32[1,48,512]{2,1,0:T(8,128)S(1)}, u32[]{:S(2)}, u32[]{:S(2)}) %collective-permute-start.30) | collective-permute-done | bytes 98336 | tf_op jit(solution)/shard_map/ppermute | solution.py:341
  (82 shorter events, 10.7 us)
Async XLA Ops:
  0.6 1.9 %collective-permute-start = (f32[2,64,512]{2,1,0:T(8,128)}, f32[2,64,512]{2,1,0:T(8,128)S(1)}, u32[]{:S(2)}, u32[]{:S(2)}) collective-permute-start(f32[2,64,512]{2,1,0:T(8,128)} %refs_0_.1), channel_id=1, source_target_pairs={{0,1},{1,0},{2,3},{3,2},{4,5},{5,4},{6,7},{7,6},{8,9},{9,8},{10,11... | collective-permute-start | bytes 786440 | tf_op jit(solution)/shard_map/ppermute | solution.py:447
  7.3 19.1 %collective-permute-start.6 = (f32[8,40,512]{2,1,0:T(8,128)S(1)}, f32[8,40,512]{2,1,0:T(8,128)S(1)}, u32[]{:S(2)}, u32[]{:S(2)}) collective-permute-start(f32[8,40,512]{2,1,0:T(8,128)S(1)} %get-tuple-element.44.token.base), channel_id=1, source_target_pairs={{0,8},{2,10},{4,12},{6,14},{24,16},{26,18},{28,20},{30,22},{1,9},{... | collective-permute-start | bytes 1966088 | tf_op jit(solution)/shard_map/ppermute | solution.py:341
  12.1 35.6 %collective-permute-start.11 = (f32[8,64,512]{2,1,0:T(8,128)S(1)}, f32[8,64,512]{2,1,0:T(8,128)S(1)}, u32[]{:S(2)}, u32[]{:S(2)}) collective-permute-start(f32[8,64,512]{2,1,0:T(8,128)S(1)} %get-tuple-element.53), channel_id=1, source_target_pairs={{0,4},{2,6},{4,0},{6,2},{8,12},{10,14},{12,8},{14,10},{16,20},{18,... | collective-permute-start | bytes 3145736 | tf_op jit(solution)/shard_map/ppermute | solution.py:341
  13.7 49.6 %collective-permute-start.9 = (f32[8,64,512]{2,1,0:T(8,128)S(1)}, f32[8,64,512]{2,1,0:T(8,128)S(1)}, u32[]{:S(2)}, u32[]{:S(2)}) collective-permute-start(f32[8,64,512]{2,1,0:T(8,128)S(1)} %get-tuple-element.51), channel_id=1, source_target_pairs={{0,2},{2,0},{4,6},{6,4},{8,10},{10,8},{12,14},{14,12},{16,18},{18,... | collective-permute-start | bytes 3145736 | tf_op jit(solution)/shard_map/ppermute | solution.py:341
  15.3 28.5 %collective-permute-start.1 = (f32[1,66,512]{2,1,0:T(8,128)S(1)}, f32[1,66,512]{2,1,0:T(8,128)S(1)}, u32[]{:S(2)}, u32[]{:S(2)}) collective-permute-start(f32[1,66,512]{2,1,0:T(8,128)S(1)} %get-tuple-element.94), channel_id=1, source_target_pairs={{0,2},{2,4},{4,6},{6,8},{8,10},{10,12},{12,14},{14,16},{16,18},{18... | collective-permute-start | bytes 405512 | tf_op jit(solution)/shard_map/ppermute | solution.py:402
  17.8 27.6 %collective-permute-start.2 = (f32[1,66,512]{2,1,0:T(8,128)S(1)}, f32[1,66,512]{2,1,0:T(8,128)S(1)}, u32[]{:S(2)}, u32[]{:S(2)}) collective-permute-start(f32[1,66,512]{2,1,0:T(8,128)S(1)} %get-tuple-element.95), channel_id=1, source_target_pairs={{2,0},{4,2},{6,4},{8,6},{10,8},{12,10},{14,12},{16,14},{18,16},{20... | collective-permute-start | bytes 405512 | tf_op jit(solution)/shard_map/ppermute | solution.py:403
  26.1 21.3 %copy-start.1 = (f32[2,64,512]{2,1,0:T(8,128)S(1)}, f32[2,64,512]{2,1,0:T(8,128)}, u32[]{:S(2)}) copy-start(f32[2,64,512]{2,1,0:T(8,128)} %param.8) | copy-start | bytes 786436
  26.5 20.0 %collective-permute-start.7 = (f32[8,40,512]{2,1,0:T(8,128)S(1)}, f32[8,40,512]{2,1,0:T(8,128)S(1)}, u32[]{:S(2)}, u32[]{:S(2)}) collective-permute-start(f32[8,40,512]{2,1,0:T(8,128)S(1)} %arrival_0_0.1.token), channel_id=1, source_target_pairs={{8,16},{10,18},{12,20},{14,22},{16,8},{18,10},{20,12},{22,14},{9,1... | collective-permute-start | bytes 1966088 | tf_op jit(solution)/shard_map/ppermute | solution.py:341
  43.8 19.5 %collective-permute-start.10 = (f32[8,48,512]{2,1,0:T(8,128)S(1)}, f32[8,48,512]{2,1,0:T(8,128)S(1)}, u32[]{:S(2)}, u32[]{:S(2)}) collective-permute-start(f32[8,48,512]{2,1,0:T(8,128)S(1)} %get-tuple-element.47.token.base), channel_id=1, source_target_pairs={{0,8},{2,10},{4,12},{6,14},{24,16},{26,18},{28,20},{30,22},{1,9},{... | collective-permute-start | bytes 2359304 | tf_op jit(solution)/shard_map/ppermute | solution.py:341
  45.4 31.6 %collective-permute-start.16 = (f32[8,48,512]{2,1,0:T(8,128)S(1)}, f32[8,48,512]{2,1,0:T(8,128)S(1)}, u32[]{:S(2)}, u32[]{:S(2)}) collective-permute-start(f32[8,48,512]{2,1,0:T(8,128)S(1)} %get-tuple-element.63), channel_id=1, source_target_pairs={{0,4},{2,6},{4,0},{6,2},{8,12},{10,14},{12,8},{14,10},{16,20},{18,... | collective-permute-start | bytes 2359304 | tf_op jit(solution)/shard_map/ppermute | solution.py:341
  46.6 23.7 %collective-permute-start.8 = (f32[4,40,512]{2,1,0:T(8,128)S(1)}, f32[4,40,512]{2,1,0:T(8,128)S(1)}, u32[]{:S(2)}, u32[]{:S(2)}) collective-permute-start(f32[4,40,512]{2,1,0:T(8,128)S(1)} %get-tuple-element.49.token), channel_id=1, source_target_pairs={{0,8},{2,10},{4,12},{6,14},{8,0},{10,2},{12,4},{14,6},{16,24},{18,... | collective-permute-start | bytes 983048 | tf_op jit(solution)/shard_map/ppermute | solution.py:341
  47.9 25.8 %collective-permute-start.13 = (f32[4,64,512]{2,1,0:T(8,128)S(1)}, f32[4,64,512]{2,1,0:T(8,128)S(1)}, u32[]{:S(2)}, u32[]{:S(2)}) collective-permute-start(f32[4,64,512]{2,1,0:T(8,128)S(1)} %get-tuple-element.55.token), channel_id=1, source_target_pairs={{0,2},{2,0},{4,6},{6,4},{8,10},{10,8},{12,14},{14,12},{16,18},{18,... | collective-permute-start | bytes 1572872 | tf_op jit(solution)/shard_map/ppermute | solution.py:341
  63.5 16.1 %collective-permute-start.15 = (f32[4,64,512]{2,1,0:T(8,128)S(1)}, f32[4,64,512]{2,1,0:T(8,128)S(1)}, u32[]{:S(2)}, u32[]{:S(2)}) collective-permute-start(f32[4,64,512]{2,1,0:T(8,128)S(1)} %get-tuple-element.56.token.base), channel_id=1, source_target_pairs={{0,8},{2,10},{4,12},{6,14},{24,16},{26,18},{28,20},{30,22},{1,9},{... | collective-permute-start | bytes 1572872 | tf_op jit(solution)/shard_map/ppermute | solution.py:341
  68.0 3.1 %collective-permute-start.3 = (f32[2,1,512]{2,1,0:T(1,128)S(1)}, f32[2,1,512]{2,1,0:T(1,128)S(1)}, u32[]{:S(2)}, u32[]{:S(2)}) collective-permute-start(f32[2,1,512]{2,1,0:T(1,128)S(1)} %broadcast_select_fusion.2), channel_id=1, source_target_pairs={{0,1},{1,0},{2,3},{3,2},{4,5},{5,4},{6,7},{7,6},{8,9},{9,8},{10,11... | collective-permute-start | bytes 12296 | tf_op jit(solution)/shard_map/ppermute | solution.py:387
  70.3 30.3 %collective-permute-start.18 = (f32[8,48,512]{2,1,0:T(8,128)S(1)}, f32[8,48,512]{2,1,0:T(8,128)S(1)}, u32[]{:S(2)}, u32[]{:S(2)}) collective-permute-start(f32[8,48,512]{2,1,0:T(8,128)S(1)} %arrival_3_0.1.token), channel_id=1, source_target_pairs={{8,16},{10,18},{12,20},{14,22},{16,8},{18,10},{20,12},{22,14},{9,1... | collective-permute-start | bytes 2359304 | tf_op jit(solution)/shard_map/ppermute | solution.py:341
  71.1 5.8 %collective-permute-start.12 = (f32[2,40,512]{2,1,0:T(8,128)S(1)}, f32[2,40,512]{2,1,0:T(8,128)S(1)}, u32[]{:S(2)}, u32[]{:S(2)}) collective-permute-start(f32[2,40,512]{2,1,0:T(8,128)S(1)} %get-tuple-element.57.token), channel_id=1, source_target_pairs={{0,2},{2,0},{4,6},{6,4},{8,10},{10,8},{12,14},{14,12},{16,18},{18,... | collective-permute-start | bytes 491528 | tf_op jit(solution)/shard_map/ppermute | solution.py:341
  79.7 38.8 %collective-permute-start.23 = (f32[4,64,512]{2,1,0:T(8,128)S(1)}, f32[4,64,512]{2,1,0:T(8,128)S(1)}, u32[]{:S(2)}, u32[]{:S(2)}) collective-permute-start(f32[4,64,512]{2,1,0:T(8,128)S(1)} %arrival_2_1.1.token), channel_id=1, source_target_pairs={{8,16},{10,18},{12,20},{14,22},{16,8},{18,10},{20,12},{22,14},{9,1... | collective-permute-start | bytes 1572872 | tf_op jit(solution)/shard_map/ppermute | solution.py:341
  80.4 8.4 %collective-permute-start.4 = (f32[1,66,512]{2,1,0:T(8,128)S(1)}, f32[1,66,512]{2,1,0:T(8,128)S(1)}, u32[]{:S(2)}, u32[]{:S(2)}) collective-permute-start(f32[1,66,512]{2,1,0:T(8,128)S(1)} %get-tuple-element.92), channel_id=1, source_target_pairs={{0,2},{2,4},{4,6},{6,8},{8,10},{10,12},{12,14},{14,16},{16,18},{18... | collective-permute-start | bytes 405512 | tf_op jit(solution)/shard_map/ppermute | solution.py:402
  84.8 8.7 %collective-permute-start.5 = (f32[1,66,512]{2,1,0:T(8,128)S(1)}, f32[1,66,512]{2,1,0:T(8,128)S(1)}, u32[]{:S(2)}, u32[]{:S(2)}) collective-permute-start(f32[1,66,512]{2,1,0:T(8,128)S(1)} %get-tuple-element.93), channel_id=1, source_target_pairs={{2,0},{4,2},{6,4},{8,6},{10,8},{12,10},{14,12},{16,14},{18,16},{20... | collective-permute-start | bytes 405512 | tf_op jit(solution)/shard_map/ppermute | solution.py:403
  86.1 21.1 %collective-permute-start.20 = (f32[4,48,512]{2,1,0:T(8,128)S(1)}, f32[4,48,512]{2,1,0:T(8,128)S(1)}, u32[]{:S(2)}, u32[]{:S(2)}) collective-permute-start(f32[4,48,512]{2,1,0:T(8,128)S(1)} %get-tuple-element.65.token), channel_id=1, source_target_pairs={{0,2},{2,0},{4,6},{6,4},{8,10},{10,8},{12,14},{14,12},{16,18},{18,... | collective-permute-start | bytes 1179656 | tf_op jit(solution)/shard_map/ppermute | solution.py:341
  88.8 11.8 %collective-permute-start.14 = (f32[1,40,512]{2,1,0:T(8,128)S(1)}, f32[1,40,512]{2,1,0:T(8,128)S(1)}, u32[]{:S(2)}, u32[]{:S(2)}) collective-permute-start(f32[1,40,512]{2,1,0:T(8,128)S(1)} %get-tuple-element.61.token), channel_id=1, source_target_pairs={{0,4},{2,6},{4,0},{6,2},{8,12},{10,14},{12,8},{14,10},{16,20},{18,... | collective-permute-start | bytes 245768 | tf_op jit(solution)/shard_map/ppermute | solution.py:341
  93.5 13.0 %collective-permute-start.17 = (f32[2,64,512]{2,1,0:T(8,128)S(1)}, f32[2,64,512]{2,1,0:T(8,128)S(1)}, u32[]{:S(2)}, u32[]{:S(2)}) collective-permute-start(f32[2,64,512]{2,1,0:T(8,128)S(1)} %get-tuple-element.60.token.base), channel_id=1, source_target_pairs={{0,8},{2,10},{4,12},{6,14},{24,16},{26,18},{28,20},{30,22},{1,9},{... | collective-permute-start | bytes 786440 | tf_op jit(solution)/shard_map/ppermute | solution.py:341
  100.7 18.0 %collective-permute-start.22 = (f32[4,48,512]{2,1,0:T(8,128)S(1)}, f32[4,48,512]{2,1,0:T(8,128)S(1)}, u32[]{:S(2)}, u32[]{:S(2)}) collective-permute-start(f32[4,48,512]{2,1,0:T(8,128)S(1)} %get-tuple-element.67.token), channel_id=1, source_target_pairs={{0,8},{2,10},{4,12},{6,14},{8,0},{10,2},{12,4},{14,6},{16,24},{18,... | collective-permute-start | bytes 1179656 | tf_op jit(solution)/shard_map/ppermute | solution.py:341
  106.5 17.3 %collective-permute-start.19 = (f32[2,64,512]{2,1,0:T(8,128)S(1)}, f32[2,64,512]{2,1,0:T(8,128)S(1)}, u32[]{:S(2)}, u32[]{:S(2)}) collective-permute-start(f32[2,64,512]{2,1,0:T(8,128)S(1)} %arrival_1_2.1.token), channel_id=1, source_target_pairs={{8,16},{10,18},{12,20},{14,22},{16,8},{18,10},{20,12},{22,14},{9,1... | collective-permute-start | bytes 786440 | tf_op jit(solution)/shard_map/ppermute | solution.py:341
  107.3 15.7 %collective-permute-start.21 = (f32[2,48,512]{2,1,0:T(8,128)S(1)}, f32[2,48,512]{2,1,0:T(8,128)S(1)}, u32[]{:S(2)}, u32[]{:S(2)}) collective-permute-start(f32[2,48,512]{2,1,0:T(8,128)S(1)} %get-tuple-element.70.token.base), channel_id=1, source_target_pairs={{0,8},{2,10},{4,12},{6,14},{24,16},{26,18},{28,20},{30,22},{1,9},{... | collective-permute-start | bytes 589832 | tf_op jit(solution)/shard_map/ppermute | solution.py:341
  118.5 10.3 %collective-permute-start.28 = (f32[2,64,512]{2,1,0:T(8,128)S(1)}, f32[2,64,512]{2,1,0:T(8,128)S(1)}, u32[]{:S(2)}, u32[]{:S(2)}) collective-permute-start(f32[2,64,512]{2,1,0:T(8,128)S(1)} %get-tuple-element.73.token), channel_id=1, source_target_pairs={{0,8},{2,10},{4,12},{6,14},{8,0},{10,2},{12,4},{14,6},{16,24},{18,... | collective-permute-start | bytes 786440 | tf_op jit(solution)/shard_map/ppermute | solution.py:341
  118.8 9.9 %collective-permute-start.25 = (f32[2,48,512]{2,1,0:T(8,128)S(1)}, f32[2,48,512]{2,1,0:T(8,128)S(1)}, u32[]{:S(2)}, u32[]{:S(2)}) collective-permute-start(f32[2,48,512]{2,1,0:T(8,128)S(1)} %get-tuple-element.74.token), channel_id=1, source_target_pairs={{0,4},{2,6},{4,0},{6,2},{8,12},{10,14},{12,8},{14,10},{16,20},{18,... | collective-permute-start | bytes 589832 | tf_op jit(solution)/shard_map/ppermute | solution.py:341
  123.0 10.0 %collective-permute-start.27 = (f32[2,48,512]{2,1,0:T(8,128)S(1)}, f32[2,48,512]{2,1,0:T(8,128)S(1)}, u32[]{:S(2)}, u32[]{:S(2)}) collective-permute-start(f32[2,48,512]{2,1,0:T(8,128)S(1)} %arrival_4_2.1.token), channel_id=1, source_target_pairs={{8,16},{10,18},{12,20},{14,22},{16,8},{18,10},{20,12},{22,14},{9,1... | collective-permute-start | bytes 589832 | tf_op jit(solution)/shard_map/ppermute | solution.py:341
  123.9 10.3 %collective-permute-start.24 = (f32[1,64,512]{2,1,0:T(8,128)S(1)}, f32[1,64,512]{2,1,0:T(8,128)S(1)}, u32[]{:S(2)}, u32[]{:S(2)}) collective-permute-start(f32[1,64,512]{2,1,0:T(8,128)S(1)} %get-tuple-element.75.token), channel_id=1, source_target_pairs={{0,8},{2,10},{4,12},{6,14},{8,0},{10,2},{12,4},{14,6},{16,24},{18,... | collective-permute-start | bytes 393224 | tf_op jit(solution)/shard_map/ppermute | solution.py:341
  128.7 5.4 %collective-permute-start.26 = (f32[1,48,512]{2,1,0:T(8,128)S(1)}, f32[1,48,512]{2,1,0:T(8,128)S(1)}, u32[]{:S(2)}, u32[]{:S(2)}) collective-permute-start(f32[1,48,512]{2,1,0:T(8,128)S(1)} %get-tuple-element.78.token), channel_id=1, source_target_pairs={{0,2},{2,0},{4,6},{6,4},{8,10},{10,8},{12,14},{14,12},{16,18},{18,... | collective-permute-start | bytes 294920 | tf_op jit(solution)/shard_map/ppermute | solution.py:341
  128.9 7.0 %collective-permute-start.29 = (f32[1,64,512]{2,1,0:T(8,128)S(1)}, f32[1,64,512]{2,1,0:T(8,128)S(1)}, u32[]{:S(2)}, u32[]{:S(2)}) collective-permute-start(f32[1,64,512]{2,1,0:T(8,128)S(1)} %get-tuple-element.82.token), channel_id=1, source_target_pairs={{0,4},{2,6},{4,0},{6,2},{8,12},{10,14},{12,8},{14,10},{16,20},{18,... | collective-permute-start | bytes 393224 | tf_op jit(solution)/shard_map/ppermute | solution.py:341
  133.0 4.7 %collective-permute-start.30 = (f32[1,48,512]{2,1,0:T(8,128)S(1)}, f32[1,48,512]{2,1,0:T(8,128)S(1)}, u32[]{:S(2)}, u32[]{:S(2)}) collective-permute-start(f32[1,48,512]{2,1,0:T(8,128)S(1)} %get-tuple-element.83.token), channel_id=1, source_target_pairs={{0,8},{2,10},{4,12},{6,14},{8,0},{10,2},{12,4},{14,6},{16,24},{18,... | collective-permute-start | bytes 294920 | tf_op jit(solution)/shard_map/ppermute | solution.py:341
  (2 other events, 35.9 us)

commit v3 on v0

v3 whole, which is shorter than its diff:
```python
import functools

import jax
import jax.numpy as jnp
from jax import lax
from jax.experimental import pallas as pl
from jax.experimental.pallas import tpu as pltpu
from jax.sharding import PartitionSpec as P

SWEEPS = 2

omega = 0.6
center_weight = 8.0 / 3.0
LANES = 128
ROW_UNIT = 16
TILE = 8
LIMIT = 24 * 2**20

PIECES = ((4, (0, 1, 3, 2)), (4, (1, 0, 2, 3)), (6, (2, 1, 0, 3)), (2, (0, 2, 1, 3)))
EARLY = 3
CARRIER = 1
EVENTS = "abFN0d132031023103c212"


def bit_of(slab, bit):
    return (slab >> bit) & 1


class Piece:
    def __init__(self, first, rows, order, extra):
        self.first, self.rows, self.order, self.extra = first, rows, order, extra
        self.bits = len(order)

    def height(self):
        return self.rows + self.extra

    def halves(self, step, slab):
        left = [bit for bit in range(self.bits) if bit not in self.order[:step]]
        inner = 1 << left.index(self.order[step])
        outer = (1 << len(left)) // (2 * inner)
        own = bit_of(slab, self.order[step])
        return [
            [i * (2 * inner) + half * inner + j for i in range(outer) for j in range(inner)]
            for half in (1 - own, own)
        ]

    def window(self, which, slab):
        index = [slice(None)] * self.bits
        own = bit_of(slab, self.order[0])
        index[self.bits - 1 - self.order[0]] = own if which else 1 - own
        return tuple(index) + (pl.ds(self.first, self.rows), slice(None))

    def window_shape(self):
        return (2,) * (self.bits - 1) + (self.rows,)

    def pairs(self, step):
        return [(i, i ^ (1 << self.order[step])) for i in range(1 << self.bits)]


def panel_copies(jobs, panel, panel_bufs, sems):
    slab = lax.axis_index("slab")
    started = []
    for number, (piece, which) in enumerate(jobs):
        copy = pltpu.make_async_copy(
            panel.at[piece.window(which, slab)], panel_bufs[number], sems.at[number]
        )
        copy.start()
        started.append((piece, piece.halves(0, slab)[which], copy, panel_bufs[number]))
    return started


def multiply(jobs, shift, chunk_rows, fields, squares, outs):
    node_count, width = fields.shape
    for (piece, chunks, copy, panel_buf), out in zip(jobs, outs):
        copy.wait()
        rows = piece.rows
        lhs = panel_buf[...].reshape(len(chunks) * rows, node_count)
        product = jnp.dot(lhs, fields[...], preferred_element_type=jnp.float32)
        for block, chunk in enumerate(chunks):
            out[block, 0:rows, :] = product[block * rows : (block + 1) * rows]
            node = shift + chunk * chunk_rows

            @pl.when((node >= 0) & (node < node_count))
            def _(block=block, node=node):
                at = pl.multiple_of(node + piece.first, ROW_UNIT)
                jump = fields[pl.ds(at, rows), :].astype(jnp.float32)
                out[block, 0:rows, :] += 0.5 * jump

            if piece.extra:
                row = lax.broadcasted_iota(jnp.int32, (TILE, width), 0)
                out[block, rows : rows + TILE, :] = jnp.where(row == 0, squares[...], 0.0)


def make_fields(blk, interiors, cells, incident, fields, squares):
    tables = []
    for block in interiors:
        depth_z, depth_y, width = block.shape
        flat_left = block[:, :, :LANES].reshape(depth_z * depth_y, LANES)
        flat_right = block[:, :, width - LANES :].reshape(depth_z * depth_y, LANES)
        tables.append((flat_left.T[0:1, :], flat_right.T[LANES - 1 : LANES, :]))
    node_count = incident.shape[0]
    per_block = node_count // (2 if len(interiors) == 2 else len(interiors))
    across = cells[...].T
    lane = lax.broadcasted_iota(jnp.int32, (LANES, tables[0][0].shape[1]), 1)
    total = jnp.zeros((8, incident.shape[1]), jnp.float32)
    for part in range(node_count // LANES):
        owner = part * LANES // per_block
        if len(interiors) == 2:
            mine = blk == owner
            left = jnp.where(mine, tables[0][0], tables[1][0])
            right = jnp.where(mine, tables[0][1], tables[1][1])
        else:
            left, right = tables[owner]
        cell = across[:, part : part + 1]
        column = cell >> 1
        value = jnp.where((cell & 1) == 1, right, left)
        trace = jnp.sum(jnp.where(lane == column, value, 0.0), axis=1, keepdims=True)
        rows = pl.ds(part * LANES, LANES)
        field = (incident[rows, :].astype(jnp.float32) + trace).astype(jnp.bfloat16)
        fields[rows, :] = field
        wide = field.astype(jnp.float32)
        total = total + jnp.sum((wide * wide).reshape(LANES // 8, 8, wide.shape[1]), axis=0)
    squares[...] = jnp.sum(total, axis=0, keepdims=True)


def shift_of(offset, panel_rows, node_count):
    return (
        offset[0] + lax.axis_index("blk") * panel_rows - lax.axis_index("slab") * node_count
    )


def first_kernel(jobs, blocks, offset, *refs):
    interiors, refs = refs[:blocks], refs[blocks:]
    cells, incident, panel, fields, squares = refs[:5]
    count = len(jobs)
    outs, refs = refs[5 : 5 + count], refs[5 + count :]
    panel_bufs, refs = refs[:count], refs[count:]
    cells_buf, incident_buf, sems, in_sems = refs
    copies = []
    for number, (source, target) in enumerate(((cells, cells_buf), (incident, incident_buf))):
        copy = pltpu.make_async_copy(source, target, in_sems.at[number])
        copy.start()
        copies.append(copy)
    started = panel_copies(jobs, panel, panel_bufs, sems)
    for copy in copies:
        copy.wait()
    make_fields(lax.axis_index("blk"), interiors, cells_buf, incident_buf, fields, squares)
    chunk_rows = panel.shape[-2]
    shift = shift_of(offset, chunk_rows * lax.axis_size("slab"), incident.shape[0])
    multiply(started, shift, chunk_rows, fields, squares, outs)


def later_kernel(jobs, offset, fields, squares, panel, token, *refs):
    count = len(jobs)
    outs, panel_bufs = refs[:count], refs[count : 2 * count]
    sems = refs[2 * count]
    started = panel_copies(jobs, panel, panel_bufs, sems)
    chunk_rows = panel.shape[-2]
    shift = shift_of(offset, chunk_rows * lax.axis_size("slab"), fields.shape[0])
    multiply(started, shift, chunk_rows, fields, squares, outs)


def piece_scratch(jobs, depth):
    return [
        pltpu.VMEM(piece.window_shape() + (depth,), jnp.bfloat16) for piece, _ in jobs
    ], pltpu.SemaphoreType.DMA((len(jobs),))


def piece_shapes(jobs, width):
    return [
        pltpu.VMEM((len(piece.halves(0, 0)[0]), piece.height(), width), jnp.float32) for piece, _ in jobs
    ]


COST = pl.CostEstimate(flops=1, bytes_accessed=1, transcendentals=0)

IN_HBM = pl.BlockSpec(memory_space=pltpu.HBM)
ANYWHERE = pl.BlockSpec(memory_space=pl.ANY)
IN_VMEM = pl.BlockSpec(memory_space=pltpu.VMEM)
IN_SMEM = pl.BlockSpec(memory_space=pltpu.SMEM)
PARAMS = pltpu.CompilerParams(vmem_limit_bytes=LIMIT)


def in_hbm(array):
    return pltpu.with_memory_space_constraint(array, pltpu.HBM)


def first_products(jobs, offset, interiors, cells, incident, panel):
    depth, width = incident.shape
    bufs, sems = piece_scratch(jobs, depth)
    return pl.pallas_call(
        functools.partial(first_kernel, jobs, len(interiors)),
        in_specs=[IN_SMEM] + [IN_VMEM] * len(interiors) + [IN_HBM] * 3,
        out_specs=[IN_VMEM] * (2 + len(jobs)),
        out_shape=[pltpu.VMEM(incident.shape, jnp.bfloat16), pltpu.VMEM((1, width), jnp.float32)]
        + piece_shapes(jobs, width),
        scratch_shapes=bufs
        + [pltpu.VMEM(array.shape, array.dtype) for array in (cells, incident)]
        + [sems, pltpu.SemaphoreType.DMA((2,))],
        compiler_params=PARAMS,
        cost_estimate=COST,
        name="fields_and_first_rows",
    )(offset, *interiors, in_hbm(cells), in_hbm(incident), in_hbm(panel))


def later_products(jobs, offset, fields, squares, panel, token):
    depth, width = fields.shape
    bufs, sems = piece_scratch(jobs, depth)
    return pl.pallas_call(
        functools.partial(later_kernel, jobs),
        in_specs=[IN_SMEM, IN_VMEM, IN_VMEM, IN_HBM, ANYWHERE],
        out_specs=[IN_VMEM] * len(jobs),
        out_shape=piece_shapes(jobs, width),
        scratch_shapes=bufs + [sems],
        compiler_params=PARAMS,
        cost_estimate=COST,
        name="other_rows",
    )(offset, fields, squares, in_hbm(panel), token)


def arrival_kernel(piece, step, got, base, token, *outs):
    halves = [[0]] if step == piece.bits else piece.halves(step, lax.axis_index("slab"))
    for blocks, out in zip(halves, outs):
        for number, block in enumerate(blocks):
            out[number] = got[block] + base[block]


def add_arrival(piece, step, got, base, token, name):
    count = 1 if step == piece.bits else 2
    shape = pltpu.VMEM((max(1, base.shape[0] // 2),) + base.shape[1:], jnp.float32)
    return pl.pallas_call(
        functools.partial(arrival_kernel, piece, step),
        in_specs=[IN_VMEM, IN_VMEM, ANYWHERE],
        out_specs=[IN_VMEM] * count,
        out_shape=[shape] * count,
        compiler_params=PARAMS,
        cost_estimate=COST,
        name=name,
    )(got, base, token)


class Course:
    def __init__(self, piece, number, far):
        self.piece, self.number = piece, number
        self.step, self.near, self.done = 0, None, None
        self.send(far)

    def send(self, rows):
        self.got = lax.ppermute(rows, "slab", self.piece.pairs(self.step))

    def arrive(self, kept, token):
        base = kept if self.step == 0 else self.near
        self.step += 1
        name = f"arrival_{self.number}_{self.step}"
        outs = add_arrival(self.piece, self.step, self.got, base, token, name)
        if self.step == self.piece.bits:
            self.done = outs[0]
        else:
            self.near = outs[1]
            self.send(outs[0])
        return outs[0]


def finish_kernel(node_total, carrier, rows, *refs):
    parts, out = refs[:-1], refs[-1]
    squares = parts[carrier][0, rows[carrier] : rows[carrier] + 1, :]
    norms = jnp.sqrt(squares / node_total + 1e-06)
    first = 0
    for part, height in zip(parts, rows):
        out[first : first + height, :] = part[0, :height, :] / norms
        first += height


def ordered_kernel(count, *refs):
    for source, target in zip(refs[:count], refs[count + 1 :]):
        target[...] = source[...]


def ordered(arrays, token):
    return pl.pallas_call(
        functools.partial(ordered_kernel, len(arrays)),
        in_specs=[IN_VMEM] * len(arrays) + [ANYWHERE],
        out_specs=[IN_VMEM] * len(arrays),
        out_shape=[pltpu.VMEM(array.shape, array.dtype) for array in arrays],
        compiler_params=PARAMS,
        cost_estimate=COST,
        name="ordered",
    )(*arrays, token)


def edge_kernel(cells, before, after, *outs):
    depth, rows = cells.shape[:2]
    odd = bit_of(lax.axis_index("slab"), 0)
    for layer, lowest in zip(outs, (odd, 1 - odd)):
        at = (1 - lowest) * (depth - 1)
        layer[0, 0:rows, :] = cells[at]
        layer[0, rows : rows + 1, :] = before[at]
        layer[0, rows + 1 : rows + 2, :] = after[at]


def edge_layers(cells, before, after, token):
    shape = pltpu.VMEM((1, cells.shape[1] + 2, cells.shape[2]), jnp.float32)
    return pl.pallas_call(
        lambda cells, before, after, token, *outs: edge_kernel(cells, before, after, *outs),
        in_specs=[IN_VMEM] * 3 + [ANYWHERE],
        out_specs=[IN_VMEM] * 2,
        out_shape=[shape, shape],
        compiler_params=PARAMS,
        cost_estimate=COST,
        name="edge_layers",
    )(cells, before, after, token)


class Interior:
    def __init__(self, interior, other, sources, absorption):
        self.cells, self.sources, self.absorption = interior, sources, absorption
        self.swap = lax.axis_size("blk") == 2
        if self.swap:
            self.take_rows(jnp.where(self.first(), other[:, :1], other[:, -1:]))
        else:
            self.send_rows()
            self.take_rows(*self.rows)

    def first(self):
        return lax.axis_index("blk") == 0

    def send_rows(self):
        head, tail = self.cells[:, :1], self.cells[:, -1:]
        if self.swap:
            rows = jnp.where(self.first(), tail, head)
            self.rows = [lax.ppermute(rows, "blk", [(0, 1), (1, 0)])]
        else:
            ends = lax.axis_size("blk") - 1
            self.rows = [
                lax.ppermute(tail, "blk", [(i, i + 1) for i in range(ends)]),
                lax.ppermute(head, "blk", [(i + 1, i) for i in range(ends)]),
            ]

    def take_rows(self, *rows):
        if self.swap:
            first = self.first()
            rows = [jnp.where(first, 0.0, rows[0]), jnp.where(first, rows[0], 0.0)]
        self.before, self.after = rows

    def make_layers(self, token):
        self.edges = edge_layers(self.cells, self.before, self.after, token)
        self.layers = []
        return self.edges[0]

    def send_layer(self, number):
        count = lax.axis_size("slab")
        pairs = []
        for low in range(number, count - 1, 2):
            pairs += [(low, low + 1), (low + 1, low)]
        self.layers.append(lax.ppermute(self.edges[number], "slab", pairs))

    def take_layers(self, token):
        layers = ordered(self.layers, token)
        odd = bit_of(lax.axis_index("slab"), 0) == 1
        below, above = jnp.where(odd, layers[0], layers[1]), jnp.where(odd, layers[1], layers[0])
        rows = self.cells.shape[1]
        cells = jnp.concatenate([below[:, :rows], self.cells, above[:, :rows]], axis=0)
        before = jnp.concatenate([below[:, rows : rows + 1], self.before, above[:, rows : rows + 1]], axis=0)
        after = jnp.concatenate([below[:, rows + 1 :], self.after, above[:, rows + 1 :]], axis=0)
        padded = jnp.concatenate([before, cells, after], axis=1)
        self.cells = sweep_once(pad_x(padded), self.sources, self.absorption)
        return layers[0]


def stiffness(padded):
    along_x = padded[:, :, :-2] + padded[:, :, 2:]
    middle = padded[:, :, 1:-1]
    plus_mid = along_x + middle
    plane_sum = plus_mid[:, :-2] + plus_mid[:, 1:-1] + plus_mid[:, 2:]
    total_sum = plane_sum[:-2] + plane_sum[1:-1] + plane_sum[2:]
    cross_xy = along_x[:, :-2] + along_x[:, 2:]
    corner_sum = cross_xy[:-2] + cross_xy[2:]
    face_sum = (
        along_x[1:-1, 1:-1]
        + middle[1:-1, :-2]
        + middle[1:-1, 2:]
        + middle[:-2, 1:-1]
        + middle[2:, 1:-1]
    )
    center = middle[1:-1, 1:-1]
    edge_sum = total_sum - center - face_sum - corner_sum
    return center_weight * center - edge_sum / 6.0 - corner_sum / 12.0


def sweep_once(padded, sources, absorption):
    center = padded[1:-1, 1:-1, 1:-1]
    applied = stiffness(padded) + absorption * center
    return center + omega * (sources - applied) / (center_weight + absorption)


def pad_x(values):
    return jnp.pad(values, ((0, 0), (0, 0), (1, 1)))


def per_device(interior, sources, absorption, bem_panel, incident, node_cell, offset):
    slab_count = lax.axis_size("slab")
    blk_count = lax.axis_size("blk")
    slab_cols, width = incident.shape
    panel_rows = bem_panel.shape[0]
    node_total = slab_cols * slab_count
    chunk_rows = panel_rows // slab_count
    bits = slab_count.bit_length() - 1

    if blk_count == 2:
        other = lax.ppermute(interior, "blk", [(0, 1), (1, 0)])
        interiors = [interior, other]
    else:
        other = None
        gathered = lax.all_gather(interior, "blk", axis=0)
        interiors = [gathered[i] for i in range(blk_count)]

    units, first, done = chunk_rows // ROW_UNIT, 0, 0
    spans = []
    for share, order in PIECES:
        done += share
        last = (units * done // 16) * ROW_UNIT
        if last > first:
            if bits != len(order):
                order = [(bit + len(spans)) % bits for bit in range(bits)]
            spans.append((first, last - first, order))
        first = last
    carrier = min(CARRIER, len(spans) - 1)
    pieces = [
        Piece(at, rows, order, TILE if number == carrier else 0)
        for number, (at, rows, order) in enumerate(spans)
    ]
    cells = node_cell.reshape(slab_cols // LANES, LANES)

    panel = bem_panel.reshape((2,) * bits + (chunk_rows, slab_cols))
    inside = Interior(interior, other, sources, absorption)
    inside.make_layers(offset)
    inside.send_layer(0)
    inside.send_layer(1)
    fields, squares, *far = first_products(
        [(piece, 0) for piece in pieces[:EARLY]], offset, interiors, cells, incident, panel
    )
    courses = [Course(piece, number, sent) for number, (piece, sent) in enumerate(zip(pieces, far))]
    token = far[0]
    events = EVENTS
    if len(pieces) * bits != sum(event.isdigit() for event in EVENTS):
        events = "F" * (len(pieces) - EARLY) + "Nabdc" + "".join(str(number) for number in range(len(pieces))) * bits
    for event in events:
        if event == "F":
            number = len(courses)
            token = later_products([(pieces[number], 0)], offset, fields, squares, panel, token)[0]
            courses.append(Course(pieces[number], number, token))
        elif event == "N":
            near = later_products([(piece, 1) for piece in pieces], offset, fields, squares, panel, token)
            token = near[0]
        elif event == "a":
            token = inside.take_layers(token)
            inside.send_rows()
        elif event == "b":
            inside.take_rows(*ordered(inside.rows, token))
            token = inside.make_layers(token)
            inside.send_layer(0)
        elif event == "d":
            inside.layers = list(ordered(inside.layers, token))
            inside.edges = ordered(inside.edges, inside.layers[0])
            inside.send_layer(1)
            token = inside.edges[0]
        elif event == "c":
            token = inside.take_layers(token)
        elif event.isdigit() and courses[int(event)].done is None:
            token = courses[int(event)].arrive(near[int(event)], token)
    owned = pl.pallas_call(
        functools.partial(finish_kernel, node_total, carrier, [piece.rows for piece in pieces]),
        in_specs=[IN_VMEM] * len(pieces),
        out_specs=IN_VMEM,
        out_shape=jax.ShapeDtypeStruct((chunk_rows, width), jnp.float32),
        compiler_params=PARAMS,
        cost_estimate=COST,
        name="divide_by_norms",
    )(*[course.done for course in courses])

    return (inside.cells, owned)


def solution(mesh):
    in_specs = (
        P("slab", "blk", None),
        P("slab", "blk", None),
        P("slab", "blk", None),
        P("blk", "slab"),
        P("slab", None),
        P("slab"),
        P(),
    )
    out_specs = (P("slab", "blk", None), P(("blk", "slab"), None))
    return jax.shard_map(
        per_device, mesh=mesh, in_specs=in_specs, out_specs=out_specs, check_vma=False
    )
```

time: 295 us -> 102 us (0.35)
  waiting for transfers between devices: 166 us -> 48.9 us
  blocking collectives: 45.2 us -> 0 us
  local copies, waits for them, and re-layouts: 33.9 us -> 2.78 us
  starting transfers between devices: 13.7 us -> 32.8 us
  matrix products: 13.4 us -> 0 us
  Pallas kernels: 0 us -> 13.3 us
  between operations: 14.9 us -> 1.69 us
  other arithmetic: 5.85 us -> 2.69 us
    reduce_scatter x1 -> x0, waiting for transfers between devices: 130 us -> none  [per_device(): owned = lax.psum_scatter(summed, 'slab', scatter_dimension=0, tiled=True)]
    psum x1 -> x0, blocking collectives: 43.3 us -> none  [per_device(): squares = lax.psum(jnp.sum(wide * wide, axis=0), 'slab')]
    gather x3 -> x0, local copies, waits for them, and re-layouts: 29.4 us -> none  [the longest x2 25.9 us: per_device(): picked = jnp.take(wide, jnp.clip(node_pos, 0, slab_cols - 1), axis=0)]
    ppermute x8 -> x22, starting transfers between devices: 13.7 us -> 32.8 us  [the longest x16 26.1 us: send(): self.got = lax.ppermute(rows, 'slab', self.piece.pairs(self.step))]
    dot_general x1 -> x0, matrix products: 13.4 us -> none  [per_device(): product = jnp.dot(bem_panel, fields, preferred_element_type=jnp.float32)]
    pallas_call x0 -> x27, Pallas kernels: none -> 13.3 us  [the longest x2 6.1 us: later_products(): pl.pallas_call(functools.partial(later_kernel, jobs), in_specs=[IN_SMEM,...]
    ppermute x8 -> x22, waiting for transfers between devices: 36.2 us -> 48.9 us  [the longest x16 35.6 us: send(): self.got = lax.ppermute(rows, 'slab', self.piece.pairs(self.step))]
  transfers between devices with their start and end apart: 9 -> 22, of which waited for: 5 -> 11; matrix products, arithmetic and copies ran while one was open for 1% -> 2% of each run, Pallas kernels for 0% -> 12%
where the time goes in v3:
time: 102 us
  waiting for transfers between devices  48.9 us (48%)
  starting transfers between devices  32.8 us (32%)
  Pallas kernels  13.3 us (13%)
  local copies, waits for them, and re-layouts  2.78 us (3%)
  other arithmetic  2.69 us (3%)
  between operations  1.69 us (2%)
    ppermute x16, waiting for transfers between devices, send(): self.got = lax.ppermute(rows, 'slab', self.piece.pairs(self.step))  35.6 us
    ppermute x16, starting transfers between devices, send(): self.got = lax.ppermute(rows, 'slab', self.piece.pairs(self.step))  26.1 us
    ppermute x4, waiting for transfers between devices, send_layer(): self.layers.append(lax.ppermute(self.edges[number], 'slab', pairs))  11.4 us
    ppermute x4, starting transfers between devices, send_layer(): self.layers.append(lax.ppermute(self.edges[number], 'slab', pairs))  6.19 us
    pallas_call x2, Pallas kernels, later_products(): pl.pallas_call(functools.partial(later_kernel, jobs), in_specs=[IN_SMEM,...  6.1 us
    pallas_call x1, Pallas kernels, first_products(): pl.pallas_call(functools.partial(first_kernel, jobs, len(interiors)), in_...  5.27 us
    unnamed x10, local copies, waits for them, and re-layouts  2.72 us
  transfers between devices with their start and end apart: 22, of which 11 were waited for; matrix products, arithmetic and copies ran while one was open for 2% of the time, Pallas kernels for 12%

profile of v3, /device:TPU:0, one launch (start us, length us, event | category | flops | bytes accessed | tf_op | source)
XLA Modules:
  0.0 102.1 jit_solution(12161731424967300099)
XLA Ops:
  1.8 0.7 collective-permute-done.refs_1_
  2.6 0.9 copy-done
  3.5 2.9 %collective-permute-start.1 = (f32[1,66,512]{2,1,0:T(8,128)S(1)}, f32[1,66,512]{2,1,0:T(8,128)S(1)}, u32[]{:S(2)}, u32[]{:S(2)}) collective-permute-start(f32[1,66,512]{2,1,0:T(8,128)S(1)} %get-tuple-element.45), channel_id=1, source_target_pairs={{0,2},{2,0},{4,6},{6,4},{8,10},{10,8},{12,14},{14,12},{16,18},{18,... | collective-permute-start | bytes 405512 | tf_op jit(solution)/shard_map/ppermute | solution.py:355
  7.1 0.9 copy-done.1
  8.1 5.3 %fields_and_first_rows.1 = (bf16[1024,512]{1,0:T(8,128)(2,1)S(1)}, f32[1,512]{1,0:T(1,128)S(1)}, f32[8,64,512]{2,1,0:T(8,128)S(1)}, f32[8,72,512]{2,1,0:T(8,128)S(1)}, f32[8,96,512]{2,1,0:T(8,128)S(1)}) custom-call(s32[1]{0:T(128)S(6)} %copy.9.token.offset, f32[2,64,512]{2,1,0:T(8,128)S(1)} %copy-done.1, f32[2,64,512]{2,1,0:T(8,128)S(1)} %collective-permute-done.refs_1_, ...), custom_call_target="tpu_custom_call" | custom-call | flops 1 | bytes 1 | tf_op jit(solution)/shard_map/fields_and_first_rows/pallas_call | solution.py:191
  13.4 4.4 %collective-permute-start.5 = (f32[8,64,512]{2,1,0:T(8,128)S(1)}, f32[8,64,512]{2,1,0:T(8,128)S(1)}, u32[]{:S(2)}, u32[]{:S(2)}) collective-permute-start(f32[8,64,512]{2,1,0:T(8,128)S(1)} %get-tuple-element.47.refs_2_), channel_id=1, source_target_pairs={{0,2},{2,0},{4,6},{6,4},{8,10},{10,8},{12,14},{14,12},{16,18},{18,... | collective-permute-start | bytes 3145736 | tf_op jit(solution)/shard_map/ppermute | solution.py:249
  17.7 1.5 %collective-permute-start.8 = (f32[8,72,512]{2,1,0:T(8,128)S(1)}, f32[8,72,512]{2,1,0:T(8,128)S(1)}, u32[]{:S(2)}, u32[]{:S(2)}) collective-permute-start(f32[8,72,512]{2,1,0:T(8,128)S(1)} %get-tuple-element.58), channel_id=1, source_target_pairs={{0,4},{2,6},{4,0},{6,2},{8,12},{10,14},{12,8},{14,10},{16,20},{18,... | collective-permute-start | bytes 3538952 | tf_op jit(solution)/shard_map/ppermute | solution.py:249
  19.2 1.5 %collective-permute-start.11 = (f32[8,96,512]{2,1,0:T(8,128)S(1)}, f32[8,96,512]{2,1,0:T(8,128)S(1)}, u32[]{:S(2)}, u32[]{:S(2)}) collective-permute-start(f32[8,96,512]{2,1,0:T(8,128)S(1)} %get-tuple-element.65), channel_id=1, source_target_pairs={{0,8},{2,10},{4,12},{6,14},{8,0},{10,2},{12,4},{14,6},{16,24},{18,... | collective-permute-start | bytes 4718600 | tf_op jit(solution)/shard_map/ppermute | solution.py:249
  21.5 0.7 copy-done.3
  22.7 1.2 %collective-permute-done.3.refs_0_ = f32[2,1,512]{2,1,0:T(1,128)S(1)} collective-permute-done((f32[2,1,512]{2,1,0:T(1,128)S(1)}, f32[2,1,512]{2,1,0:T(1,128)S(1)}, u32[]{:S(2)}, u32[]{:S(2)}) %collective-permute-start.3) | collective-permute-done | bytes 4128 | tf_op jit(solution)/shard_map/ppermute | solution.py:331
  23.9 1.6 %other_rows.2.token = f32[8,32,512]{2,1,0:T(8,128)S(1)} custom-call(s32[1]{0:T(128)S(6)} %copy.9.token.offset, bf16[1024,512]{1,0:T(8,128)(2,1)S(1)} %get-tuple-element.51.fields, f32[1,512]{1,0:T(1,128)S(1)} %get-tuple-element.52.squares, bf16[2,2,2,2,256,1024]{5,4,3,2,1,0:T(8,128)(2,1)} %bitcast.3, f32[1,66,512]{2,1,0:T(8,128)S(1)} %get-tuple-element.50.token.refs_0_), custom_call_target="tpu_custom_call" | custom-call | flops 1 | bytes 1 | tf_op jit(solution)/shard_map/other_rows/pallas_call | solution.py:209
  25.7 1.9 %collective-permute-start.4 = (f32[1,66,512]{2,1,0:T(8,128)S(1)}, f32[1,66,512]{2,1,0:T(8,128)S(1)}, u32[]{:S(2)}, u32[]{:S(2)}) collective-permute-start(f32[1,66,512]{2,1,0:T(8,128)S(1)} %get-tuple-element.50.token.refs_0_), channel_id=1, source_target_pairs={{0,2},{2,0},{4,6},{6,4},{8,10},{10,8},{12,14},{14,12},{16,18},{18,... | collective-permute-start | bytes 405512 | tf_op jit(solution)/shard_map/ppermute | solution.py:355
  27.6 4.5 %other_rows.3 = (f32[8,64,512]{2,1,0:T(8,128)S(1)}, f32[8,72,512]{2,1,0:T(8,128)S(1)}, f32[8,96,512]{2,1,0:T(8,128)S(1)}, f32[8,32,512]{2,1,0:T(8,128)S(1)}) custom-call(s32[1]{0:T(128)S(6)} %copy.9.token.offset, bf16[1024,512]{1,0:T(8,128)(2,1)S(1)} %get-tuple-element.51.fields, f32[1,512]{1,0:T(1,128)S(1)} %get-tuple-element.52.squares, ...), custom_call_target="tpu_custom_call" | custom-call | flops 1 | bytes 1 | tf_op jit(solution)/shard_map/other_rows/pallas_call | solution.py:209
  32.2 9.6 %collective-permute-done.5.got = f32[8,64,512]{2,1,0:T(8,128)S(1)} collective-permute-done((f32[8,64,512]{2,1,0:T(8,128)S(1)}, f32[8,64,512]{2,1,0:T(8,128)S(1)}, u32[]{:S(2)}, u32[]{:S(2)}) %collective-permute-start.5) | collective-permute-done | bytes 1048608 | tf_op jit(solution)/shard_map/ppermute | solution.py:249
  41.9 1.6 %collective-permute-start.10 = (f32[4,64,512]{2,1,0:T(8,128)S(1)}, f32[4,64,512]{2,1,0:T(8,128)S(1)}, u32[]{:S(2)}, u32[]{:S(2)}) collective-permute-start(f32[4,64,512]{2,1,0:T(8,128)S(1)} %get-tuple-element.54.refs_1_), channel_id=1, source_target_pairs={{0,4},{2,6},{4,0},{6,2},{8,12},{10,14},{12,8},{14,10},{16,20},{18,... | collective-permute-start | bytes 1572872 | tf_op jit(solution)/shard_map/ppermute | solution.py:249
  43.5 11.4 %collective-permute-done.4.refs_0_ = f32[1,66,512]{2,1,0:T(8,128)S(1)} collective-permute-done((f32[1,66,512]{2,1,0:T(8,128)S(1)}, f32[1,66,512]{2,1,0:T(8,128)S(1)}, u32[]{:S(2)}, u32[]{:S(2)}) %collective-permute-start.4) | collective-permute-done | bytes 135200 | tf_op jit(solution)/shard_map/ppermute | solution.py:355
  55.1 1.8 %collective-permute-start.15 = (f32[4,72,512]{2,1,0:T(8,128)S(1)}, f32[4,72,512]{2,1,0:T(8,128)S(1)}, u32[]{:S(2)}, u32[]{:S(2)}) collective-permute-start(f32[4,72,512]{2,1,0:T(8,128)S(1)} %get-tuple-element.61.token), channel_id=1, source_target_pairs={{0,2},{2,0},{4,6},{6,4},{8,10},{10,8},{12,14},{14,12},{16,18},{18,... | collective-permute-start | bytes 1769480 | tf_op jit(solution)/shard_map/ppermute | solution.py:249
  57.2 1.6 %collective-permute-start.13 = (f32[4,96,512]{2,1,0:T(8,128)S(1)}, f32[4,96,512]{2,1,0:T(8,128)S(1)}, u32[]{:S(2)}, u32[]{:S(2)}) collective-permute-start(f32[4,96,512]{2,1,0:T(8,128)S(1)} %get-tuple-element.67.token), channel_id=1, source_target_pairs={{0,4},{2,6},{4,0},{6,2},{8,12},{10,14},{12,8},{14,10},{16,20},{18,... | collective-permute-start | bytes 2359304 | tf_op jit(solution)/shard_map/ppermute | solution.py:249
  58.7 1.6 %collective-permute-start.9 = (f32[4,32,512]{2,1,0:T(8,128)S(1)}, f32[4,32,512]{2,1,0:T(8,128)S(1)}, u32[]{:S(2)}, u32[]{:S(2)}) collective-permute-start(f32[4,32,512]{2,1,0:T(8,128)S(1)} %get-tuple-element.62.token), channel_id=1, source_target_pairs={{0,8},{2,10},{4,12},{6,14},{8,0},{10,2},{12,4},{14,6},{16,24},{18,... | collective-permute-start | bytes 786440 | tf_op jit(solution)/shard_map/ppermute | solution.py:249
  60.4 1.2 %collective-permute-start.14 = (f32[2,64,512]{2,1,0:T(8,128)S(1)}, f32[2,64,512]{2,1,0:T(8,128)S(1)}, u32[]{:S(2)}, u32[]{:S(2)}) collective-permute-start(f32[2,64,512]{2,1,0:T(8,128)S(1)} %get-tuple-element.68.token), channel_id=1, source_target_pairs={{0,16},{2,18},{4,20},{6,22},{8,24},{10,26},{12,28},{14,30},{16,0},... | collective-permute-start | bytes 786440 | tf_op jit(solution)/shard_map/ppermute | solution.py:249
  61.6 8.8 %collective-permute-done.9.got = f32[4,32,512]{2,1,0:T(8,128)S(1)} collective-permute-done((f32[4,32,512]{2,1,0:T(8,128)S(1)}, f32[4,32,512]{2,1,0:T(8,128)S(1)}, u32[]{:S(2)}, u32[]{:S(2)}) %collective-permute-start.9) | collective-permute-done | bytes 262176 | tf_op jit(solution)/shard_map/ppermute | solution.py:249
  70.5 0.7 collective-permute-start.18
  71.2 1.5 %collective-permute-start.12 = (f32[2,32,512]{2,1,0:T(8,128)S(1)}, f32[2,32,512]{2,1,0:T(8,128)S(1)}, u32[]{:S(2)}, u32[]{:S(2)}) collective-permute-start(f32[2,32,512]{2,1,0:T(8,128)S(1)} %get-tuple-element.69.token), channel_id=1, source_target_pairs={{0,4},{2,6},{4,0},{6,2},{8,12},{10,14},{12,8},{14,10},{16,20},{18,... | collective-permute-start | bytes 393224 | tf_op jit(solution)/shard_map/ppermute | solution.py:249
  73.4 4.1 %collective-permute-start.17 = (f32[1,64,512]{2,1,0:T(8,128)S(1)}, f32[1,64,512]{2,1,0:T(8,128)S(1)}, u32[]{:S(2)}, u32[]{:S(2)}) collective-permute-start(f32[1,64,512]{2,1,0:T(8,128)S(1)} %get-tuple-element.75.token), channel_id=1, source_target_pairs={{0,8},{2,10},{4,12},{6,14},{8,0},{10,2},{12,4},{14,6},{16,24},{18,... | collective-permute-start | bytes 393224 | tf_op jit(solution)/shard_map/ppermute | solution.py:249
  77.6 2.3 %collective-permute-done.12.got = f32[2,32,512]{2,1,0:T(8,128)S(1)} collective-permute-done((f32[2,32,512]{2,1,0:T(8,128)S(1)}, f32[2,32,512]{2,1,0:T(8,128)S(1)}, u32[]{:S(2)}, u32[]{:S(2)}) %collective-permute-start.12) | collective-permute-done | bytes 131104 | tf_op jit(solution)/shard_map/ppermute | solution.py:249
  79.9 3.7 %collective-permute-start.16 = (f32[1,32,512]{2,1,0:T(8,128)S(1)}, f32[1,32,512]{2,1,0:T(8,128)S(1)}, u32[]{:S(2)}, u32[]{:S(2)}) collective-permute-start(f32[1,32,512]{2,1,0:T(8,128)S(1)} %get-tuple-element.77.token), channel_id=1, source_target_pairs={{0,16},{2,18},{4,20},{6,22},{8,24},{10,26},{12,28},{14,30},{16,0},... | collective-permute-start | bytes 196616 | tf_op jit(solution)/shard_map/ppermute | solution.py:249
  84.3 1.6 %collective-permute-done.17.got = f32[1,64,512]{2,1,0:T(8,128)S(1)} collective-permute-done((f32[1,64,512]{2,1,0:T(8,128)S(1)}, f32[1,64,512]{2,1,0:T(8,128)S(1)}, u32[]{:S(2)}, u32[]{:S(2)}) %collective-permute-start.17) | collective-permute-done | bytes 131104 | tf_op jit(solution)/shard_map/ppermute | solution.py:249
  87.3 4.1 %collective-permute-done.20.got = f32[2,96,512]{2,1,0:T(8,128)S(1)} collective-permute-done((f32[2,96,512]{2,1,0:T(8,128)S(1)}, f32[2,96,512]{2,1,0:T(8,128)S(1)}, u32[]{:S(2)}, u32[]{:S(2)}) %collective-permute-start.20) | collective-permute-done | bytes 393248 | tf_op jit(solution)/shard_map/ppermute | solution.py:249
  91.7 3.7 %collective-permute-done.19.got = f32[1,72,512]{2,1,0:T(8,128)S(1)} collective-permute-done((f32[1,72,512]{2,1,0:T(8,128)S(1)}, f32[1,72,512]{2,1,0:T(8,128)S(1)}, u32[]{:S(2)}, u32[]{:S(2)}) %collective-permute-start.19) | collective-permute-done | bytes 147488 | tf_op jit(solution)/shard_map/ppermute | solution.py:249
  95.4 4.9 %collective-permute-done.21.got = f32[1,96,512]{2,1,0:T(8,128)S(1)} collective-permute-done((f32[1,96,512]{2,1,0:T(8,128)S(1)}, f32[1,96,512]{2,1,0:T(8,128)S(1)}, u32[]{:S(2)}, u32[]{:S(2)}) %collective-permute-start.21) | collective-permute-done | bytes 196640 | tf_op jit(solution)/shard_map/ppermute | solution.py:249
  100.3 1.0 fusion.12
  101.3 0.8 divide_by_norms.1
  (72 shorter events, 6.4 us)
Async XLA Ops:
  0.6 1.9 %collective-permute-start = (f32[2,64,512]{2,1,0:T(8,128)}, f32[2,64,512]{2,1,0:T(8,128)S(1)}, u32[]{:S(2)}, u32[]{:S(2)}) collective-permute-start(f32[2,64,512]{2,1,0:T(8,128)} %refs_0_.1), channel_id=1, source_target_pairs={{0,1},{1,0},{2,3},{3,2},{4,5},{5,4},{6,7},{7,6},{8,9},{9,8},{10,11... | collective-permute-start | bytes 786440 | tf_op jit(solution)/shard_map/ppermute | solution.py:410
  2.5 1.0 copy-start
  3.5 17.2 %collective-permute-start.1 = (f32[1,66,512]{2,1,0:T(8,128)S(1)}, f32[1,66,512]{2,1,0:T(8,128)S(1)}, u32[]{:S(2)}, u32[]{:S(2)}) collective-permute-start(f32[1,66,512]{2,1,0:T(8,128)S(1)} %get-tuple-element.45), channel_id=1, source_target_pairs={{0,2},{2,0},{4,6},{6,4},{8,10},{10,8},{12,14},{14,12},{16,18},{18,... | collective-permute-start | bytes 405512 | tf_op jit(solution)/shard_map/ppermute | solution.py:355
  6.5 14.3 %collective-permute-start.2 = (f32[1,66,512]{2,1,0:T(8,128)S(1)}, f32[1,66,512]{2,1,0:T(8,128)S(1)}, u32[]{:S(2)}, u32[]{:S(2)}) collective-permute-start(f32[1,66,512]{2,1,0:T(8,128)S(1)} %get-tuple-element.46), channel_id=1, source_target_pairs={{2,4},{4,2},{6,8},{8,6},{10,12},{12,10},{14,16},{16,14},{18,20},{2... | collective-permute-start | bytes 405512 | tf_op jit(solution)/shard_map/ppermute | solution.py:355
  7.1 1.0 copy-start.1
  13.4 7.5 %copy-start.2 = (f32[2,64,512]{2,1,0:T(8,128)S(1)}, f32[2,64,512]{2,1,0:T(8,128)}, u32[]{:S(2)}) copy-start(f32[2,64,512]{2,1,0:T(8,128)} %refs_0_.1) | copy-start | bytes 786436
  13.4 28.4 %collective-permute-start.5 = (f32[8,64,512]{2,1,0:T(8,128)S(1)}, f32[8,64,512]{2,1,0:T(8,128)S(1)}, u32[]{:S(2)}, u32[]{:S(2)}) collective-permute-start(f32[8,64,512]{2,1,0:T(8,128)S(1)} %get-tuple-element.47.refs_2_), channel_id=1, source_target_pairs={{0,2},{2,0},{4,6},{6,4},{8,10},{10,8},{12,14},{14,12},{16,18},{18,... | collective-permute-start | bytes 3145736 | tf_op jit(solution)/shard_map/ppermute | solution.py:249
  17.7 37.2 %collective-permute-start.8 = (f32[8,72,512]{2,1,0:T(8,128)S(1)}, f32[8,72,512]{2,1,0:T(8,128)S(1)}, u32[]{:S(2)}, u32[]{:S(2)}) collective-permute-start(f32[8,72,512]{2,1,0:T(8,128)S(1)} %get-tuple-element.58), channel_id=1, source_target_pairs={{0,4},{2,6},{4,0},{6,2},{8,12},{10,14},{12,8},{14,10},{16,20},{18,... | collective-permute-start | bytes 3538952 | tf_op jit(solution)/shard_map/ppermute | solution.py:249
  19.2 37.7 %collective-permute-start.11 = (f32[8,96,512]{2,1,0:T(8,128)S(1)}, f32[8,96,512]{2,1,0:T(8,128)S(1)}, u32[]{:S(2)}, u32[]{:S(2)}) collective-permute-start(f32[8,96,512]{2,1,0:T(8,128)S(1)} %get-tuple-element.65), channel_id=1, source_target_pairs={{0,8},{2,10},{4,12},{6,14},{8,0},{10,2},{12,4},{14,6},{16,24},{18,... | collective-permute-start | bytes 4718600 | tf_op jit(solution)/shard_map/ppermute | solution.py:249
  21.3 1.0 copy-start.3
  21.3 1.0 %copy-start.4 = (f32[2,64,512]{2,1,0:T(8,128)S(1)}, f32[2,64,512]{2,1,0:T(8,128)}, u32[]{:S(2)}) copy-start(f32[2,64,512]{2,1,0:T(8,128)} %param.9) | copy-start | bytes 786436
  22.7 1.2 %collective-permute-start.3 = (f32[2,1,512]{2,1,0:T(1,128)S(1)}, f32[2,1,512]{2,1,0:T(1,128)S(1)}, u32[]{:S(2)}, u32[]{:S(2)}) collective-permute-start(f32[2,1,512]{2,1,0:T(1,128)S(1)} %broadcast_select_fusion.6), channel_id=1, source_target_pairs={{0,1},{1,0},{2,3},{3,2},{4,5},{5,4},{6,7},{7,6},{8,9},{9,8},{10,11... | collective-permute-start | bytes 12296 | tf_op jit(solution)/shard_map/ppermute | solution.py:331
  25.5 31.4 %collective-permute-start.7 = (f32[8,32,512]{2,1,0:T(8,128)S(1)}, f32[8,32,512]{2,1,0:T(8,128)S(1)}, u32[]{:S(2)}, u32[]{:S(2)}) collective-permute-start(f32[8,32,512]{2,1,0:T(8,128)S(1)} %other_rows.2.token), channel_id=1, source_target_pairs={{0,2},{2,0},{4,6},{6,4},{8,10},{10,8},{12,14},{14,12},{16,18},{18,... | collective-permute-start | bytes 1572872 | tf_op jit(solution)/shard_map/ppermute | solution.py:249
  25.7 29.2 %collective-permute-start.4 = (f32[1,66,512]{2,1,0:T(8,128)S(1)}, f32[1,66,512]{2,1,0:T(8,128)S(1)}, u32[]{:S(2)}, u32[]{:S(2)}) collective-permute-start(f32[1,66,512]{2,1,0:T(8,128)S(1)} %get-tuple-element.50.token.refs_0_), channel_id=1, source_target_pairs={{0,2},{2,0},{4,6},{6,4},{8,10},{10,8},{12,14},{14,12},{16,18},{18,... | collective-permute-start | bytes 405512 | tf_op jit(solution)/shard_map/ppermute | solution.py:355
  41.9 18.5 %collective-permute-start.10 = (f32[4,64,512]{2,1,0:T(8,128)S(1)}, f32[4,64,512]{2,1,0:T(8,128)S(1)}, u32[]{:S(2)}, u32[]{:S(2)}) collective-permute-start(f32[4,64,512]{2,1,0:T(8,128)S(1)} %get-tuple-element.54.refs_1_), channel_id=1, source_target_pairs={{0,4},{2,6},{4,0},{6,2},{8,12},{10,14},{12,8},{14,10},{16,20},{18,... | collective-permute-start | bytes 1572872 | tf_op jit(solution)/shard_map/ppermute | solution.py:249
  55.1 15.3 %collective-permute-start.15 = (f32[4,72,512]{2,1,0:T(8,128)S(1)}, f32[4,72,512]{2,1,0:T(8,128)S(1)}, u32[]{:S(2)}, u32[]{:S(2)}) collective-permute-start(f32[4,72,512]{2,1,0:T(8,128)S(1)} %get-tuple-element.61.token), channel_id=1, source_target_pairs={{0,2},{2,0},{4,6},{6,4},{8,10},{10,8},{12,14},{14,12},{16,18},{18,... | collective-permute-start | bytes 1769480 | tf_op jit(solution)/shard_map/ppermute | solution.py:249
  57.2 20.4 %collective-permute-start.13 = (f32[4,96,512]{2,1,0:T(8,128)S(1)}, f32[4,96,512]{2,1,0:T(8,128)S(1)}, u32[]{:S(2)}, u32[]{:S(2)}) collective-permute-start(f32[4,96,512]{2,1,0:T(8,128)S(1)} %get-tuple-element.67.token), channel_id=1, source_target_pairs={{0,4},{2,6},{4,0},{6,2},{8,12},{10,14},{12,8},{14,10},{16,20},{18,... | collective-permute-start | bytes 2359304 | tf_op jit(solution)/shard_map/ppermute | solution.py:249
  58.7 11.6 %collective-permute-start.9 = (f32[4,32,512]{2,1,0:T(8,128)S(1)}, f32[4,32,512]{2,1,0:T(8,128)S(1)}, u32[]{:S(2)}, u32[]{:S(2)}) collective-permute-start(f32[4,32,512]{2,1,0:T(8,128)S(1)} %get-tuple-element.62.token), channel_id=1, source_target_pairs={{0,8},{2,10},{4,12},{6,14},{8,0},{10,2},{12,4},{14,6},{16,24},{18,... | collective-permute-start | bytes 786440 | tf_op jit(solution)/shard_map/ppermute | solution.py:249
  60.4 13.0 %collective-permute-start.14 = (f32[2,64,512]{2,1,0:T(8,128)S(1)}, f32[2,64,512]{2,1,0:T(8,128)S(1)}, u32[]{:S(2)}, u32[]{:S(2)}) collective-permute-start(f32[2,64,512]{2,1,0:T(8,128)S(1)} %get-tuple-element.68.token), channel_id=1, source_target_pairs={{0,16},{2,18},{4,20},{6,22},{8,24},{10,26},{12,28},{14,30},{16,0},... | collective-permute-start | bytes 786440 | tf_op jit(solution)/shard_map/ppermute | solution.py:249
  70.5 13.6 %collective-permute-start.18 = (f32[2,72,512]{2,1,0:T(8,128)S(1)}, f32[2,72,512]{2,1,0:T(8,128)S(1)}, u32[]{:S(2)}, u32[]{:S(2)}) collective-permute-start(f32[2,72,512]{2,1,0:T(8,128)S(1)} %get-tuple-element.74.token), channel_id=1, source_target_pairs={{0,8},{2,10},{4,12},{6,14},{8,0},{10,2},{12,4},{14,6},{16,24},{18,... | collective-permute-start | bytes 884744 | tf_op jit(solution)/shard_map/ppermute | solution.py:249
  71.2 8.7 %collective-permute-start.12 = (f32[2,32,512]{2,1,0:T(8,128)S(1)}, f32[2,32,512]{2,1,0:T(8,128)S(1)}, u32[]{:S(2)}, u32[]{:S(2)}) collective-permute-start(f32[2,32,512]{2,1,0:T(8,128)S(1)} %get-tuple-element.69.token), channel_id=1, source_target_pairs={{0,4},{2,6},{4,0},{6,2},{8,12},{10,14},{12,8},{14,10},{16,20},{18,... | collective-permute-start | bytes 393224 | tf_op jit(solution)/shard_map/ppermute | solution.py:249
  72.7 13.9 %collective-permute-start.6 = (f32[1,66,512]{2,1,0:T(8,128)S(1)}, f32[1,66,512]{2,1,0:T(8,128)S(1)}, u32[]{:S(2)}, u32[]{:S(2)}) collective-permute-start(f32[1,66,512]{2,1,0:T(8,128)S(1)} %get-tuple-element.56), channel_id=1, source_target_pairs={{2,4},{4,2},{6,8},{8,6},{10,12},{12,10},{14,16},{16,14},{18,20},{2... | collective-permute-start | bytes 405512 | tf_op jit(solution)/shard_map/ppermute | solution.py:355
  73.4 12.4 %collective-permute-start.17 = (f32[1,64,512]{2,1,0:T(8,128)S(1)}, f32[1,64,512]{2,1,0:T(8,128)S(1)}, u32[]{:S(2)}, u32[]{:S(2)}) collective-permute-start(f32[1,64,512]{2,1,0:T(8,128)S(1)} %get-tuple-element.75.token), channel_id=1, source_target_pairs={{0,8},{2,10},{4,12},{6,14},{8,0},{10,2},{12,4},{14,6},{16,24},{18,... | collective-permute-start | bytes 393224 | tf_op jit(solution)/shard_map/ppermute | solution.py:249
  79.9 6.6 %collective-permute-start.16 = (f32[1,32,512]{2,1,0:T(8,128)S(1)}, f32[1,32,512]{2,1,0:T(8,128)S(1)}, u32[]{:S(2)}, u32[]{:S(2)}) collective-permute-start(f32[1,32,512]{2,1,0:T(8,128)S(1)} %get-tuple-element.77.token), channel_id=1, source_target_pairs={{0,16},{2,18},{4,20},{6,22},{8,24},{10,26},{12,28},{14,30},{16,0},... | collective-permute-start | bytes 196616 | tf_op jit(solution)/shard_map/ppermute | solution.py:249
  83.6 7.8 %collective-permute-start.20 = (f32[2,96,512]{2,1,0:T(8,128)S(1)}, f32[2,96,512]{2,1,0:T(8,128)S(1)}, u32[]{:S(2)}, u32[]{:S(2)}) collective-permute-start(f32[2,96,512]{2,1,0:T(8,128)S(1)} %get-tuple-element.76.token), channel_id=1, source_target_pairs={{0,2},{2,0},{4,6},{6,4},{8,10},{10,8},{12,14},{14,12},{16,18},{18,... | collective-permute-start | bytes 1179656 | tf_op jit(solution)/shard_map/ppermute | solution.py:249
  84.2 11.2 %collective-permute-start.19 = (f32[1,72,512]{2,1,0:T(8,128)S(1)}, f32[1,72,512]{2,1,0:T(8,128)S(1)}, u32[]{:S(2)}, u32[]{:S(2)}) collective-permute-start(f32[1,72,512]{2,1,0:T(8,128)S(1)} %get-tuple-element.81.token), channel_id=1, source_target_pairs={{0,16},{2,18},{4,20},{6,22},{8,24},{10,26},{12,28},{14,30},{16,0},... | collective-permute-start | bytes 442376 | tf_op jit(solution)/shard_map/ppermute | solution.py:249
  91.4 8.8 %collective-permute-start.21 = (f32[1,96,512]{2,1,0:T(8,128)S(1)}, f32[1,96,512]{2,1,0:T(8,128)S(1)}, u32[]{:S(2)}, u32[]{:S(2)}) collective-permute-start(f32[1,96,512]{2,1,0:T(8,128)S(1)} %get-tuple-element.86.token), channel_id=1, source_target_pairs={{0,16},{2,18},{4,20},{6,22},{8,24},{10,26},{12,28},{14,30},{16,0},... | collective-permute-start | bytes 589832 | tf_op jit(solution)/shard_map/ppermute | solution.py:249

commit v4 on v3

--- a/solution.py
+++ b/solution.py
@@ -14,12 +14,12 @@
 LANES = 128
 ROW_UNIT = 16
 TILE = 8
-LIMIT = 24 * 2**20
+LIMIT = 16 * 2**20
 
 PIECES = ((4, (0, 1, 3, 2)), (4, (1, 0, 2, 3)), (6, (2, 1, 0, 3)), (2, (0, 2, 1, 3)))
 EARLY = 3
-CARRIER = 1
-EVENTS = "abFN0d132031023103c212"
+CARRIER = 0
+EVENTS = "abFN0d123031203103c212"
 
 
 def bit_of(slab, bit):
@@ -31,8 +31,8 @@
         self.first, self.rows, self.order, self.extra = first, rows, order, extra
         self.bits = len(order)
 
-    def height(self):
-        return self.rows + self.extra
+    def height(self, blocks):
+        return blocks * self.rows + self.extra
 
     def halves(self, step, slab):
         left = [bit for bit in range(self.bits) if bit not in self.order[:step]]
@@ -77,18 +77,20 @@
         lhs = panel_buf[...].reshape(len(chunks) * rows, node_count)
         product = jnp.dot(lhs, fields[...], preferred_element_type=jnp.float32)
         for block, chunk in enumerate(chunks):
-            out[block, 0:rows, :] = product[block * rows : (block + 1) * rows]
+            at = block * rows
+            out[at : at + rows, :] = product[at : at + rows]
             node = shift + chunk * chunk_rows
 
             @pl.when((node >= 0) & (node < node_count))
-            def _(block=block, node=node):
-                at = pl.multiple_of(node + piece.first, ROW_UNIT)
-                jump = fields[pl.ds(at, rows), :].astype(jnp.float32)
-                out[block, 0:rows, :] += 0.5 * jump
-
-            if piece.extra:
-                row = lax.broadcasted_iota(jnp.int32, (TILE, width), 0)
-                out[block, rows : rows + TILE, :] = jnp.where(row == 0, squares[...], 0.0)
+            def _(at=at, node=node):
+                first = pl.multiple_of(node + piece.first, ROW_UNIT)
+                jump = fields[pl.ds(first, rows), :].astype(jnp.float32)
+                out[at : at + rows, :] += 0.5 * jump
+
+        if piece.extra:
+            row = lax.broadcasted_iota(jnp.int32, (TILE, width), 0)
+            at = len(chunks) * rows
+            out[at : at + TILE, :] = jnp.where(row == 0, squares[...], 0.0)
 
 
 def make_fields(blk, interiors, cells, incident, fields, squares):
@@ -135,16 +137,17 @@
     count = len(jobs)
     outs, refs = refs[5 : 5 + count], refs[5 + count :]
     panel_bufs, refs = refs[:count], refs[count:]
+    interior_bufs, refs = refs[:blocks], refs[blocks:]
     cells_buf, incident_buf, sems, in_sems = refs
     copies = []
-    for number, (source, target) in enumerate(((cells, cells_buf), (incident, incident_buf))):
+    for number, (source, target) in enumerate(zip(list(interiors) + [cells, incident], list(interior_bufs) + [cells_buf, incident_buf])):
         copy = pltpu.make_async_copy(source, target, in_sems.at[number])
         copy.start()
         copies.append(copy)
     started = panel_copies(jobs, panel, panel_bufs, sems)
     for copy in copies:
         copy.wait()
-    make_fields(lax.axis_index("blk"), interiors, cells_buf, incident_buf, fields, squares)
+    make_fields(lax.axis_index("blk"), interior_bufs, cells_buf, incident_buf, fields, squares)
     chunk_rows = panel.shape[-2]
     shift = shift_of(offset, chunk_rows * lax.axis_size("slab"), incident.shape[0])
     multiply(started, shift, chunk_rows, fields, squares, outs)
@@ -168,7 +171,7 @@
 
 def piece_shapes(jobs, width):
     return [
-        pltpu.VMEM((len(piece.halves(0, 0)[0]), piece.height(), width), jnp.float32) for piece, _ in jobs
+        pltpu.VMEM((piece.height(len(piece.halves(0, 0)[0])), width), jnp.float32) for piece, _ in jobs
     ]
 
 
@@ -190,17 +193,17 @@
     bufs, sems = piece_scratch(jobs, depth)
     return pl.pallas_call(
         functools.partial(first_kernel, jobs, len(interiors)),
-        in_specs=[IN_SMEM] + [IN_VMEM] * len(interiors) + [IN_HBM] * 3,
+        in_specs=[IN_SMEM] + [ANYWHERE] * len(interiors) + [IN_HBM] * 3,
         out_specs=[IN_VMEM] * (2 + len(jobs)),
         out_shape=[pltpu.VMEM(incident.shape, jnp.bfloat16), pltpu.VMEM((1, width), jnp.float32)]
         + piece_shapes(jobs, width),
         scratch_shapes=bufs
-        + [pltpu.VMEM(array.shape, array.dtype) for array in (cells, incident)]
-        + [sems, pltpu.SemaphoreType.DMA((2,))],
+        + [pltpu.VMEM(array.shape, array.dtype) for array in (*interiors, cells, incident)]
+        + [sems, pltpu.SemaphoreType.DMA((len(interiors) + 2,))],
         compiler_params=PARAMS,
         cost_estimate=COST,
         name="fields_and_first_rows",
-    )(offset, *interiors, in_hbm(cells), in_hbm(incident), in_hbm(panel))
+    )(offset, in_hbm(interiors[0]), *interiors[1:], in_hbm(cells), in_hbm(incident), in_hbm(panel))
 
 
 def later_products(jobs, offset, fields, squares, panel, token):
@@ -219,15 +222,22 @@
 
 
 def arrival_kernel(piece, step, got, base, token, *outs):
+    rows, extra = piece.rows, piece.extra
     halves = [[0]] if step == piece.bits else piece.halves(step, lax.axis_index("slab"))
     for blocks, out in zip(halves, outs):
         for number, block in enumerate(blocks):
-            out[number] = got[block] + base[block]
+            here = pl.ds(pl.multiple_of(block * rows, TILE), rows)
+            out[number * rows : (number + 1) * rows, :] = got[here, :] + base[here, :]
+        if extra:
+            last = base.shape[0] - extra
+            at = len(blocks) * rows
+            out[at : at + extra, :] = got[last:, :] + base[last:, :]
 
 
 def add_arrival(piece, step, got, base, token, name):
     count = 1 if step == piece.bits else 2
-    shape = pltpu.VMEM((max(1, base.shape[0] // 2),) + base.shape[1:], jnp.float32)
+    blocks = max(1, (1 << piece.bits) >> (step + 1))
+    shape = pltpu.VMEM((piece.height(blocks), base.shape[1]), jnp.float32)
     return pl.pallas_call(
         functools.partial(arrival_kernel, piece, step),
         in_specs=[IN_VMEM, IN_VMEM, ANYWHERE],
@@ -263,11 +273,11 @@
 
 def finish_kernel(node_total, carrier, rows, *refs):
     parts, out = refs[:-1], refs[-1]
-    squares = parts[carrier][0, rows[carrier] : rows[carrier] + 1, :]
+    squares = parts[carrier][rows[carrier] : rows[carrier] + 1, :]
     norms = jnp.sqrt(squares / node_total + 1e-06)
     first = 0
     for part, height in zip(parts, rows):
-        out[first : first + height, :] = part[0, :height, :] / norms
+        out[first : first + height, :] = part[:height, :] / norms
         first += height
 
 
@@ -296,6 +306,37 @@
         layer[0, 0:rows, :] = cells[at]
         layer[0, rows : rows + 1, :] = before[at]
         layer[0, rows + 1 : rows + 2, :] = after[at]
+
+
+def edge_copies_kernel(cells, before, after, token, *refs):
+    outs, bufs, sems = refs[:2], refs[2], refs[3]
+    depth, rows = cells.shape[:2]
+    odd = bit_of(lax.axis_index("slab"), 0)
+    copies = []
+    for number, lowest in enumerate((odd, 1 - odd)):
+        at = (1 - lowest) * (depth - 1)
+        copy = pltpu.make_async_copy(cells.at[at], bufs.at[number], sems.at[number])
+        copy.start()
+        copies.append((copy, at))
+    for number, (layer, (copy, at)) in enumerate(zip(outs, copies)):
+        copy.wait()
+        layer[0, 0:rows, :] = bufs[number]
+        layer[0, rows : rows + 1, :] = before[at]
+        layer[0, rows + 1 : rows + 2, :] = after[at]
+
+
+def first_layers(cells, before, after, token):
+    shape = pltpu.VMEM((1, cells.shape[1] + 2, cells.shape[2]), jnp.float32)
+    return pl.pallas_call(
+        edge_copies_kernel,
+        in_specs=[IN_HBM] + [IN_VMEM] * 2 + [ANYWHERE],
+        out_specs=[IN_VMEM] * 2,
+        out_shape=[shape, shape],
+        scratch_shapes=[pltpu.VMEM((2,) + cells.shape[1:], jnp.float32), pltpu.SemaphoreType.DMA((2,))],
+        compiler_params=PARAMS,
+        cost_estimate=COST,
+        name="first_layers",
+    )(in_hbm(cells), before, after, token)
 
 
 def edge_layers(cells, before, after, token):
@@ -342,8 +383,8 @@
             rows = [jnp.where(first, 0.0, rows[0]), jnp.where(first, rows[0], 0.0)]
         self.before, self.after = rows
 
-    def make_layers(self, token):
-        self.edges = edge_layers(self.cells, self.before, self.after, token)
+    def make_layers(self, token, make=edge_layers):
+        self.edges = make(self.cells, self.before, self.after, token)
         self.layers = []
         return self.edges[0]
 
@@ -433,7 +474,7 @@
 
     panel = bem_panel.reshape((2,) * bits + (chunk_rows, slab_cols))
     inside = Interior(interior, other, sources, absorption)
-    inside.make_layers(offset)
+    inside.make_layers(offset, first_layers)
     inside.send_layer(0)
     inside.send_layer(1)
     fields, squares, *far = first_products(

time: 102 us -> 98.9 us (0.970)
  waiting for transfers between devices: 48.9 us -> 46.6 us
  local copies, waits for them, and re-layouts: 2.78 us -> 0.89 us
    ppermute x4, waiting for transfers between devices: 11.4 us -> 1.47 us  [send_layer(): self.layers.append(lax.ppermute(self.edges[number], 'slab', pairs))]
    ppermute x16, waiting for transfers between devices: 35.6 us -> 43.3 us  [send(): self.got = lax.ppermute(rows, 'slab', self.piece.pairs(self.step))]
    unnamed x10 -> x6, local copies, waits for them, and re-layouts: 2.72 us -> 0.83 us
    ppermute x4, starting transfers between devices: 6.19 us -> 4.38 us  [send_layer(): self.layers.append(lax.ppermute(self.edges[number], 'slab', pairs))]
    ppermute x16, starting transfers between devices: 26.1 us -> 27.6 us  [send(): self.got = lax.ppermute(rows, 'slab', self.piece.pairs(self.step))]
  transfers between devices with their start and end apart: 22 -> 22, of which waited for: 11 -> 11; matrix products, arithmetic and copies ran while one was open for 2% -> 2% of each run, Pallas kernels for 12% -> 13%
where the time goes in v4:
time: 98.9 us; the launch traced here: 98.7 us
  waiting for transfers between devices  46.6 us (47%)
  starting transfers between devices  32.5 us (33%)
  Pallas kernels  14.3 us (14%)
  other arithmetic  2.68 us (3%)
  between operations  1.69 us (2%)
    ppermute x16, waiting for transfers between devices, send(): self.got = lax.ppermute(rows, 'slab', self.piece.pairs(self.step))  43.3 us
    ppermute x16, starting transfers between devices, send(): self.got = lax.ppermute(rows, 'slab', self.piece.pairs(self.step))  27.6 us
    pallas_call x2, Pallas kernels, later_products(): pl.pallas_call(functools.partial(later_kernel, jobs), in_specs=[IN_SMEM,...  6.08 us
    pallas_call x1, Pallas kernels, first_products(): pl.pallas_call(functools.partial(first_kernel, jobs, len(interiors)), in_...  5.36 us
    ppermute x4, starting transfers between devices, send_layer(): self.layers.append(lax.ppermute(self.edges[number], 'slab', pairs))  4.38 us
  transfers between devices with their start and end apart: 22, of which 11 were waited for; matrix products, arithmetic and copies ran while one was open for 2% of the time, Pallas kernels for 13%

profile of v4, /device:TPU:0, one launch (start us, length us, event | category | flops | bytes accessed | tf_op | source)
XLA Modules:
  0.0 98.7 jit_solution(9963824644449404675)
XLA Ops:
  1.8 0.7 collective-permute-done.refs_1_
  2.5 1.0 %first_layers.1 = (f32[1,66,512]{2,1,0:T(8,128)S(1)}, f32[1,66,512]{2,1,0:T(8,128)S(1)}) custom-call(f32[2,64,512]{2,1,0:T(8,128)} %refs_0_.1, f32[2,1,512]{2,1,0:T(1,128)S(1)} %broadcast_select_fusion.8.before, f32[2,1,512]{2,1,0:T(1,128)S(1)} %get-tuple-element.92.after, s32[1]{0:T(128)S(6)} %copy.9.token.offset), custom_call_target="tpu_custom_call" | custom-call | flops 1 | bytes 1 | tf_op jit(solution)/shard_map/first_layers/pallas_call | solution.py:330
  3.6 2.9 %collective-permute-start.1 = (f32[1,66,512]{2,1,0:T(8,128)S(1)}, f32[1,66,512]{2,1,0:T(8,128)S(1)}, u32[]{:S(2)}, u32[]{:S(2)}) collective-permute-start(f32[1,66,512]{2,1,0:T(8,128)S(1)} %get-tuple-element.45), channel_id=1, source_target_pairs={{0,2},{2,0},{4,6},{6,4},{8,10},{10,8},{12,14},{14,12},{16,18},{18,... | collective-permute-start | bytes 405512 | tf_op jit(solution)/shard_map/ppermute | solution.py:396
  6.5 0.7 collective-permute-start.2
  7.2 5.4 %fields_and_first_rows.1 = (bf16[1024,512]{1,0:T(8,128)(2,1)S(1)}, f32[1,512]{1,0:T(1,128)S(1)}, f32[520,512]{1,0:T(8,128)S(1)}, f32[512,512]{1,0:T(8,128)S(1)}, f32[768,512]{1,0:T(8,128)S(1)}) custom-call(s32[1]{0:T(128)S(6)} %copy.9.token.offset, f32[2,64,512]{2,1,0:T(8,128)} %refs_0_.1, f32[2,64,512]{2,1,0:T(8,128)S(1)} %collective-permute-done.refs_1_, ...), custom_call_target="tpu_custom_call" | custom-call | flops 1 | bytes 1 | tf_op jit(solution)/shard_map/fields_and_first_rows/pallas_call | solution.py:194
  12.5 4.4 %collective-permute-start.5 = (f32[520,512]{1,0:T(8,128)S(1)}, f32[520,512]{1,0:T(8,128)S(1)}, u32[]{:S(2)}, u32[]{:S(2)}) collective-permute-start(f32[520,512]{1,0:T(8,128)S(1)} %get-tuple-element.47.refs_2_), channel_id=1, source_target_pairs={{0,2},{2,0},{4,6},{6,4},{8,10},{10,8},{12,14},{14,12},{16,18},{18,... | collective-permute-start | bytes 3194888 | tf_op jit(solution)/shard_map/ppermute | solution.py:259
  16.9 1.5 %collective-permute-start.9 = (f32[512,512]{1,0:T(8,128)S(1)}, f32[512,512]{1,0:T(8,128)S(1)}, u32[]{:S(2)}, u32[]{:S(2)}) collective-permute-start(f32[512,512]{1,0:T(8,128)S(1)} %get-tuple-element.60), channel_id=1, source_target_pairs={{0,4},{2,6},{4,0},{6,2},{8,12},{10,14},{12,8},{14,10},{16,20},{18,... | collective-permute-start | bytes 3145736 | tf_op jit(solution)/shard_map/ppermute | solution.py:259
  18.4 1.5 %collective-permute-start.8 = (f32[768,512]{1,0:T(8,128)S(1)}, f32[768,512]{1,0:T(8,128)S(1)}, u32[]{:S(2)}, u32[]{:S(2)}) collective-permute-start(f32[768,512]{1,0:T(8,128)S(1)} %get-tuple-element.58), channel_id=1, source_target_pairs={{0,8},{2,10},{4,12},{6,14},{8,0},{10,2},{12,4},{14,6},{16,24},{18,... | collective-permute-start | bytes 4718600 | tf_op jit(solution)/shard_map/ppermute | solution.py:259
  20.7 0.7 copy-done.1
  21.9 1.2 %collective-permute-done.3.refs_0_ = f32[2,1,512]{2,1,0:T(1,128)S(1)} collective-permute-done((f32[2,1,512]{2,1,0:T(1,128)S(1)}, f32[2,1,512]{2,1,0:T(1,128)S(1)}, u32[]{:S(2)}, u32[]{:S(2)}) %collective-permute-start.3) | collective-permute-done | bytes 4128 | tf_op jit(solution)/shard_map/ppermute | solution.py:372
  23.3 1.6 %other_rows.2.token = f32[256,512]{1,0:T(8,128)S(1)} custom-call(s32[1]{0:T(128)S(6)} %copy.9.token.offset, bf16[1024,512]{1,0:T(8,128)(2,1)S(1)} %get-tuple-element.51.fields, f32[1,512]{1,0:T(1,128)S(1)} %get-tuple-element.52.squares, bf16[2,2,2,2,256,1024]{5,4,3,2,1,0:T(8,128)(2,1)} %bitcast.3, f32[1,66,512]{2,1,0:T(8,128)S(1)} %get-tuple-element.50.token.refs_0_), custom_call_target="tpu_custom_call" | custom-call | flops 1 | bytes 1 | tf_op jit(solution)/shard_map/other_rows/pallas_call | solution.py:212
  24.8 2.0 %collective-permute-start.7 = (f32[256,512]{1,0:T(8,128)S(1)}, f32[256,512]{1,0:T(8,128)S(1)}, u32[]{:S(2)}, u32[]{:S(2)}) collective-permute-start(f32[256,512]{1,0:T(8,128)S(1)} %other_rows.2.token), channel_id=1, source_target_pairs={{0,2},{2,0},{4,6},{6,4},{8,10},{10,8},{12,14},{14,12},{16,18},{18,... | collective-permute-start | bytes 1572872 | tf_op jit(solution)/shard_map/ppermute | solution.py:259
  26.8 4.5 %other_rows.3 = (f32[520,512]{1,0:T(8,128)S(1)}, f32[512,512]{1,0:T(8,128)S(1)}, f32[768,512]{1,0:T(8,128)S(1)}, f32[256,512]{1,0:T(8,128)S(1)}) custom-call(s32[1]{0:T(128)S(6)} %copy.9.token.offset, bf16[1024,512]{1,0:T(8,128)(2,1)S(1)} %get-tuple-element.51.fields, f32[1,512]{1,0:T(1,128)S(1)} %get-tuple-element.52.squares, ...), custom_call_target="tpu_custom_call" | custom-call | flops 1 | bytes 1 | tf_op jit(solution)/shard_map/other_rows/pallas_call | solution.py:212
  31.4 9.9 %collective-permute-done.5.got = f32[520,512]{1,0:T(8,128)S(1)} collective-permute-done((f32[520,512]{1,0:T(8,128)S(1)}, f32[520,512]{1,0:T(8,128)S(1)}, u32[]{:S(2)}, u32[]{:S(2)}) %collective-permute-start.5) | collective-permute-done | bytes 1064992 | tf_op jit(solution)/shard_map/ppermute | solution.py:259
  41.4 1.6 %collective-permute-start.11 = (f32[264,512]{1,0:T(8,128)S(1)}, f32[264,512]{1,0:T(8,128)S(1)}, u32[]{:S(2)}, u32[]{:S(2)}) collective-permute-start(f32[264,512]{1,0:T(8,128)S(1)} %get-tuple-element.54.refs_1_), channel_id=1, source_target_pairs={{0,4},{2,6},{4,0},{6,2},{8,12},{10,14},{12,8},{14,10},{16,20},{18,... | collective-permute-start | bytes 1622024 | tf_op jit(solution)/shard_map/ppermute | solution.py:259
  43.0 1.5 %collective-permute-done.4.refs_0_ = f32[1,66,512]{2,1,0:T(8,128)S(1)} collective-permute-done((f32[1,66,512]{2,1,0:T(8,128)S(1)}, f32[1,66,512]{2,1,0:T(8,128)S(1)}, u32[]{:S(2)}, u32[]{:S(2)}) %collective-permute-start.4) | collective-permute-done | bytes 135200 | tf_op jit(solution)/shard_map/ppermute | solution.py:396
  44.6 9.0 %collective-permute-done.8.got = f32[768,512]{1,0:T(8,128)S(1)} collective-permute-done((f32[768,512]{1,0:T(8,128)S(1)}, f32[768,512]{1,0:T(8,128)S(1)}, u32[]{:S(2)}, u32[]{:S(2)}) %collective-permute-start.8) | collective-permute-done | bytes 1572896 | tf_op jit(solution)/shard_map/ppermute | solution.py:259
  54.8 1.8 %collective-permute-start.10 = (f32[128,512]{1,0:T(8,128)S(1)}, f32[128,512]{1,0:T(8,128)S(1)}, u32[]{:S(2)}, u32[]{:S(2)}) collective-permute-start(f32[128,512]{1,0:T(8,128)S(1)} %get-tuple-element.65.token), channel_id=1, source_target_pairs={{0,8},{2,10},{4,12},{6,14},{8,0},{10,2},{12,4},{14,6},{16,24},{18,... | collective-permute-start | bytes 786440 | tf_op jit(solution)/shard_map/ppermute | solution.py:259
  56.7 2.5 %collective-permute-start.13 = (f32[136,512]{1,0:T(8,128)S(1)}, f32[136,512]{1,0:T(8,128)S(1)}, u32[]{:S(2)}, u32[]{:S(2)}) collective-permute-start(f32[136,512]{1,0:T(8,128)S(1)} %get-tuple-element.68.token), channel_id=1, source_target_pairs={{0,16},{2,18},{4,20},{6,22},{8,24},{10,26},{12,28},{14,30},{16,0},... | collective-permute-start | bytes 835592 | tf_op jit(solution)/shard_map/ppermute | solution.py:259
  59.2 8.3 %collective-permute-done.10.got = f32[128,512]{1,0:T(8,128)S(1)} collective-permute-done((f32[128,512]{1,0:T(8,128)S(1)}, f32[128,512]{1,0:T(8,128)S(1)}, u32[]{:S(2)}, u32[]{:S(2)}) %collective-permute-start.10) | collective-permute-done | bytes 262176 | tf_op jit(solution)/shard_map/ppermute | solution.py:259
  67.8 1.8 %collective-permute-start.12 = (f32[64,512]{1,0:T(8,128)S(1)}, f32[64,512]{1,0:T(8,128)S(1)}, u32[]{:S(2)}, u32[]{:S(2)}) collective-permute-start(f32[64,512]{1,0:T(8,128)S(1)} %get-tuple-element.69.token), channel_id=1, source_target_pairs={{0,4},{2,6},{4,0},{6,2},{8,12},{10,14},{12,8},{14,10},{16,20},{18,... | collective-permute-start | bytes 393224 | tf_op jit(solution)/shard_map/ppermute | solution.py:259
  69.6 3.0 %collective-permute-done.14.got = f32[384,512]{1,0:T(8,128)S(1)} collective-permute-done((f32[384,512]{1,0:T(8,128)S(1)}, f32[384,512]{1,0:T(8,128)S(1)}, u32[]{:S(2)}, u32[]{:S(2)}) %collective-permute-start.14) | collective-permute-done | bytes 786464 | tf_op jit(solution)/shard_map/ppermute | solution.py:259
  72.8 1.9 %collective-permute-start.17 = (f32[72,512]{1,0:T(8,128)S(1)}, f32[72,512]{1,0:T(8,128)S(1)}, u32[]{:S(2)}, u32[]{:S(2)}) collective-permute-start(f32[72,512]{1,0:T(8,128)S(1)} %get-tuple-element.76.token), channel_id=1, source_target_pairs={{0,8},{2,10},{4,12},{6,14},{8,0},{10,2},{12,4},{14,6},{16,24},{18,... | collective-permute-start | bytes 442376 | tf_op jit(solution)/shard_map/ppermute | solution.py:259
  75.4 3.6 %collective-permute-start.16 = (f32[32,512]{1,0:T(8,128)S(1)}, f32[32,512]{1,0:T(8,128)S(1)}, u32[]{:S(2)}, u32[]{:S(2)}) collective-permute-start(f32[32,512]{1,0:T(8,128)S(1)} %get-tuple-element.77.token), channel_id=1, source_target_pairs={{0,16},{2,18},{4,20},{6,22},{8,24},{10,26},{12,28},{14,30},{16,0},... | collective-permute-start | bytes 196616 | tf_op jit(solution)/shard_map/ppermute | solution.py:259
  79.0 2.1 %collective-permute-start.20 = (f32[192,512]{1,0:T(8,128)S(1)}, f32[192,512]{1,0:T(8,128)S(1)}, u32[]{:S(2)}, u32[]{:S(2)}) collective-permute-start(f32[192,512]{1,0:T(8,128)S(1)} %get-tuple-element.75.token), channel_id=1, source_target_pairs={{0,2},{2,0},{4,6},{6,4},{8,10},{10,8},{12,14},{14,12},{16,18},{18,... | collective-permute-start | bytes 1179656 | tf_op jit(solution)/shard_map/ppermute | solution.py:259
  81.7 3.5 %collective-permute-done.16.got = f32[32,512]{1,0:T(8,128)S(1)} collective-permute-done((f32[32,512]{1,0:T(8,128)S(1)}, f32[32,512]{1,0:T(8,128)S(1)}, u32[]{:S(2)}, u32[]{:S(2)}) %collective-permute-start.16) | collective-permute-done | bytes 65568 | tf_op jit(solution)/shard_map/ppermute | solution.py:259
  85.9 1.6 %collective-permute-done.20.got = f32[192,512]{1,0:T(8,128)S(1)} collective-permute-done((f32[192,512]{1,0:T(8,128)S(1)}, f32[192,512]{1,0:T(8,128)S(1)}, u32[]{:S(2)}, u32[]{:S(2)}) %collective-permute-start.20) | collective-permute-done | bytes 393248 | tf_op jit(solution)/shard_map/ppermute | solution.py:259
  87.5 1.2 %collective-permute-start.21 = (f32[96,512]{1,0:T(8,128)S(1)}, f32[96,512]{1,0:T(8,128)S(1)}, u32[]{:S(2)}, u32[]{:S(2)}) collective-permute-start(f32[96,512]{1,0:T(8,128)S(1)} %get-tuple-element.86.token), channel_id=1, source_target_pairs={{0,16},{2,18},{4,20},{6,22},{8,24},{10,26},{12,28},{14,30},{16,0},... | collective-permute-start | bytes 589832 | tf_op jit(solution)/shard_map/ppermute | solution.py:259
  88.9 2.8 %collective-permute-done.19.got = f32[64,512]{1,0:T(8,128)S(1)} collective-permute-done((f32[64,512]{1,0:T(8,128)S(1)}, f32[64,512]{1,0:T(8,128)S(1)}, u32[]{:S(2)}, u32[]{:S(2)}) %collective-permute-start.19) | collective-permute-done | bytes 131104 | tf_op jit(solution)/shard_map/ppermute | solution.py:259
  91.7 5.1 %collective-permute-done.21.got = f32[96,512]{1,0:T(8,128)S(1)} collective-permute-done((f32[96,512]{1,0:T(8,128)S(1)}, f32[96,512]{1,0:T(8,128)S(1)}, u32[]{:S(2)}, u32[]{:S(2)}) %collective-permute-start.21) | collective-permute-done | bytes 196640 | tf_op jit(solution)/shard_map/ppermute | solution.py:259
  96.9 1.0 %fusion.12 = f32[2,64,512]{2,1,0:T(8,128)} fusion(f32[2,64,512]{2,1,0:T(8,128)S(1)} %fusion.29.cells, f32[2,64,512]{2,1,0:T(8,128)S(1)} %copy-done.1, f32[1,64,512]{2,1,0:T(8,128)S(1)} %slice.248, f32[1,64,512]{2,1,0:T(8,128)S(1)} %slice.247, f32[1,1,512]{2,1,0:T(1,128)S(1)} %get-tuple-element.101, f32[2,1,512]{2,1,0:T(1,128)S(1)} %get-tuple-element.106.after, ...), kind=kLoop, calls=%fused_computation.26 | loop fusion | flops 2228224 | bytes 2899968 | tf_op jit(solution)/shard_map/add | solution.py:434
  97.9 0.8 divide_by_norms.1
  (68 shorter events, 5.9 us)
Async XLA Ops:
  0.6 1.9 %collective-permute-start = (f32[2,64,512]{2,1,0:T(8,128)}, f32[2,64,512]{2,1,0:T(8,128)S(1)}, u32[]{:S(2)}, u32[]{:S(2)}) collective-permute-start(f32[2,64,512]{2,1,0:T(8,128)} %refs_0_.1), channel_id=1, source_target_pairs={{0,1},{1,0},{2,3},{3,2},{4,5},{5,4},{6,7},{7,6},{8,9},{9,8},{10,11... | collective-permute-start | bytes 786440 | tf_op jit(solution)/shard_map/ppermute | solution.py:451
  3.6 16.3 %collective-permute-start.1 = (f32[1,66,512]{2,1,0:T(8,128)S(1)}, f32[1,66,512]{2,1,0:T(8,128)S(1)}, u32[]{:S(2)}, u32[]{:S(2)}) collective-permute-start(f32[1,66,512]{2,1,0:T(8,128)S(1)} %get-tuple-element.45), channel_id=1, source_target_pairs={{0,2},{2,0},{4,6},{6,4},{8,10},{10,8},{12,14},{14,12},{16,18},{18,... | collective-permute-start | bytes 405512 | tf_op jit(solution)/shard_map/ppermute | solution.py:396
  6.5 13.4 %collective-permute-start.2 = (f32[1,66,512]{2,1,0:T(8,128)S(1)}, f32[1,66,512]{2,1,0:T(8,128)S(1)}, u32[]{:S(2)}, u32[]{:S(2)}) collective-permute-start(f32[1,66,512]{2,1,0:T(8,128)S(1)} %get-tuple-element.46), channel_id=1, source_target_pairs={{2,4},{4,2},{6,8},{8,6},{10,12},{12,10},{14,16},{16,14},{18,20},{2... | collective-permute-start | bytes 405512 | tf_op jit(solution)/shard_map/ppermute | solution.py:396
  12.5 7.5 %copy-start = (f32[2,64,512]{2,1,0:T(8,128)S(1)}, f32[2,64,512]{2,1,0:T(8,128)}, u32[]{:S(2)}) copy-start(f32[2,64,512]{2,1,0:T(8,128)} %refs_0_.1) | copy-start | bytes 786436
  12.5 28.8 %collective-permute-start.5 = (f32[520,512]{1,0:T(8,128)S(1)}, f32[520,512]{1,0:T(8,128)S(1)}, u32[]{:S(2)}, u32[]{:S(2)}) collective-permute-start(f32[520,512]{1,0:T(8,128)S(1)} %get-tuple-element.47.refs_2_), channel_id=1, source_target_pairs={{0,2},{2,0},{4,6},{6,4},{8,10},{10,8},{12,14},{14,12},{16,18},{18,... | collective-permute-start | bytes 3194888 | tf_op jit(solution)/shard_map/ppermute | solution.py:259
  16.9 27.6 %collective-permute-start.9 = (f32[512,512]{1,0:T(8,128)S(1)}, f32[512,512]{1,0:T(8,128)S(1)}, u32[]{:S(2)}, u32[]{:S(2)}) collective-permute-start(f32[512,512]{1,0:T(8,128)S(1)} %get-tuple-element.60), channel_id=1, source_target_pairs={{0,4},{2,6},{4,0},{6,2},{8,12},{10,14},{12,8},{14,10},{16,20},{18,... | collective-permute-start | bytes 3145736 | tf_op jit(solution)/shard_map/ppermute | solution.py:259
  18.4 35.2 %collective-permute-start.8 = (f32[768,512]{1,0:T(8,128)S(1)}, f32[768,512]{1,0:T(8,128)S(1)}, u32[]{:S(2)}, u32[]{:S(2)}) collective-permute-start(f32[768,512]{1,0:T(8,128)S(1)} %get-tuple-element.58), channel_id=1, source_target_pairs={{0,8},{2,10},{4,12},{6,14},{8,0},{10,2},{12,4},{14,6},{16,24},{18,... | collective-permute-start | bytes 4718600 | tf_op jit(solution)/shard_map/ppermute | solution.py:259
  20.5 1.0 copy-start.1
  20.5 1.0 %copy-start.2 = (f32[2,64,512]{2,1,0:T(8,128)S(1)}, f32[2,64,512]{2,1,0:T(8,128)}, u32[]{:S(2)}) copy-start(f32[2,64,512]{2,1,0:T(8,128)} %param.9) | copy-start | bytes 786436
  21.8 1.2 %collective-permute-start.3 = (f32[2,1,512]{2,1,0:T(1,128)S(1)}, f32[2,1,512]{2,1,0:T(1,128)S(1)}, u32[]{:S(2)}, u32[]{:S(2)}) collective-permute-start(f32[2,1,512]{2,1,0:T(1,128)S(1)} %broadcast_select_fusion.6), channel_id=1, source_target_pairs={{0,1},{1,0},{2,3},{3,2},{4,5},{5,4},{6,7},{7,6},{8,9},{9,8},{10,11... | collective-permute-start | bytes 12296 | tf_op jit(solution)/shard_map/ppermute | solution.py:372
  23.1 21.3 %collective-permute-start.4 = (f32[1,66,512]{2,1,0:T(8,128)S(1)}, f32[1,66,512]{2,1,0:T(8,128)S(1)}, u32[]{:S(2)}, u32[]{:S(2)}) collective-permute-start(f32[1,66,512]{2,1,0:T(8,128)S(1)} %get-tuple-element.50.token.refs_0_), channel_id=1, source_target_pairs={{0,2},{2,0},{4,6},{6,4},{8,10},{10,8},{12,14},{14,12},{16,18},{18,... | collective-permute-start | bytes 405512 | tf_op jit(solution)/shard_map/ppermute | solution.py:396
  24.8 29.9 %collective-permute-start.7 = (f32[256,512]{1,0:T(8,128)S(1)}, f32[256,512]{1,0:T(8,128)S(1)}, u32[]{:S(2)}, u32[]{:S(2)}) collective-permute-start(f32[256,512]{1,0:T(8,128)S(1)} %other_rows.2.token), channel_id=1, source_target_pairs={{0,2},{2,0},{4,6},{6,4},{8,10},{10,8},{12,14},{14,12},{16,18},{18,... | collective-permute-start | bytes 1572872 | tf_op jit(solution)/shard_map/ppermute | solution.py:259
  41.4 15.2 %collective-permute-start.11 = (f32[264,512]{1,0:T(8,128)S(1)}, f32[264,512]{1,0:T(8,128)S(1)}, u32[]{:S(2)}, u32[]{:S(2)}) collective-permute-start(f32[264,512]{1,0:T(8,128)S(1)} %get-tuple-element.54.refs_1_), channel_id=1, source_target_pairs={{0,4},{2,6},{4,0},{6,2},{8,12},{10,14},{12,8},{14,10},{16,20},{18,... | collective-permute-start | bytes 1622024 | tf_op jit(solution)/shard_map/ppermute | solution.py:259
  53.8 18.9 %collective-permute-start.14 = (f32[384,512]{1,0:T(8,128)S(1)}, f32[384,512]{1,0:T(8,128)S(1)}, u32[]{:S(2)}, u32[]{:S(2)}) collective-permute-start(f32[384,512]{1,0:T(8,128)S(1)} %get-tuple-element.64.token), channel_id=1, source_target_pairs={{0,4},{2,6},{4,0},{6,2},{8,12},{10,14},{12,8},{14,10},{16,20},{18,... | collective-permute-start | bytes 2359304 | tf_op jit(solution)/shard_map/ppermute | solution.py:259
  54.3 13.2 %collective-permute-start.15 = (f32[256,512]{1,0:T(8,128)S(1)}, f32[256,512]{1,0:T(8,128)S(1)}, u32[]{:S(2)}, u32[]{:S(2)}) collective-permute-start(f32[256,512]{1,0:T(8,128)S(1)} %get-tuple-element.63.token), channel_id=1, source_target_pairs={{0,2},{2,0},{4,6},{6,4},{8,10},{10,8},{12,14},{14,12},{16,18},{18,... | collective-permute-start | bytes 1572872 | tf_op jit(solution)/shard_map/ppermute | solution.py:259
  54.8 12.7 %collective-permute-start.10 = (f32[128,512]{1,0:T(8,128)S(1)}, f32[128,512]{1,0:T(8,128)S(1)}, u32[]{:S(2)}, u32[]{:S(2)}) collective-permute-start(f32[128,512]{1,0:T(8,128)S(1)} %get-tuple-element.65.token), channel_id=1, source_target_pairs={{0,8},{2,10},{4,12},{6,14},{8,0},{10,2},{12,4},{14,6},{16,24},{18,... | collective-permute-start | bytes 786440 | tf_op jit(solution)/shard_map/ppermute | solution.py:259
  56.7 16.1 %collective-permute-start.13 = (f32[136,512]{1,0:T(8,128)S(1)}, f32[136,512]{1,0:T(8,128)S(1)}, u32[]{:S(2)}, u32[]{:S(2)}) collective-permute-start(f32[136,512]{1,0:T(8,128)S(1)} %get-tuple-element.68.token), channel_id=1, source_target_pairs={{0,16},{2,18},{4,20},{6,22},{8,24},{10,26},{12,28},{14,30},{16,0},... | collective-permute-start | bytes 835592 | tf_op jit(solution)/shard_map/ppermute | solution.py:259
  67.6 13.6 %collective-permute-start.18 = (f32[128,512]{1,0:T(8,128)S(1)}, f32[128,512]{1,0:T(8,128)S(1)}, u32[]{:S(2)}, u32[]{:S(2)}) collective-permute-start(f32[128,512]{1,0:T(8,128)S(1)} %get-tuple-element.74.token), channel_id=1, source_target_pairs={{0,8},{2,10},{4,12},{6,14},{8,0},{10,2},{12,4},{14,6},{16,24},{18,... | collective-permute-start | bytes 786440 | tf_op jit(solution)/shard_map/ppermute | solution.py:259
  67.8 7.6 %collective-permute-start.12 = (f32[64,512]{1,0:T(8,128)S(1)}, f32[64,512]{1,0:T(8,128)S(1)}, u32[]{:S(2)}, u32[]{:S(2)}) collective-permute-start(f32[64,512]{1,0:T(8,128)S(1)} %get-tuple-element.69.token), channel_id=1, source_target_pairs={{0,4},{2,6},{4,0},{6,2},{8,12},{10,14},{12,8},{14,10},{16,20},{18,... | collective-permute-start | bytes 393224 | tf_op jit(solution)/shard_map/ppermute | solution.py:259
  72.8 8.9 %collective-permute-start.17 = (f32[72,512]{1,0:T(8,128)S(1)}, f32[72,512]{1,0:T(8,128)S(1)}, u32[]{:S(2)}, u32[]{:S(2)}) collective-permute-start(f32[72,512]{1,0:T(8,128)S(1)} %get-tuple-element.76.token), channel_id=1, source_target_pairs={{0,8},{2,10},{4,12},{6,14},{8,0},{10,2},{12,4},{14,6},{16,24},{18,... | collective-permute-start | bytes 442376 | tf_op jit(solution)/shard_map/ppermute | solution.py:259
  74.7 10.6 %collective-permute-start.6 = (f32[1,66,512]{2,1,0:T(8,128)S(1)}, f32[1,66,512]{2,1,0:T(8,128)S(1)}, u32[]{:S(2)}, u32[]{:S(2)}) collective-permute-start(f32[1,66,512]{2,1,0:T(8,128)S(1)} %get-tuple-element.56), channel_id=1, source_target_pairs={{2,4},{4,2},{6,8},{8,6},{10,12},{12,10},{14,16},{16,14},{18,20},{2... | collective-permute-start | bytes 405512 | tf_op jit(solution)/shard_map/ppermute | solution.py:396
  75.4 9.9 %collective-permute-start.16 = (f32[32,512]{1,0:T(8,128)S(1)}, f32[32,512]{1,0:T(8,128)S(1)}, u32[]{:S(2)}, u32[]{:S(2)}) collective-permute-start(f32[32,512]{1,0:T(8,128)S(1)} %get-tuple-element.77.token), channel_id=1, source_target_pairs={{0,16},{2,18},{4,20},{6,22},{8,24},{10,26},{12,28},{14,30},{16,0},... | collective-permute-start | bytes 196616 | tf_op jit(solution)/shard_map/ppermute | solution.py:259
  79.0 8.5 %collective-permute-start.20 = (f32[192,512]{1,0:T(8,128)S(1)}, f32[192,512]{1,0:T(8,128)S(1)}, u32[]{:S(2)}, u32[]{:S(2)}) collective-permute-start(f32[192,512]{1,0:T(8,128)S(1)} %get-tuple-element.75.token), channel_id=1, source_target_pairs={{0,2},{2,0},{4,6},{6,4},{8,10},{10,8},{12,14},{14,12},{16,18},{18,... | collective-permute-start | bytes 1179656 | tf_op jit(solution)/shard_map/ppermute | solution.py:259
  81.2 10.5 %collective-permute-start.19 = (f32[64,512]{1,0:T(8,128)S(1)}, f32[64,512]{1,0:T(8,128)S(1)}, u32[]{:S(2)}, u32[]{:S(2)}) collective-permute-start(f32[64,512]{1,0:T(8,128)S(1)} %get-tuple-element.81.token), channel_id=1, source_target_pairs={{0,16},{2,18},{4,20},{6,22},{8,24},{10,26},{12,28},{14,30},{16,0},... | collective-permute-start | bytes 393224 | tf_op jit(solution)/shard_map/ppermute | solution.py:259
  87.5 9.3 %collective-permute-start.21 = (f32[96,512]{1,0:T(8,128)S(1)}, f32[96,512]{1,0:T(8,128)S(1)}, u32[]{:S(2)}, u32[]{:S(2)}) collective-permute-start(f32[96,512]{1,0:T(8,128)S(1)} %get-tuple-element.86.token), channel_id=1, source_target_pairs={{0,16},{2,18},{4,20},{6,22},{8,24},{10,26},{12,28},{14,30},{16,0},... | collective-permute-start | bytes 589832 | tf_op jit(solution)/shard_map/ppermute | solution.py:259

commit v5 on v4

--- a/solution.py
+++ b/solution.py
@@ -485,7 +485,9 @@
     events = EVENTS
     if len(pieces) * bits != sum(event.isdigit() for event in EVENTS):
         events = "F" * (len(pieces) - EARLY) + "Nabdc" + "".join(str(number) for number in range(len(pieces))) * bits
-    for event in events:
+    for number_of_event, event in enumerate(events):
+        if number_of_event == len(events) - 1:
+            token = inside.cells
         if event == "F":
             number = len(courses)
             token = later_products([(pieces[number], 0)], offset, fields, squares, panel, token)[0]

time: 98.9 us -> 98 us (level)
  no operation moved by 1% of the time
where the time goes in v5:
time: 98 us; the launch traced here: 97.7 us
  waiting for transfers between devices  46.3 us (47%)
  starting transfers between devices  32.6 us (33%)
  Pallas kernels  14.3 us (15%)
  other arithmetic  1.97 us (2%)
  between operations  1.69 us (2%)
    ppermute x16, waiting for transfers between devices, send(): self.got = lax.ppermute(rows, 'slab', self.piece.pairs(self.step))  42.9 us
    ppermute x16, starting transfers between devices, send(): self.got = lax.ppermute(rows, 'slab', self.piece.pairs(self.step))  27.6 us
    pallas_call x2, Pallas kernels, later_products(): pl.pallas_call(functools.partial(later_kernel, jobs), in_specs=[IN_SMEM,...  6.08 us
    pallas_call x1, Pallas kernels, first_products(): pl.pallas_call(functools.partial(first_kernel, jobs, len(interiors)), in_...  5.37 us
    ppermute x4, starting transfers between devices, send_layer(): self.layers.append(lax.ppermute(self.edges[number], 'slab', pairs))  4.38 us
  transfers between devices with their start and end apart: 22, of which 11 were waited for; matrix products, arithmetic and copies ran while one was open for 2% of the time, Pallas kernels for 13%

profile of v5, /device:TPU:0, one launch (start us, length us, event | category | flops | bytes accessed | tf_op | source)
XLA Modules:
  0.0 97.7 jit_solution(12322244466371731504)
XLA Ops:
  1.8 0.7 collective-permute-done.refs_1_
  2.5 1.0 %first_layers.1 = (f32[1,66,512]{2,1,0:T(8,128)S(1)}, f32[1,66,512]{2,1,0:T(8,128)S(1)}) custom-call(f32[2,64,512]{2,1,0:T(8,128)} %refs_0_.1, f32[2,1,512]{2,1,0:T(1,128)S(1)} %broadcast_select_fusion.8.before, f32[2,1,512]{2,1,0:T(1,128)S(1)} %get-tuple-element.92.after, s32[1]{0:T(128)S(6)} %copy.9.token.offset), custom_call_target="tpu_custom_call" | custom-call | flops 1 | bytes 1 | tf_op jit(solution)/shard_map/first_layers/pallas_call | solution.py:330
  3.6 2.9 %collective-permute-start.1 = (f32[1,66,512]{2,1,0:T(8,128)S(1)}, f32[1,66,512]{2,1,0:T(8,128)S(1)}, u32[]{:S(2)}, u32[]{:S(2)}) collective-permute-start(f32[1,66,512]{2,1,0:T(8,128)S(1)} %get-tuple-element.45), channel_id=1, source_target_pairs={{0,2},{2,0},{4,6},{6,4},{8,10},{10,8},{12,14},{14,12},{16,18},{18,... | collective-permute-start | bytes 405512 | tf_op jit(solution)/shard_map/ppermute | solution.py:396
  6.5 0.7 collective-permute-start.2
  7.2 5.4 %fields_and_first_rows.1 = (bf16[1024,512]{1,0:T(8,128)(2,1)S(1)}, f32[1,512]{1,0:T(1,128)S(1)}, f32[520,512]{1,0:T(8,128)S(1)}, f32[512,512]{1,0:T(8,128)S(1)}, f32[768,512]{1,0:T(8,128)S(1)}) custom-call(s32[1]{0:T(128)S(6)} %copy.9.token.offset, f32[2,64,512]{2,1,0:T(8,128)} %refs_0_.1, f32[2,64,512]{2,1,0:T(8,128)S(1)} %collective-permute-done.refs_1_, ...), custom_call_target="tpu_custom_call" | custom-call | flops 1 | bytes 1 | tf_op jit(solution)/shard_map/fields_and_first_rows/pallas_call | solution.py:194
  12.5 4.4 %collective-permute-start.5 = (f32[520,512]{1,0:T(8,128)S(1)}, f32[520,512]{1,0:T(8,128)S(1)}, u32[]{:S(2)}, u32[]{:S(2)}) collective-permute-start(f32[520,512]{1,0:T(8,128)S(1)} %get-tuple-element.47.refs_2_), channel_id=1, source_target_pairs={{0,2},{2,0},{4,6},{6,4},{8,10},{10,8},{12,14},{14,12},{16,18},{18,... | collective-permute-start | bytes 3194888 | tf_op jit(solution)/shard_map/ppermute | solution.py:259
  16.9 1.5 %collective-permute-start.9 = (f32[512,512]{1,0:T(8,128)S(1)}, f32[512,512]{1,0:T(8,128)S(1)}, u32[]{:S(2)}, u32[]{:S(2)}) collective-permute-start(f32[512,512]{1,0:T(8,128)S(1)} %get-tuple-element.60), channel_id=1, source_target_pairs={{0,4},{2,6},{4,0},{6,2},{8,12},{10,14},{12,8},{14,10},{16,20},{18,... | collective-permute-start | bytes 3145736 | tf_op jit(solution)/shard_map/ppermute | solution.py:259
  18.4 1.4 %collective-permute-start.8 = (f32[768,512]{1,0:T(8,128)S(1)}, f32[768,512]{1,0:T(8,128)S(1)}, u32[]{:S(2)}, u32[]{:S(2)}) collective-permute-start(f32[768,512]{1,0:T(8,128)S(1)} %get-tuple-element.58), channel_id=1, source_target_pairs={{0,8},{2,10},{4,12},{6,14},{8,0},{10,2},{12,4},{14,6},{16,24},{18,... | collective-permute-start | bytes 4718600 | tf_op jit(solution)/shard_map/ppermute | solution.py:259
  20.7 0.7 copy-done.2
  21.9 1.2 %collective-permute-done.3.refs_0_ = f32[2,1,512]{2,1,0:T(1,128)S(1)} collective-permute-done((f32[2,1,512]{2,1,0:T(1,128)S(1)}, f32[2,1,512]{2,1,0:T(1,128)S(1)}, u32[]{:S(2)}, u32[]{:S(2)}) %collective-permute-start.3) | collective-permute-done | bytes 4128 | tf_op jit(solution)/shard_map/ppermute | solution.py:372
  23.3 1.6 %other_rows.2.token = f32[256,512]{1,0:T(8,128)S(1)} custom-call(s32[1]{0:T(128)S(6)} %copy.9.token.offset, bf16[1024,512]{1,0:T(8,128)(2,1)S(1)} %get-tuple-element.51.fields, f32[1,512]{1,0:T(1,128)S(1)} %get-tuple-element.52.squares, bf16[2,2,2,2,256,1024]{5,4,3,2,1,0:T(8,128)(2,1)} %bitcast.3, f32[1,66,512]{2,1,0:T(8,128)S(1)} %get-tuple-element.50.token.refs_0_), custom_call_target="tpu_custom_call" | custom-call | flops 1 | bytes 1 | tf_op jit(solution)/shard_map/other_rows/pallas_call | solution.py:212
  24.8 2.0 %collective-permute-start.7 = (f32[256,512]{1,0:T(8,128)S(1)}, f32[256,512]{1,0:T(8,128)S(1)}, u32[]{:S(2)}, u32[]{:S(2)}) collective-permute-start(f32[256,512]{1,0:T(8,128)S(1)} %other_rows.2.token), channel_id=1, source_target_pairs={{0,2},{2,0},{4,6},{6,4},{8,10},{10,8},{12,14},{14,12},{16,18},{18,... | collective-permute-start | bytes 1572872 | tf_op jit(solution)/shard_map/ppermute | solution.py:259
  26.8 4.5 %other_rows.3 = (f32[520,512]{1,0:T(8,128)S(1)}, f32[512,512]{1,0:T(8,128)S(1)}, f32[768,512]{1,0:T(8,128)S(1)}, f32[256,512]{1,0:T(8,128)S(1)}) custom-call(s32[1]{0:T(128)S(6)} %copy.9.token.offset, bf16[1024,512]{1,0:T(8,128)(2,1)S(1)} %get-tuple-element.51.fields, f32[1,512]{1,0:T(1,128)S(1)} %get-tuple-element.52.squares, ...), custom_call_target="tpu_custom_call" | custom-call | flops 1 | bytes 1 | tf_op jit(solution)/shard_map/other_rows/pallas_call | solution.py:212
  31.4 9.9 %collective-permute-done.5.got = f32[520,512]{1,0:T(8,128)S(1)} collective-permute-done((f32[520,512]{1,0:T(8,128)S(1)}, f32[520,512]{1,0:T(8,128)S(1)}, u32[]{:S(2)}, u32[]{:S(2)}) %collective-permute-start.5) | collective-permute-done | bytes 1064992 | tf_op jit(solution)/shard_map/ppermute | solution.py:259
  41.4 1.6 %collective-permute-start.11 = (f32[264,512]{1,0:T(8,128)S(1)}, f32[264,512]{1,0:T(8,128)S(1)}, u32[]{:S(2)}, u32[]{:S(2)}) collective-permute-start(f32[264,512]{1,0:T(8,128)S(1)} %get-tuple-element.54.refs_1_), channel_id=1, source_target_pairs={{0,4},{2,6},{4,0},{6,2},{8,12},{10,14},{12,8},{14,10},{16,20},{18,... | collective-permute-start | bytes 1622024 | tf_op jit(solution)/shard_map/ppermute | solution.py:259
  43.0 1.5 %collective-permute-done.4.refs_0_ = f32[1,66,512]{2,1,0:T(8,128)S(1)} collective-permute-done((f32[1,66,512]{2,1,0:T(8,128)S(1)}, f32[1,66,512]{2,1,0:T(8,128)S(1)}, u32[]{:S(2)}, u32[]{:S(2)}) %collective-permute-start.4) | collective-permute-done | bytes 135200 | tf_op jit(solution)/shard_map/ppermute | solution.py:396
  44.6 9.0 %collective-permute-done.8.got = f32[768,512]{1,0:T(8,128)S(1)} collective-permute-done((f32[768,512]{1,0:T(8,128)S(1)}, f32[768,512]{1,0:T(8,128)S(1)}, u32[]{:S(2)}, u32[]{:S(2)}) %collective-permute-start.8) | collective-permute-done | bytes 1572896 | tf_op jit(solution)/shard_map/ppermute | solution.py:259
  54.8 1.8 %collective-permute-start.10 = (f32[128,512]{1,0:T(8,128)S(1)}, f32[128,512]{1,0:T(8,128)S(1)}, u32[]{:S(2)}, u32[]{:S(2)}) collective-permute-start(f32[128,512]{1,0:T(8,128)S(1)} %get-tuple-element.65.token), channel_id=1, source_target_pairs={{0,8},{2,10},{4,12},{6,14},{8,0},{10,2},{12,4},{14,6},{16,24},{18,... | collective-permute-start | bytes 786440 | tf_op jit(solution)/shard_map/ppermute | solution.py:259
  56.7 2.5 %collective-permute-start.13 = (f32[136,512]{1,0:T(8,128)S(1)}, f32[136,512]{1,0:T(8,128)S(1)}, u32[]{:S(2)}, u32[]{:S(2)}) collective-permute-start(f32[136,512]{1,0:T(8,128)S(1)} %get-tuple-element.68.token), channel_id=1, source_target_pairs={{0,16},{2,18},{4,20},{6,22},{8,24},{10,26},{12,28},{14,30},{16,0},... | collective-permute-start | bytes 835592 | tf_op jit(solution)/shard_map/ppermute | solution.py:259
  59.2 8.3 %collective-permute-done.10.got = f32[128,512]{1,0:T(8,128)S(1)} collective-permute-done((f32[128,512]{1,0:T(8,128)S(1)}, f32[128,512]{1,0:T(8,128)S(1)}, u32[]{:S(2)}, u32[]{:S(2)}) %collective-permute-start.10) | collective-permute-done | bytes 262176 | tf_op jit(solution)/shard_map/ppermute | solution.py:259
  67.8 1.8 %collective-permute-start.12 = (f32[64,512]{1,0:T(8,128)S(1)}, f32[64,512]{1,0:T(8,128)S(1)}, u32[]{:S(2)}, u32[]{:S(2)}) collective-permute-start(f32[64,512]{1,0:T(8,128)S(1)} %get-tuple-element.69.token), channel_id=1, source_target_pairs={{0,4},{2,6},{4,0},{6,2},{8,12},{10,14},{12,8},{14,10},{16,20},{18,... | collective-permute-start | bytes 393224 | tf_op jit(solution)/shard_map/ppermute | solution.py:259
  69.6 3.0 %collective-permute-done.14.got = f32[384,512]{1,0:T(8,128)S(1)} collective-permute-done((f32[384,512]{1,0:T(8,128)S(1)}, f32[384,512]{1,0:T(8,128)S(1)}, u32[]{:S(2)}, u32[]{:S(2)}) %collective-permute-start.14) | collective-permute-done | bytes 786464 | tf_op jit(solution)/shard_map/ppermute | solution.py:259
  72.8 1.9 %collective-permute-start.17 = (f32[72,512]{1,0:T(8,128)S(1)}, f32[72,512]{1,0:T(8,128)S(1)}, u32[]{:S(2)}, u32[]{:S(2)}) collective-permute-start(f32[72,512]{1,0:T(8,128)S(1)} %get-tuple-element.76.token), channel_id=1, source_target_pairs={{0,8},{2,10},{4,12},{6,14},{8,0},{10,2},{12,4},{14,6},{16,24},{18,... | collective-permute-start | bytes 442376 | tf_op jit(solution)/shard_map/ppermute | solution.py:259
  74.7 0.7 collective-permute-start.6
  75.4 3.6 %collective-permute-start.16 = (f32[32,512]{1,0:T(8,128)S(1)}, f32[32,512]{1,0:T(8,128)S(1)}, u32[]{:S(2)}, u32[]{:S(2)}) collective-permute-start(f32[32,512]{1,0:T(8,128)S(1)} %get-tuple-element.77.token), channel_id=1, source_target_pairs={{0,16},{2,18},{4,20},{6,22},{8,24},{10,26},{12,28},{14,30},{16,0},... | collective-permute-start | bytes 196616 | tf_op jit(solution)/shard_map/ppermute | solution.py:259
  79.0 2.1 %collective-permute-start.20 = (f32[192,512]{1,0:T(8,128)S(1)}, f32[192,512]{1,0:T(8,128)S(1)}, u32[]{:S(2)}, u32[]{:S(2)}) collective-permute-start(f32[192,512]{1,0:T(8,128)S(1)} %get-tuple-element.75.token), channel_id=1, source_target_pairs={{0,2},{2,0},{4,6},{6,4},{8,10},{10,8},{12,14},{14,12},{16,18},{18,... | collective-permute-start | bytes 1179656 | tf_op jit(solution)/shard_map/ppermute | solution.py:259
  81.7 3.5 %collective-permute-done.16.got = f32[32,512]{1,0:T(8,128)S(1)} collective-permute-done((f32[32,512]{1,0:T(8,128)S(1)}, f32[32,512]{1,0:T(8,128)S(1)}, u32[]{:S(2)}, u32[]{:S(2)}) %collective-permute-start.16) | collective-permute-done | bytes 65568 | tf_op jit(solution)/shard_map/ppermute | solution.py:259
  86.1 1.4 %collective-permute-done.20.got = f32[192,512]{1,0:T(8,128)S(1)} collective-permute-done((f32[192,512]{1,0:T(8,128)S(1)}, f32[192,512]{1,0:T(8,128)S(1)}, u32[]{:S(2)}, u32[]{:S(2)}) %collective-permute-start.20) | collective-permute-done | bytes 393248 | tf_op jit(solution)/shard_map/ppermute | solution.py:259
  87.6 1.2 %collective-permute-start.21 = (f32[96,512]{1,0:T(8,128)S(1)}, f32[96,512]{1,0:T(8,128)S(1)}, u32[]{:S(2)}, u32[]{:S(2)}) collective-permute-start(f32[96,512]{1,0:T(8,128)S(1)} %get-tuple-element.86.token), channel_id=1, source_target_pairs={{0,16},{2,18},{4,20},{6,22},{8,24},{10,26},{12,28},{14,30},{16,0},... | collective-permute-start | bytes 589832 | tf_op jit(solution)/shard_map/ppermute | solution.py:259
  89.1 2.6 %collective-permute-done.19.got = f32[64,512]{1,0:T(8,128)S(1)} collective-permute-done((f32[64,512]{1,0:T(8,128)S(1)}, f32[64,512]{1,0:T(8,128)S(1)}, u32[]{:S(2)}, u32[]{:S(2)}) %collective-permute-start.19) | collective-permute-done | bytes 131104 | tf_op jit(solution)/shard_map/ppermute | solution.py:259
  91.7 5.1 %collective-permute-done.21.got = f32[96,512]{1,0:T(8,128)S(1)} collective-permute-done((f32[96,512]{1,0:T(8,128)S(1)}, f32[96,512]{1,0:T(8,128)S(1)}, u32[]{:S(2)}, u32[]{:S(2)}) %collective-permute-start.21) | collective-permute-done | bytes 196640 | tf_op jit(solution)/shard_map/ppermute | solution.py:259
  96.9 0.8 divide_by_norms.1
  (70 shorter events, 5.6 us)
Async XLA Ops:
  0.6 1.9 %collective-permute-start = (f32[2,64,512]{2,1,0:T(8,128)}, f32[2,64,512]{2,1,0:T(8,128)S(1)}, u32[]{:S(2)}, u32[]{:S(2)}) collective-permute-start(f32[2,64,512]{2,1,0:T(8,128)} %refs_0_.1), channel_id=1, source_target_pairs={{0,1},{1,0},{2,3},{3,2},{4,5},{5,4},{6,7},{7,6},{8,9},{9,8},{10,11... | collective-permute-start | bytes 786440 | tf_op jit(solution)/shard_map/ppermute | solution.py:451
  3.6 16.3 %collective-permute-start.1 = (f32[1,66,512]{2,1,0:T(8,128)S(1)}, f32[1,66,512]{2,1,0:T(8,128)S(1)}, u32[]{:S(2)}, u32[]{:S(2)}) collective-permute-start(f32[1,66,512]{2,1,0:T(8,128)S(1)} %get-tuple-element.45), channel_id=1, source_target_pairs={{0,2},{2,0},{4,6},{6,4},{8,10},{10,8},{12,14},{14,12},{16,18},{18,... | collective-permute-start | bytes 405512 | tf_op jit(solution)/shard_map/ppermute | solution.py:396
  6.5 13.4 %collective-permute-start.2 = (f32[1,66,512]{2,1,0:T(8,128)S(1)}, f32[1,66,512]{2,1,0:T(8,128)S(1)}, u32[]{:S(2)}, u32[]{:S(2)}) collective-permute-start(f32[1,66,512]{2,1,0:T(8,128)S(1)} %get-tuple-element.46), channel_id=1, source_target_pairs={{2,4},{4,2},{6,8},{8,6},{10,12},{12,10},{14,16},{16,14},{18,20},{2... | collective-permute-start | bytes 405512 | tf_op jit(solution)/shard_map/ppermute | solution.py:396
  12.5 7.5 %copy-start.1 = (f32[2,64,512]{2,1,0:T(8,128)S(1)}, f32[2,64,512]{2,1,0:T(8,128)}, u32[]{:S(2)}) copy-start(f32[2,64,512]{2,1,0:T(8,128)} %refs_0_.1) | copy-start | bytes 786436
  12.5 28.8 %collective-permute-start.5 = (f32[520,512]{1,0:T(8,128)S(1)}, f32[520,512]{1,0:T(8,128)S(1)}, u32[]{:S(2)}, u32[]{:S(2)}) collective-permute-start(f32[520,512]{1,0:T(8,128)S(1)} %get-tuple-element.47.refs_2_), channel_id=1, source_target_pairs={{0,2},{2,0},{4,6},{6,4},{8,10},{10,8},{12,14},{14,12},{16,18},{18,... | collective-permute-start | bytes 3194888 | tf_op jit(solution)/shard_map/ppermute | solution.py:259
  16.9 27.6 %collective-permute-start.9 = (f32[512,512]{1,0:T(8,128)S(1)}, f32[512,512]{1,0:T(8,128)S(1)}, u32[]{:S(2)}, u32[]{:S(2)}) collective-permute-start(f32[512,512]{1,0:T(8,128)S(1)} %get-tuple-element.60), channel_id=1, source_target_pairs={{0,4},{2,6},{4,0},{6,2},{8,12},{10,14},{12,8},{14,10},{16,20},{18,... | collective-permute-start | bytes 3145736 | tf_op jit(solution)/shard_map/ppermute | solution.py:259
  18.4 35.2 %collective-permute-start.8 = (f32[768,512]{1,0:T(8,128)S(1)}, f32[768,512]{1,0:T(8,128)S(1)}, u32[]{:S(2)}, u32[]{:S(2)}) collective-permute-start(f32[768,512]{1,0:T(8,128)S(1)} %get-tuple-element.58), channel_id=1, source_target_pairs={{0,8},{2,10},{4,12},{6,14},{8,0},{10,2},{12,4},{14,6},{16,24},{18,... | collective-permute-start | bytes 4718600 | tf_op jit(solution)/shard_map/ppermute | solution.py:259
  20.5 1.0 copy-start.2
  20.5 1.0 %copy-start.3 = (f32[2,64,512]{2,1,0:T(8,128)S(1)}, f32[2,64,512]{2,1,0:T(8,128)}, u32[]{:S(2)}) copy-start(f32[2,64,512]{2,1,0:T(8,128)} %param.9) | copy-start | bytes 786436
  21.8 1.2 %collective-permute-start.3 = (f32[2,1,512]{2,1,0:T(1,128)S(1)}, f32[2,1,512]{2,1,0:T(1,128)S(1)}, u32[]{:S(2)}, u32[]{:S(2)}) collective-permute-start(f32[2,1,512]{2,1,0:T(1,128)S(1)} %broadcast_select_fusion.6), channel_id=1, source_target_pairs={{0,1},{1,0},{2,3},{3,2},{4,5},{5,4},{6,7},{7,6},{8,9},{9,8},{10,11... | collective-permute-start | bytes 12296 | tf_op jit(solution)/shard_map/ppermute | solution.py:372
  23.1 21.3 %collective-permute-start.4 = (f32[1,66,512]{2,1,0:T(8,128)S(1)}, f32[1,66,512]{2,1,0:T(8,128)S(1)}, u32[]{:S(2)}, u32[]{:S(2)}) collective-permute-start(f32[1,66,512]{2,1,0:T(8,128)S(1)} %get-tuple-element.50.token.refs_0_), channel_id=1, source_target_pairs={{0,2},{2,0},{4,6},{6,4},{8,10},{10,8},{12,14},{14,12},{16,18},{18,... | collective-permute-start | bytes 405512 | tf_op jit(solution)/shard_map/ppermute | solution.py:396
  24.8 29.9 %collective-permute-start.7 = (f32[256,512]{1,0:T(8,128)S(1)}, f32[256,512]{1,0:T(8,128)S(1)}, u32[]{:S(2)}, u32[]{:S(2)}) collective-permute-start(f32[256,512]{1,0:T(8,128)S(1)} %other_rows.2.token), channel_id=1, source_target_pairs={{0,2},{2,0},{4,6},{6,4},{8,10},{10,8},{12,14},{14,12},{16,18},{18,... | collective-permute-start | bytes 1572872 | tf_op jit(solution)/shard_map/ppermute | solution.py:259
  41.4 15.2 %collective-permute-start.11 = (f32[264,512]{1,0:T(8,128)S(1)}, f32[264,512]{1,0:T(8,128)S(1)}, u32[]{:S(2)}, u32[]{:S(2)}) collective-permute-start(f32[264,512]{1,0:T(8,128)S(1)} %get-tuple-element.54.refs_1_), channel_id=1, source_target_pairs={{0,4},{2,6},{4,0},{6,2},{8,12},{10,14},{12,8},{14,10},{16,20},{18,... | collective-permute-start | bytes 1622024 | tf_op jit(solution)/shard_map/ppermute | solution.py:259
  53.8 18.9 %collective-permute-start.14 = (f32[384,512]{1,0:T(8,128)S(1)}, f32[384,512]{1,0:T(8,128)S(1)}, u32[]{:S(2)}, u32[]{:S(2)}) collective-permute-start(f32[384,512]{1,0:T(8,128)S(1)} %get-tuple-element.64.token), channel_id=1, source_target_pairs={{0,4},{2,6},{4,0},{6,2},{8,12},{10,14},{12,8},{14,10},{16,20},{18,... | collective-permute-start | bytes 2359304 | tf_op jit(solution)/shard_map/ppermute | solution.py:259
  54.3 13.2 %collective-permute-start.15 = (f32[256,512]{1,0:T(8,128)S(1)}, f32[256,512]{1,0:T(8,128)S(1)}, u32[]{:S(2)}, u32[]{:S(2)}) collective-permute-start(f32[256,512]{1,0:T(8,128)S(1)} %get-tuple-element.63.token), channel_id=1, source_target_pairs={{0,2},{2,0},{4,6},{6,4},{8,10},{10,8},{12,14},{14,12},{16,18},{18,... | collective-permute-start | bytes 1572872 | tf_op jit(solution)/shard_map/ppermute | solution.py:259
  54.8 12.7 %collective-permute-start.10 = (f32[128,512]{1,0:T(8,128)S(1)}, f32[128,512]{1,0:T(8,128)S(1)}, u32[]{:S(2)}, u32[]{:S(2)}) collective-permute-start(f32[128,512]{1,0:T(8,128)S(1)} %get-tuple-element.65.token), channel_id=1, source_target_pairs={{0,8},{2,10},{4,12},{6,14},{8,0},{10,2},{12,4},{14,6},{16,24},{18,... | collective-permute-start | bytes 786440 | tf_op jit(solution)/shard_map/ppermute | solution.py:259
  56.7 16.1 %collective-permute-start.13 = (f32[136,512]{1,0:T(8,128)S(1)}, f32[136,512]{1,0:T(8,128)S(1)}, u32[]{:S(2)}, u32[]{:S(2)}) collective-permute-start(f32[136,512]{1,0:T(8,128)S(1)} %get-tuple-element.68.token), channel_id=1, source_target_pairs={{0,16},{2,18},{4,20},{6,22},{8,24},{10,26},{12,28},{14,30},{16,0},... | collective-permute-start | bytes 835592 | tf_op jit(solution)/shard_map/ppermute | solution.py:259
  67.6 13.6 %collective-permute-start.18 = (f32[128,512]{1,0:T(8,128)S(1)}, f32[128,512]{1,0:T(8,128)S(1)}, u32[]{:S(2)}, u32[]{:S(2)}) collective-permute-start(f32[128,512]{1,0:T(8,128)S(1)} %get-tuple-element.74.token), channel_id=1, source_target_pairs={{0,8},{2,10},{4,12},{6,14},{8,0},{10,2},{12,4},{14,6},{16,24},{18,... | collective-permute-start | bytes 786440 | tf_op jit(solution)/shard_map/ppermute | solution.py:259
  67.8 7.6 %collective-permute-start.12 = (f32[64,512]{1,0:T(8,128)S(1)}, f32[64,512]{1,0:T(8,128)S(1)}, u32[]{:S(2)}, u32[]{:S(2)}) collective-permute-start(f32[64,512]{1,0:T(8,128)S(1)} %get-tuple-element.69.token), channel_id=1, source_target_pairs={{0,4},{2,6},{4,0},{6,2},{8,12},{10,14},{12,8},{14,10},{16,20},{18,... | collective-permute-start | bytes 393224 | tf_op jit(solution)/shard_map/ppermute | solution.py:259
  72.8 8.9 %collective-permute-start.17 = (f32[72,512]{1,0:T(8,128)S(1)}, f32[72,512]{1,0:T(8,128)S(1)}, u32[]{:S(2)}, u32[]{:S(2)}) collective-permute-start(f32[72,512]{1,0:T(8,128)S(1)} %get-tuple-element.76.token), channel_id=1, source_target_pairs={{0,8},{2,10},{4,12},{6,14},{8,0},{10,2},{12,4},{14,6},{16,24},{18,... | collective-permute-start | bytes 442376 | tf_op jit(solution)/shard_map/ppermute | solution.py:259
  74.7 10.6 %collective-permute-start.6 = (f32[1,66,512]{2,1,0:T(8,128)S(1)}, f32[1,66,512]{2,1,0:T(8,128)S(1)}, u32[]{:S(2)}, u32[]{:S(2)}) collective-permute-start(f32[1,66,512]{2,1,0:T(8,128)S(1)} %get-tuple-element.56), channel_id=1, source_target_pairs={{2,4},{4,2},{6,8},{8,6},{10,12},{12,10},{14,16},{16,14},{18,20},{2... | collective-permute-start | bytes 405512 | tf_op jit(solution)/shard_map/ppermute | solution.py:396
  75.4 9.8 %collective-permute-start.16 = (f32[32,512]{1,0:T(8,128)S(1)}, f32[32,512]{1,0:T(8,128)S(1)}, u32[]{:S(2)}, u32[]{:S(2)}) collective-permute-start(f32[32,512]{1,0:T(8,128)S(1)} %get-tuple-element.77.token), channel_id=1, source_target_pairs={{0,16},{2,18},{4,20},{6,22},{8,24},{10,26},{12,28},{14,30},{16,0},... | collective-permute-start | bytes 196616 | tf_op jit(solution)/shard_map/ppermute | solution.py:259
  79.0 8.5 %collective-permute-start.20 = (f32[192,512]{1,0:T(8,128)S(1)}, f32[192,512]{1,0:T(8,128)S(1)}, u32[]{:S(2)}, u32[]{:S(2)}) collective-permute-start(f32[192,512]{1,0:T(8,128)S(1)} %get-tuple-element.75.token), channel_id=1, source_target_pairs={{0,2},{2,0},{4,6},{6,4},{8,10},{10,8},{12,14},{14,12},{16,18},{18,... | collective-permute-start | bytes 1179656 | tf_op jit(solution)/shard_map/ppermute | solution.py:259
  81.2 10.5 %collective-permute-start.19 = (f32[64,512]{1,0:T(8,128)S(1)}, f32[64,512]{1,0:T(8,128)S(1)}, u32[]{:S(2)}, u32[]{:S(2)}) collective-permute-start(f32[64,512]{1,0:T(8,128)S(1)} %get-tuple-element.81.token), channel_id=1, source_target_pairs={{0,16},{2,18},{4,20},{6,22},{8,24},{10,26},{12,28},{14,30},{16,0},... | collective-permute-start | bytes 393224 | tf_op jit(solution)/shard_map/ppermute | solution.py:259
  87.6 9.3 %collective-permute-start.21 = (f32[96,512]{1,0:T(8,128)S(1)}, f32[96,512]{1,0:T(8,128)S(1)}, u32[]{:S(2)}, u32[]{:S(2)}) collective-permute-start(f32[96,512]{1,0:T(8,128)S(1)} %get-tuple-element.86.token), channel_id=1, source_target_pairs={{0,16},{2,18},{4,20},{6,22},{8,24},{10,26},{12,28},{14,30},{16,0},... | collective-permute-start | bytes 589832 | tf_op jit(solution)/shard_map/ppermute | solution.py:259
  89.1 8.6 %copy-start = (f32[2,64,512]{2,1,0:T(8,128)}, f32[2,64,512]{2,1,0:T(8,128)S(1)}, u32[]{:S(2)}) copy-start(f32[2,64,512]{2,1,0:T(8,128)S(1)} %fusion.12.token) | copy-start | bytes 786436
